TPU v7x, 32 devices: a whole 2x2x4 slice. The times are simulated.
32 devices in a mesh: ctx: 16 (over z, y, x), head: 2 (over core).
Axes of the slice: x: 2, y: 2, z: 4, core: 2. Of those that a mesh axis runs over, the one named last changes fastest.
Arguments:
- queries: bfloat16 [4096, 32, 128], P('ctx', 'head'), may hold values from -300 to 300
- keys: bfloat16 [4096, 8, 128], P('ctx', 'head'), may hold values from -12 to 12
- values: bfloat16 [4096, 8, 128], P('ctx', 'head'), may hold values from -150 to 150
- tangent_queries: bfloat16 [4096, 32, 128], P('ctx', 'head'), may hold values from -6 to 6
- tangent_keys: bfloat16 [4096, 8, 128], P('ctx', 'head'), may hold values from -6 to 6
- tangent_values: bfloat16 [4096, 8, 128], P('ctx', 'head'), may hold values from -6 to 6
- doc_start: int32 [32], P('ctx'), may hold values from 0 to 31, as said below
- out_gain: float32 [4096], P('head'), may hold values from 0.1 to 1.9
Outputs:
- product_queries: float32 [4096, 32, 128], P('ctx', 'head')
- product_keys: float32 [4096, 8, 128], P('ctx', 'head')
- product_values: float32 [4096, 8, 128], P('ctx', 'head')
Inputs may be any that keep to these rules, and one draw needn't show every extreme that they name: Documents are runs of whole mask blocks; doc_start[b] is the first block of b's document, so it never falls and doc_start[b] <= b. No document is longer than 16 blocks, and one is exactly 16 blocks long.
All inputs are finite; a program needn't handle non-finite values.
Results may differ from a plain program's by a relative error of at most 0.014.
Values may be sent and summed in bfloat16 or wider, within the bound.
No kernel may reach another device: no remote copies, remote signals or barrier semaphores. Data moves between devices by JAX's collectives and lax.ppermute only.
A program may use at most 192 MiB of HBM per device.

v0:
```python
import functools

import jax
import jax.numpy as jnp
from jax import lax
from jax.experimental import pallas as pl
from jax.experimental.pallas import tpu as pltpu
from jax.sharding import Mesh, PartitionSpec as P

DOC_DEVS = 8
EPSILON = 1e-06
VMEM_BYTES = 18 * 1024 * 1024
NOTE_ROWS = 16
ONES_ROWS = 16
WIDE_VMEM_BYTES = 60 * 1024 * 1024
MASKED = -1e30
F32 = jnp.float32
BF16 = jnp.bfloat16
SMEM = pl.BlockSpec(memory_space=pltpu.SMEM)
VMEM = pl.BlockSpec(memory_space=pltpu.VMEM)


def params(size=VMEM_BYTES):
    return pltpu.CompilerParams(vmem_limit_bytes=size)


def cost(flops, moved, powers=0):
    return pl.CostEstimate(flops=int(flops), bytes_accessed=int(moved), transcendentals=int(powers))


def nn(a, b):
    return lax.dot_general(a, b, (((1,), (0,)), ((), ())), preferred_element_type=F32)


def nt(a, b):
    return lax.dot_general(a, b, (((1,), (1,)), ((), ())), preferred_element_type=F32)


def split_heads(arrays, parts, per_part, notes=None):
    count = len(arrays)
    total, width = arrays[0].shape
    heads = parts * per_part
    rows = total // heads
    length = count * per_part * rows
    span = per_part * rows
    extra = 0 if notes is None else NOTE_ROWS
    scalars = [] if notes is None else [notes]

    def kernel(*refs):
        ins = list(refs[: len(scalars) + count])
        results = refs[len(scalars) + count : len(scalars) + count + parts]
        held, wide, sems, *staged = refs[len(scalars) + count + parts :]
        outs, out_sems = (staged[:-1], staged[-1]) if extra else (results, None)
        mine = lax.axis_index("part")
        if extra:
            note_ref = ins.pop(0)
        copies = [pltpu.make_async_copy(ins[a], held.at[a], sems.at[a]) for a in range(count)]
        for copy in copies:
            copy.start()
        leaving = []

        def leave(m, a, start, size):
            part = pl.ds(start, size)
            sem = out_sems.at[m * (count + 1) + a]
            leaving.append(pltpu.make_async_copy(outs[m].at[part], results[m].at[part], sem))
            leaving[-1].start()

        if extra:
            first = (lax.axis_index("span") * parts + mine) * notes.shape[0]
            line = lax.broadcasted_iota(jnp.int32, (extra, width), 0)
            lines = jnp.zeros((extra, width), jnp.int32)
            for i in range(notes.shape[0]):
                lines = jnp.where(line == i, first + i - note_ref[i], lines)
            for m, out in enumerate(outs):
                out[length:, :] = lines.astype(F32).astype(BF16)
                leave(m, count, length, extra)
        for a in range(count):
            copies[a].wait()
            wide[...] = held[a].astype(F32)
            for m in range(parts):
                for r in range(per_part):
                    head = jnp.bitwise_xor(mine, m) * per_part + r
                    at = (a * per_part + r) * rows
                    outs[m][at : at + rows, :] = wide[pl.ds(head, rows, stride=heads), :].astype(BF16)
                if extra:
                    leave(m, a, a * span, span)
        for copy in leaving:
            copy.wait()

    piece = (length + extra, width)
    scratch = [
        pltpu.VMEM((count, total, width), BF16),
        pltpu.VMEM((total, width), F32),
        pltpu.SemaphoreType.DMA((count,)),
    ]
    if extra:
        scratch += [pltpu.VMEM(piece, BF16)] * parts
        scratch.append(pltpu.SemaphoreType.DMA((parts * (count + 1),)))
    return pl.pallas_call(
        kernel,
        in_specs=[SMEM] * len(scalars) + [pl.BlockSpec(memory_space=pltpu.HBM)] * count,
        out_specs=[pl.BlockSpec(memory_space=pltpu.HBM) if extra else VMEM] * parts,
        out_shape=[jax.ShapeDtypeStruct(piece, BF16)] * parts,
        scratch_shapes=scratch,
        compiler_params=params(VMEM_BYTES if notes is None else WIDE_VMEM_BYTES),
        cost_estimate=cost(0, 4 * count * total * width),
        name="split_heads",
    )(*scalars, *arrays)


def join_heads(pieces, count, per_part):
    parts = len(pieces)
    rows, width = pieces[0].shape[-2:]
    heads = parts * per_part

    steps = 4
    cut = rows // steps

    def kernel(*refs):
        ins, outs = refs[:parts], refs[parts:]
        mine = lax.axis_index("part")
        for a in range(count):
            for m in range(parts):
                for r in range(per_part):
                    head = jnp.bitwise_xor(mine, m) * per_part + r
                    outs[a][pl.ds(head, cut, stride=heads), :] = ins[m][a, r].astype(F32)

    return pl.pallas_call(
        kernel,
        grid=(steps,),
        in_specs=[pl.BlockSpec((count, per_part, cut, width), lambda i: (0, 0, i, 0))] * parts,
        out_specs=[pl.BlockSpec((cut * heads, width), lambda i: (i, 0))] * count,
        out_shape=[jax.ShapeDtypeStruct((rows * heads, width), F32)] * count,
        compiler_params=params(),
        cost_estimate=cost(0, 6 * count * rows * heads * width),
        name="join_heads",
    )(*pieces)


def slot_of(me_ref, m, rows):
    return pl.multiple_of(jnp.bitwise_xor(me_ref[0], m) * rows, rows)


class Shape:
    def __init__(self, parts, group, rows, width, block):
        self.parts, self.group, self.rows, self.width, self.block = parts, group, rows, width, block
        self.tokens = parts * rows
        self.blocks = self.tokens // block
        self.lanes = group * block
        self.scale = width**-0.5


def diagonal(sh):
    shape = (sh.block, sh.block)
    key = lax.broadcasted_iota(jnp.int32, shape, 0)
    query = lax.broadcasted_iota(jnp.int32, shape, 1)
    return key <= query


def below_diagonal(sh, value, other):
    allowed = diagonal(sh)
    cut = [value[:, at : at + sh.block] for at in range(0, value.shape[1], sh.block)]
    return jnp.concatenate([jnp.where(allowed, part, other) for part in cut], axis=1)


def halves(sh):
    if sh.group % 2:
        return [slice(0, sh.lanes)]
    return [slice(0, sh.lanes // 2), slice(sh.lanes // 2, sh.lanes)]


def stacked_keys(keys, start, size):
    k_s, tk_s = keys
    k = k_s[pl.ds(start, size), :]
    tk = tk_s[pl.ds(start, size), :]
    left = jnp.concatenate([k, tk], axis=0)
    right = jnp.concatenate([jnp.zeros_like(k), k], axis=0)
    return jnp.concatenate([left, right], axis=1)


def pieces_of(sh, start, blocks):
    sizes = [2] * (blocks // 2) + [1] * (blocks % 2)
    firsts = [sum(sizes[:i]) for i in range(len(sizes))]
    return [
        (pl.multiple_of(start + first * sh.block, sh.block), size * sh.block, i == len(sizes) - 1)
        for i, (first, size) in enumerate(zip(firsts, sizes))
    ]


def cut_diagonal(sh, value, other):
    low = below_diagonal(sh, value[value.shape[0] - sh.block :], other)
    if value.shape[0] == sh.block:
        return low
    return jnp.concatenate([value[: value.shape[0] - sh.block], low], axis=0)


def block_rows(sh, block):
    return pl.multiple_of(block * sh.block, sh.block)


def load_state(stat, lanes):
    return tuple(stat[r : r + 1, lanes] for r in range(3))


def forward_tile(sh, keys, vt_s, acc, stat, kept, qq, block, blocks, masked):
    w = sh.width
    start = block_rows(sh, block)
    pieces = pieces_of(sh, start, blocks)
    stacked = [stacked_keys(keys, at, size) for at, size, _ in pieces]
    at = pl.ds(start, blocks * sh.block)
    lanes = halves(sh)
    scores = [[] for _ in lanes]
    mixed = [[] for _ in lanes]
    most = [None for _ in lanes]
    state = [None if masked else load_state(stat, part) for part in lanes]

    def score(h, c):
        both = nt(stacked[c], qq[lanes[h], :])
        s, d = both[: pieces[c][1]], both[pieces[c][1] :]
        if masked and pieces[c][2]:
            s = cut_diagonal(sh, s, MASKED)
        scores[h].append((s, d))

    def top(h):
        peaks = [jnp.max(s, axis=0, keepdims=True) for s, _ in scores[h]]
        most[h] = functools.reduce(jnp.maximum, peaks) * sh.scale
        if not masked:
            most[h] = jnp.maximum(most[h], state[h][0])
        if kept is not None:
            for j in range(blocks):
                kept[1][block + j, :, lanes[h]] = most[h]

    def soften(h, c):
        s, d = scores[h][c]
        e = jnp.exp(s * sh.scale - most[h])
        mixed[h].append((e.astype(BF16), (e * d).astype(BF16)))
        if kept is not None:
            kept[0][pl.ds(pieces[c][0], pieces[c][1]), lanes[h]] = mixed[h][-1][0]

    def gather(h, i):
        return jnp.concatenate([pair[i] for pair in mixed[h]], axis=0)

    def finish(h, plain, moving):
        total, cross = plain[2 * w : 2 * w + 1], moving[w : w + 1]
        tangent = plain[:w] + moving[:w] * sh.scale
        plain = plain[w : 2 * w]
        if not masked:
            decay = jnp.exp(state[h][0] - most[h])
            plain = acc[:w, lanes[h]] * decay + plain
            tangent = acc[w:, lanes[h]] * decay + tangent
            total, cross = state[h][1] * decay + total, state[h][2] * decay + cross
        acc[:w, lanes[h]] = plain
        acc[w:, lanes[h]] = tangent
        for r, value in enumerate((most[h], total, cross)):
            stat[r : r + 1, lanes[h]] = value

    for h in range(len(lanes) + 1):
        if h > 0:
            top(h - 1)
        for c in range(len(pieces)):
            if h < len(lanes):
                score(h, c)
            if h > 0:
                soften(h - 1, c)
        if h > 0:
            plain = nn(vt_s[:, at], gather(h - 1, 0))
            moving = nn(vt_s[w:, at], gather(h - 1, 1))
            finish(h - 1, plain, moving)


def by_count(sh, low, count, run, masked):
    most = min(4 if masked else 3, sh.blocks)
    head = lax.rem(count - 1, 4) + 1 if masked else lax.rem(count, 4)
    for blocks in range(1, most + 1):

        @pl.when(head == blocks)
        def _(blocks=blocks):
            run(low + count - blocks if masked else low, blocks, masked)

    def step(i, carry):
        run(low + (0 if masked else head) + 4 * i, 4, False)
        return carry

    if sh.blocks >= 4:
        lax.fori_loop(0, (count - head) // 4, step, 0)


def lay_chunk(sh, me_ref, sources, targets):
    for m, (ref, base) in enumerate(sources):
        slot = pl.ds(slot_of(me_ref, m, sh.rows), sh.rows)
        for i, target in enumerate(targets):
            at = base + i * sh.rows
            target[slot, :] = ref[at : at + sh.rows, :]


def lay_queries(sh, me_ref, order, pieces, qq):
    per = sh.rows // sh.block
    for m, ref in zip(order, pieces):
        for i in range(2):
            for g in range(sh.group):
                for r in range(per):
                    block = jnp.bitwise_xor(me_ref[0], m) * per + r
                    at = (i * sh.group + g) * sh.rows + r * sh.block
                    qq[
                        block,
                        g * sh.block : (g + 1) * sh.block,
                        i * sh.width : (i + 1) * sh.width,
                    ] = ref[at : at + sh.block, :]


def lay_span(sh, me_ref, sources, laid):
    w = sh.width
    k_s, v_s, kt_s, tk_s, vt_s, tv_s = laid
    lay_chunk(sh, me_ref, sources, (k_s, v_s, tk_s, tv_s))
    kt_s[...] = transposed(k_s[...])
    vt_s[:w, :] = transposed(tv_s[...])
    vt_s[w : 2 * w, :] = transposed(v_s[...])
    vt_s[2 * w :, :] = jnp.ones((ONES_ROWS, sh.tokens), BF16)


def transposed(x):
    return x.astype(F32).T.astype(BF16)


def located(sh, refs):
    length = refs[0].shape[0]
    return [(ref, at) for ref in refs for at in range(0, ref.shape[0], length)]


def back_of(sh, me_ref, back_ref, qb):
    per = sh.rows // sh.block
    return back_ref[jnp.bitwise_xor(me_ref[0], qb // per) * per + qb % per]


def each_block(count, run):
    def step(i, carry):
        run(i)
        return carry

    lax.fori_loop(0, count, step, 0)


def block_in_turn(sh, me_ref, order, i):
    per = sh.rows // sh.block
    if order == list(range(sh.parts)):
        return i
    partner = order[0]
    for j in range(1, len(order)):
        partner = jnp.where(i // per == j, order[j], partner)
    return jnp.bitwise_xor(me_ref[0], partner) * per + i % per


def kept_shapes(sh):
    return [
        jax.ShapeDtypeStruct((sh.blocks, sh.tokens, sh.lanes), BF16),
        jax.ShapeDtypeStruct((sh.blocks, sh.blocks, 1, sh.lanes), F32),
    ]


def forward_own(sh, me, back, order, queries, chunk, before):
    w = sh.width
    first = before is None
    turns = len(order) * (sh.rows // sh.block)

    def kernel(me_ref, back_ref, *refs):
        refs = list(refs)

        def take(count):
            taken = refs[:count]
            del refs[:count]
            return taken

        q_in = take(len(order))
        if first:
            kv_in = take(len(chunk))
            accs, stats, qq_s, es, ms = take(5)
            laid = refs
            lay_span(sh, me_ref, located(sh, kv_in), laid)
        else:
            laid = take(len(chunk))
            take(5)
            accs, stats, qq_s, es, ms = refs
        k_s, _, _, tk_s, vt_s = laid[:5]
        lay_queries(sh, me_ref, order, q_in, qq_s)

        def query_block(i):
            qb = block_in_turn(sh, me_ref, order, i)
            low = jnp.clip(qb - back_of(sh, me_ref, back_ref, qb), 0, qb)
            run = functools.partial(
                forward_tile,
                sh,
                (k_s, tk_s),
                vt_s,
                accs.at[qb],
                stats.at[qb],
                (es.at[qb], ms.at[qb]),
                qq_s[qb],
            )
            by_count(sh, low, qb + 1 - low, run, True)

        each_block(turns, query_block)

    def array(*shape, dtype=F32):
        return jax.ShapeDtypeStruct(shape, dtype)

    span = array(sh.tokens, w, dtype=BF16)
    out_shape = [
        array(sh.blocks, 2 * w, sh.lanes),
        array(sh.blocks, 8, sh.lanes),
        array(sh.blocks, sh.lanes, 2 * w, dtype=BF16),
        *kept_shapes(sh),
    ]
    operands = [*queries, *chunk]
    aliases = {}
    if first:
        out_shape += [span, span, array(w, sh.tokens, dtype=BF16), span]
        out_shape.append(array(2 * w + ONES_ROWS, sh.tokens, dtype=BF16))
    else:
        aliases = {2 + len(operands) + i: i for i in range(5)}
        operands += before
    work = sh.group * sh.tokens * sh.block * turns // 2
    return pl.pallas_call(
        kernel,
        in_specs=[SMEM, SMEM] + [VMEM] * len(operands),
        out_specs=[VMEM] * len(out_shape),
        out_shape=out_shape,
        input_output_aliases=aliases,
        scratch_shapes=[pltpu.VMEM((sh.tokens, w), BF16)] * first,
        compiler_params=params(),
        cost_estimate=cost(12 * work * w, 4 * sh.tokens * sh.lanes, work),
        name="forward_own",
    )(me, back, *operands)


def forward_chunk(sh, me, back, qq, chunk, distance, state, gain_square=None):
    w = sh.width
    closing = gain_square is not None

    def kernel(me_ref, back_ref, qq_s, *refs):
        refs = list(refs)

        def take(count):
            taken = refs[:count]
            del refs[:count]
            return taken

        kv_in = take(len(chunk))
        take(2)
        if closing:
            (gain_ref,) = take(1)
        k_s, v_s, kt_s, accs, stats = take(5)
        last = take(2)
        if closing:
            lse, sums = last
        tk_s, tv_s, vt_s = refs
        lay_span(sh, me_ref, located(sh, kv_in), (k_s, v_s, kt_s, tk_s, vt_s, tv_s))

        def query_block(qb):
            acc, stat = accs.at[qb], stats.at[qb]
            first = qb - back_of(sh, me_ref, back_ref, qb) + distance * sh.blocks
            first = jnp.clip(first, 0, sh.blocks)
            count = sh.blocks - first

            @pl.when(count > 0)
            def _():
                kept = None if closing else [ref.at[qb] for ref in last]
                run = functools.partial(
                    forward_tile, sh, (k_s, tk_s), vt_s, acc, stat, kept, qq_s[qb]
                )
                by_count(sh, first, count, run, False)

            if closing:
                most, total, cross = load_state(stat, slice(None))
                inverse = 1.0 / total
                plain = acc[:w, :] * inverse
                moved = acc[w:, :] * inverse - (cross * inverse * sh.scale) * plain
                acc[:w, :] = plain
                acc[w:, :] = moved
                lse[qb] = most + jnp.log(total)
                square = plain * plain
                product = plain * moved
                gain = gain_ref[...]
                for r, value in enumerate((square, product, gain * square, gain * product)):
                    line = jnp.sum(value, axis=0, keepdims=True)
                    pieces = [line[:, g * sh.block : (g + 1) * sh.block] for g in range(sh.group)]
                    sums[qb, r : r + 1, :] = functools.reduce(jnp.add, pieces)

        each_block(sh.blocks, query_block)

    def array(*shape, dtype=F32):
        return jax.ShapeDtypeStruct(shape, dtype)

    out_shape = [
        array(sh.tokens, w, dtype=BF16),
        array(sh.tokens, w, dtype=BF16),
        array(w, sh.tokens, dtype=BF16),
        array(sh.blocks, 2 * w, sh.lanes),
        array(sh.blocks, 8, sh.lanes),
    ]
    if closing:
        out_shape += [array(sh.blocks, 1, sh.lanes), array(sh.blocks, 4, sh.block)]
    else:
        out_shape += kept_shapes(sh)
    operands = [qq, *chunk]
    aliases = {2 + len(operands): 3, 3 + len(operands): 4}
    operands += state
    if closing:
        operands.append(gain_square)
    work = sh.group * sh.tokens * sh.tokens // 2
    return pl.pallas_call(
        kernel,
        in_specs=[SMEM, SMEM] + [VMEM] * len(operands),
        out_specs=[VMEM] * len(out_shape),
        out_shape=out_shape,
        input_output_aliases=aliases,
        scratch_shapes=[
            pltpu.VMEM((sh.tokens, w), BF16),
            pltpu.VMEM((sh.tokens, w), BF16),
            pltpu.VMEM((2 * w + ONES_ROWS, sh.tokens), BF16),
        ],
        compiler_params=params(),
        cost_estimate=cost(24 * work * w, 12 * sh.tokens * sh.lanes * 2, work),
        name="forward_far" if closing else "forward_chunk",
    )(me, back, *operands)


def backward_tile(sh, keys, kt_s, dkv_s, dq_s, qg, lse, dot, block, blocks, _):
    start, size = block_rows(sh, block), blocks * sh.block
    rows = pl.ds(start, size)
    k_s, v_s = keys
    k, v = k_s[rows, :], v_s[rows, :]
    empty = jnp.zeros_like(k)
    left = jnp.concatenate([k, empty], axis=0)
    right = jnp.concatenate([empty, v], axis=0)
    stacked = jnp.concatenate([left, right], axis=1)
    scores = [nt(stacked, qg[lanes, :]) for lanes in halves(sh)]
    for lanes, both in zip(halves(sh), scores):
        p = jnp.exp(both[:size] * sh.scale - lse[:, lanes])
        ds = (p * (both[size:] - dot[:, lanes])).astype(BF16)
        dkv_s[0, rows, :] += nn(ds, qg[lanes, : sh.width])
        dkv_s[1, rows, :] += nn(p.astype(BF16), qg[lanes, sh.width :])
        dq_s[:, lanes] += nn(kt_s[:, rows], ds)


def backward_kept(sh, keys, kt_s, dkv_s, dq_s, qg, lse, dot, kept, block, blocks, _):
    start, size = block_rows(sh, block), blocks * sh.block
    rows = pl.ds(start, size)
    v = keys[1][rows, :]
    slopes = [nt(v, qg[lanes, sh.width :]) for lanes in halves(sh)]
    for lanes, slope in zip(halves(sh), slopes):
        parts = []
        for j in range(blocks):
            factor = jnp.exp(kept[1][block + j, :, lanes] - lse[:, lanes])
            at = pl.ds(block_rows(sh, block + j), sh.block)
            parts.append(kept[0][at, lanes].astype(F32) * factor)
        p = jnp.concatenate(parts, axis=0)
        ds = (p * (slope - dot[:, lanes])).astype(BF16)
        dkv_s[0, rows, :] += nn(ds, qg[lanes, : sh.width])
        dkv_s[1, rows, :] += nn(p.astype(BF16), qg[lanes, sh.width :])
        dq_s[:, lanes] += nn(kt_s[:, rows], ds)


def backward_chunk(sh, me, back, qq, keys, distance, grads, lse, dots, dq, norm, order, held):
    w = sh.width
    opening, closing = norm is not None, distance == 0
    per = sh.rows // sh.block

    def kernel(me_ref, back_ref, *refs):
        refs = list(refs)

        def take(count):
            taken = refs[:count]
            del refs[:count]
            return taken

        qq_s, k_s, v_s, kt_s = take(4)
        kept = take(len(keys) - 3)
        (lse_s,) = take(1)
        if opening:
            out_s, gain_ref, *sum_refs = take(2 + len(norm[0]))
        else:
            grad_s, dot_s, dq_in = take(3)
        (held_ref,) = take(1) if held is not None else (None,)
        (dkv_out,) = take(1)
        dq_out = take(len(order) if closing else 1)
        if opening:
            grad_s, dot_s = take(2)
        dkv_s, dq_own = (dkv_out, *refs) if closing else refs
        if held_ref is None:
            dkv_s[...] = jnp.zeros_like(dkv_s)

        def query_block(i):
            qb = block_in_turn(sh, me_ref, order, i)
            dq_s = dq_own if closing else dq_out[0].at[qb]
            if opening:
                features = norm[2]
                token = functools.reduce(jnp.add, [ref[qb] for ref in sum_refs])
                sums = jnp.concatenate([token] * sh.group, axis=1)
                square = sums[0:1] / features + EPSILON
                inverse = lax.rsqrt(square)
                ratio = sums[1:2] / (features * square)
                again = (sums[3:4] - ratio * sums[2:3]) * inverse
                again = again / (features * square)
                plain = out_s[qb, :w, :]
                moved = out_s[qb, w:, :]
                first_grad = gain_ref[...] * (moved - plain * ratio) * inverse
                cot = ((first_grad - plain * again) * inverse).astype(BF16).astype(F32)
                dot_s[qb] = jnp.sum(cot * plain, axis=0, keepdims=True)
                grad_s[qb] = cot.T.astype(BF16)
                dq_s[...] = jnp.zeros((w, sh.lanes), F32)
            elif closing:
                dq_s[...] = dq_in[qb]

            top = sh.blocks if distance else qb + 1
            first = jnp.clip(qb - back_of(sh, me_ref, back_ref, qb) + distance * sh.blocks, 0, top)
            count = top - first

            @pl.when(count > 0)
            def _():
                qg = jnp.concatenate([qq_s[qb, :, :w], grad_s[qb]], axis=1)
                common = (sh, (k_s, v_s), kt_s, dkv_s, dq_s, qg, lse_s[qb], dot_s[qb])
                if kept:
                    run = functools.partial(backward_kept, *common, [ref.at[qb] for ref in kept])
                else:
                    run = functools.partial(backward_tile, *common)
                by_count(sh, first, count, run, False)

            if closing:
                done = (dq_s[...] * sh.scale).T.reshape(sh.group, sh.block, w).astype(BF16)
                at = pl.ds(pl.multiple_of(i % per * sh.block, sh.block), sh.block)
                for j, out in enumerate(dq_out):

                    @pl.when(i // per == j)
                    def _(out=out):
                        out[:, at, :] = done

        each_block(len(order) * per, query_block)
        if not closing:
            dkv_out[0] = (dkv_s[0] * sh.scale).astype(BF16)
            dkv_out[1] = dkv_s[1].astype(BF16)

    def array(*shape, dtype=F32):
        return jax.ShapeDtypeStruct(shape, dtype)

    operands = [qq, *keys, lse]
    if opening:
        operands += [grads, norm[1], *norm[0]]
    else:
        operands += [grads, dots, dq]
    aliases = {}
    if not opening and not closing:
        aliases = {1 + len(operands): 1}
    if held is not None:
        aliases = {2 + len(operands): 0}
        operands.append(held)
    out_shape = [array(2, sh.tokens, w, dtype=F32 if closing else BF16)]
    if closing:
        out_shape += [array(sh.group, sh.rows, w, dtype=BF16)] * len(order)
    else:
        out_shape.append(array(sh.blocks, w, sh.lanes))
    if opening:
        out_shape += [
            array(sh.blocks, sh.lanes, w, dtype=BF16),
            array(sh.blocks, 1, sh.lanes),
        ]
    work = sh.group * sh.tokens * len(order) * sh.rows // 2
    return pl.pallas_call(
        kernel,
        in_specs=[SMEM, SMEM] + [VMEM] * len(operands),
        out_specs=[VMEM] * len(out_shape),
        out_shape=out_shape,
        input_output_aliases=aliases,
        scratch_shapes=[pltpu.VMEM((2, sh.tokens, w), F32)] * (not closing)
        + [pltpu.VMEM((w, sh.lanes), F32)],
        compiler_params=params(),
        cost_estimate=cost(1, 1) if closing else cost(20 * work * w, 16 * work, work),
        name="backward_chunk",
    )(me, back, *operands)


def combine(sh, me, arrived, held):
    count = len(arrived)

    def kernel(me_ref, held_ref, *refs):
        for m, out in enumerate(refs[count:]):
            slot = pl.ds(slot_of(me_ref, m, sh.rows), sh.rows)
            for a, factor in ((0, sh.scale), (1, 1.0)):
                part = held_ref[a, slot, :] * factor
                for ref in refs[:count]:
                    part += ref[a, slot, :].astype(F32)
                out[a] = part.astype(BF16)

    return pl.pallas_call(
        kernel,
        in_specs=[SMEM] + [VMEM] * (1 + count),
        out_specs=[VMEM] * sh.parts,
        out_shape=[jax.ShapeDtypeStruct((2, sh.rows, sh.width), BF16)] * sh.parts,
        compiler_params=params(),
        cost_estimate=cost(0, 1),
        name="combine",
    )(me, held, *arrived)


def exchanged_with(piece, parts, m):
    return lax.ppermute(piece, "part", [(i, i ^ m) for i in range(parts)]) if m else piece


def exchanged(pieces, parts):
    return [exchanged_with(piece, parts, m) for m, piece in enumerate(pieces)]


def moved_on(value, steps):
    count = lax.axis_size("span")
    pairs = [(i, i + steps) for i in range(count) if 0 <= i + steps < count]
    return lax.ppermute(value, "span", pairs)


def summed_over_head(value):
    count = lax.axis_size("head")
    if count & (count - 1):
        return lax.psum(value, "head")
    step = 1
    while step < count:
        value = value + lax.ppermute(value, "head", [(i, i ^ step) for i in range(count)])
        step *= 2
    return value


def body(queries, keys, values, tangent_queries, tangent_keys, tangent_values, doc_start, out_gain):
    rows, query_heads, width = queries.shape
    key_heads = keys.shape[1]
    group = query_heads // key_heads
    parts = lax.axis_size("part")
    per = doc_start.shape[0]
    block = rows // per
    features = query_heads * width * lax.axis_size("head")
    hops = -(-DOC_DEVS // parts)
    sh = Shape(parts, group, rows, width, block)
    place = lax.axis_index("part")
    me = place.astype(jnp.int32).reshape(1)

    def flat(array):
        return array.reshape(-1, width)

    pieces = split_heads(
        [flat(a) for a in (keys, values, tangent_keys, tangent_values)], parts, 1, doc_start
    )
    q_rows, _ = lax.optimization_barrier(((flat(queries), flat(tangent_queries)), pieces[0]))
    q_pieces = split_heads(q_rows, parts, group)
    own = moved_on(pieces[0], 1)
    pieces = exchanged(pieces, parts)
    chunks = [pieces]
    if parts > 1:
        own, q_pieces = lax.optimization_barrier((own, q_pieces))
        owns = [own]
        for _ in range(hops - 1):
            owns.append(moved_on(owns[-1], 1))
        late, owns = lax.optimization_barrier((pieces[1:], owns))
        rest = jnp.concatenate([moved_on(piece, 1) for piece in late], axis=0)
        chunks.append([owns[0], rest])
        for own in owns[1:]:
            rest = moved_on(rest, 1)
            chunks.append([own, rest])
    else:
        for _ in range(hops):
            chunks.append([own])
            own = moved_on(own, 1)
    q_parts = exchanged(q_pieces[:-1], parts)
    if parts > 1:
        last, _ = lax.optimization_barrier((q_pieces[-1], q_parts[min(1, parts - 2)]))
        q_parts.append(exchanged_with(last, parts, parts - 1))
    else:
        q_parts = q_pieces
    back = jnp.concatenate([p[4 * rows : 4 * rows + per, 0] for p in pieces]).astype(jnp.int32)
    gain = lax.dynamic_index_in_dim(out_gain.reshape(key_heads, group, width), place, 0, False)
    gain_square = jnp.repeat((gain * gain).T, block, axis=1)

    everyone = list(range(parts))
    before, laid = None, chunks[0]
    for order in [everyone[:1], everyone[1:-1], everyone[-1:]] if parts > 1 else [everyone]:
        if order:
            turn = forward_own(sh, me, back, order, [q_parts[m] for m in order], laid, before)
            laid = turn[5:] or laid
            before = list(turn[:5])
    state, qq = before[:2], before[2]
    spans = [(*laid[:3], *before[3:])]
    for distance in range(1, hops):
        k, v, kt, acc, stat, *kept = forward_chunk(
            sh, me, back, qq, chunks[distance], distance, state
        )
        state = [acc, stat]
        spans.append((k, v, kt, *kept))
    k, v, kt, out, _, lse, sums = forward_chunk(
        sh, me, back, qq, chunks[hops], hops, state, gain_square
    )
    spans.append((k, v, kt))
    norm = (exchanged([summed_over_head(sums)] * parts, parts), gain_square, features)

    part, dq, grads, dots = backward_chunk(
        sh, me, back, qq, spans[hops], hops, out, lse, None, None, norm, everyone, None
    )
    arrived = [moved_on(part, -hops)]
    for distance in range(hops - 1, 0, -1):
        part, dq = backward_chunk(
            sh, me, back, qq, spans[distance], distance, grads, lse, dots, dq, None,
            everyone, None,
        )
        arrived.append(moved_on(part, -distance))
    turns = [turn[::-1] for turn in (everyone[-1:], everyone[:-1]) if turn]
    held, dq_pieces = None, [None] * parts
    for order in turns:
        if held is not None:
            arrived[0], held = lax.optimization_barrier((arrived[0], held))
        held, *done = backward_chunk(
            sh, me, back, qq, spans[0], 0, grads, lse, dots, dq, None, order, held
        )
        for m, piece in zip(order, done):
            dq_pieces[m] = piece.reshape(1, group, rows, width)
    dq_pieces = exchanged(dq_pieces, parts)
    dq_pieces[-1], held = lax.optimization_barrier((dq_pieces[-1], held))
    dkv_pieces = exchanged(combine(sh, me, arrived, held), parts)
    (product_queries,) = join_heads(dq_pieces, 1, group)
    dkv_pieces = [p.reshape(2, 1, rows, width) for p in dkv_pieces]
    product_keys, product_values = join_heads(dkv_pieces, 2, 1)
    return (
        product_queries.reshape(queries.shape),
        product_keys.reshape(keys.shape),
        product_values.reshape(keys.shape),
    )


def solution(mesh):
    def run(*arguments):
        count, heads = mesh.shape["ctx"], mesh.shape["head"]
        parts = arguments[1].shape[1] // heads
        split = Mesh(
            mesh.devices.reshape(count // parts, parts, heads), ("span", "part", "head")
        )
        ctx = ("span", "part")
        array = P(ctx, "head", None)
        return jax.shard_map(
            body,
            mesh=split,
            in_specs=(array,) * 6 + (P(ctx), P("head")),
            out_specs=(array,) * 3,
            check_vma=False,
        )(*arguments)

    return run
```

profile of v0, /device:TPU:8, one launch (start us, length us, event | category | flops | bytes accessed | tf_op | source)
XLA Modules:
  0.0 131.1 jit_solution(11249972285526185960)
XLA Ops:
  0.6 2.9 %split_heads.2 = (bf16[1040,128]{1,0:T(8,128)(2,1)}, bf16[1040,128]{1,0:T(8,128)(2,1)}, bf16[1040,128]{1,0:T(8,128)(2,1)}, bf16[1040,128]{1,0:T(8,128)(2,1)}) custom-call(s32[2]{0:T(128)} %refs_0_.1, bf16[1024,128]{1,0:T(8,128)(2,1)} %bitcast.41, bf16[1024,128]{1,0:T(8,128)(2,1)} %bitcast.42, bf16[1024,128]{1,0:T(8,128)(2,1)} %bitcast.43, ...), custom_call_target="tpu_custom_call" | custom-call | bytes 2097152 | tf_op jit(solution)/shard_map/split_heads/pallas_call | solution.py:99
  3.5 3.5 %collective-permute-start.3 = (bf16[1040,128]{1,0:T(8,128)(2,1)}, bf16[1040,128]{1,0:T(8,128)(2,1)S(1)}, u32[]{:S(2)}, u32[]{:S(2)}) collective-permute-start(bf16[1040,128]{1,0:T(8,128)(2,1)} %get-tuple-element.79.refs_1_), channel_id=1, source_target_pairs={{0,8},{8,16},{16,24},{1,9},{9,17},{17,25},{2,10},{10,18},{18,26},{... | collective-permute-start | bytes 798728 | tf_op jit(solution)/shard_map/ppermute | solution.py:715
  7.0 2.5 %collective-permute-start.2 = (bf16[1040,128]{1,0:T(8,128)(2,1)}, bf16[1040,128]{1,0:T(8,128)(2,1)S(1)}, u32[]{:S(2)}, u32[]{:S(2)}) collective-permute-start(bf16[1040,128]{1,0:T(8,128)(2,1)} %get-tuple-element.82), channel_id=1, source_target_pairs={{0,6},{2,4},{4,2},{6,0},{1,7},{3,5},{5,3},{7,1},{8,14},{10,12},{12... | collective-permute-start | bytes 798728 | tf_op jit(solution)/shard_map/ppermute | solution.py:705
  9.5 0.5 collective-permute-start.1
  10.1 0.5 collective-permute-start
  10.6 0.8 slice_reduce_fusion.3
  11.4 1.2 copy-done
  12.6 1.2 copy-done.1
  13.8 2.2 %split_heads.3 = (bf16[2048,128]{1,0:T(8,128)(2,1)S(1)}, bf16[2048,128]{1,0:T(8,128)(2,1)S(1)}, bf16[2048,128]{1,0:T(8,128)(2,1)S(1)}, bf16[2048,128]{1,0:T(8,128)(2,1)S(1)}) custom-call(bf16[4096,128]{1,0:T(8,128)(2,1)S(1)} %bitcast.27, bf16[4096,128]{1,0:T(8,128)(2,1)S(1)} %bitcast.28), custom_call_target="tpu_custom_call" | custom-call | bytes 4194304 | tf_op jit(solution)/shard_map/split_heads/pallas_call | solution.py:99
  16.0 3.5 %collective-permute-start.7 = (bf16[1040,128]{1,0:T(8,128)(2,1)S(1)}, bf16[1040,128]{1,0:T(8,128)(2,1)S(1)}, u32[]{:S(2)}, u32[]{:S(2)}) collective-permute-start(bf16[1040,128]{1,0:T(8,128)(2,1)S(1)} %collective-permute-done.3.refs_0_), channel_id=1, source_target_pairs={{0,8},{8,16},{16,24},{1,9},{9,17},{17,25},{2,10},{10,18},{18,26},{... | collective-permute-start | bytes 798728 | tf_op jit(solution)/shard_map/ppermute | solution.py:715
  19.5 0.7 multiply_bitcast_fusion
  20.2 0.1 copy.27
  20.3 0.2 broadcast_in_dim.3
  20.6 1.6 %collective-permute-start.4 = (bf16[2048,128]{1,0:T(8,128)(2,1)S(1)}, bf16[2048,128]{1,0:T(8,128)(2,1)S(1)}, u32[]{:S(2)}, u32[]{:S(2)}) collective-permute-start(bf16[2048,128]{1,0:T(8,128)(2,1)S(1)} %get-tuple-element.90), channel_id=1, source_target_pairs={{0,2},{2,0},{4,6},{6,4},{1,3},{3,1},{5,7},{7,5},{8,10},{10,8},{12,... | collective-permute-start | bytes 1572872 | tf_op jit(solution)/shard_map/ppermute | solution.py:705
  22.1 0.0 collective-permute-done.2.refs_4_
  22.1 1.5 %collective-permute-start.6 = (bf16[2048,128]{1,0:T(8,128)(2,1)S(1)}, bf16[2048,128]{1,0:T(8,128)(2,1)S(1)}, u32[]{:S(2)}, u32[]{:S(2)}) collective-permute-start(bf16[2048,128]{1,0:T(8,128)(2,1)S(1)} %get-tuple-element.98), channel_id=1, source_target_pairs={{0,4},{2,6},{4,0},{6,2},{1,5},{3,7},{5,1},{7,3},{8,12},{10,14},{12... | collective-permute-start | bytes 1572872 | tf_op jit(solution)/shard_map/ppermute | solution.py:705
  23.6 0.1 slice_reduce_fusion
  23.8 0.0 collective-permute-done.1.refs_3_
  23.8 0.1 slice_reduce_fusion.1
  23.9 1.1 collective-permute-done.7.refs_0_
  24.9 3.5 %collective-permute-start.8 = (bf16[1040,128]{1,0:T(8,128)(2,1)S(1)}, bf16[1040,128]{1,0:T(8,128)(2,1)S(1)}, u32[]{:S(2)}, u32[]{:S(2)}) collective-permute-start(bf16[1040,128]{1,0:T(8,128)(2,1)S(1)} %collective-permute-done.refs_2_), channel_id=1, source_target_pairs={{0,8},{8,16},{16,24},{1,9},{9,17},{17,25},{2,10},{10,18},{18,26},{... | collective-permute-start | bytes 798728 | tf_op jit(solution)/shard_map/ppermute | solution.py:715
  28.4 0.1 slice_reduce_fusion.2
  28.5 0.1 maximum_convert_fusion.back_ref
  28.6 2.2 %collective-permute-start.9 = (bf16[1040,128]{1,0:T(8,128)(2,1)S(1)}, bf16[1040,128]{1,0:T(8,128)(2,1)S(1)}, u32[]{:S(2)}, u32[]{:S(2)}) collective-permute-start(bf16[1040,128]{1,0:T(8,128)(2,1)S(1)} %collective-permute-done.1.refs_3_), channel_id=1, source_target_pairs={{0,8},{8,16},{16,24},{1,9},{9,17},{17,25},{2,10},{10,18},{18,26},{... | collective-permute-start | bytes 798728 | tf_op jit(solution)/shard_map/ppermute | solution.py:715
  30.8 0.0 copy-start.2
  30.8 0.9 copy-done.2
  31.8 2.0 %forward_own.3 = (f32[8,256,512]{2,1,0:T(8,128)S(1)}, f32[8,8,512]{2,1,0:T(8,128)S(1)}, bf16[8,512,256]{2,1,0:T(8,128)(2,1)S(1)}, bf16[8,1024,512]{2,1,0:T(8,128...) custom-call(s32[1]{0:T(128)} %bitcast.me_ref, ...), custom_call_target="tpu_custom_call" | custom-call | flops 805306368 | bytes 2097152 | tf_op jit(solution)/shard_map/forward_own/pallas_call | solution.py:422
  33.8 2.1 %collective-permute-start.10 = (bf16[1040,128]{1,0:T(8,128)(2,1)S(1)}, bf16[1040,128]{1,0:T(8,128)(2,1)S(1)}, u32[]{:S(2)}, u32[]{:S(2)}) collective-permute-start(bf16[1040,128]{1,0:T(8,128)(2,1)S(1)} %collective-permute-done.2.refs_4_), channel_id=1, source_target_pairs={{0,8},{8,16},{16,24},{1,9},{9,17},{17,25},{2,10},{10,18},{18,26},{... | collective-permute-start | bytes 798728 | tf_op jit(solution)/shard_map/ppermute | solution.py:715
  35.9 0.0 collective-permute-done.4.refs_0_
  35.9 5.1 %collective-permute-start.5 = (bf16[2048,128]{1,0:T(8,128)(2,1)S(1)}, bf16[2048,128]{1,0:T(8,128)(2,1)S(1)}, u32[]{:S(2)}, u32[]{:S(2)}) collective-permute-start(bf16[2048,128]{1,0:T(8,128)(2,1)S(1)} %get-tuple-element.91), channel_id=1, source_target_pairs={{0,6},{2,4},{4,2},{6,0},{1,7},{3,5},{5,3},{7,1},{8,14},{10,12},{12... | collective-permute-start | bytes 1572872 | tf_op jit(solution)/shard_map/ppermute | solution.py:705
  41.0 0.6 collective-permute-done.9
  41.6 3.0 %collective-permute-done.10 = bf16[1040,128]{1,0:T(8,128)(2,1)S(1)} collective-permute-done((bf16[1040,128]{1,0:T(8,128)(2,1)S(1)}, bf16[1040,128]{1,0:T(8,128)(2,1)S(1)}, u32[]{:S(2)}, u32[]{:S(2)}) %collective-permute-start.10) | collective-permute-done | bytes 266272 | tf_op jit(solution)/shard_map/ppermute | solution.py:715
  44.7 3.3 %collective-permute-start.11 = (bf16[3120,128]{1,0:T(8,128)(2,1)S(1)}, bf16[3120,128]{1,0:T(8,128)(2,1)S(1)}, u32[]{:S(2)}, u32[]{:S(2)}) collective-permute-start(bf16[3120,128]{1,0:T(8,128)(2,1)S(1)} %constant_dynamic-update-slice_fusion.refs_1_), channel_id=1, source_target_pairs={{0,8},{8,16},{16,24},{1,9},{9,17},{17,25},{2,10},{10,18},{18,26},{... | collective-permute-start | bytes 2396168 | tf_op jit(solution)/shard_map/ppermute | solution.py:715
  48.0 0.0 collective-permute-done.6.refs_1_
  48.1 3.7 %forward_own.4 = (f32[8,256,512]{2,1,0:T(8,128)S(1)}, f32[8,8,512]{2,1,0:T(8,128)S(1)}, bf16[8,512,256]{2,1,0:T(8,128)(2,1)S(1)}, bf16[8,1024,512]{2,1,0:T(8,128)(2,1)S(1)}, f32[8,8,1,512]{3,2,1,0:T(1,128)S(1)}) custom-call(s32[1]{0:T(128)} %bitcast.me_ref, ...), custom_call_target="tpu_custom_call", output_to_operand_aliasing={{0}: (9, {}), {1}: (10, {}), {2}: (11, {}), {3}: (12, {}), ... | custom-call | flops 1610612736 | bytes 2097152 | tf_op jit(solution)/shard_map/forward_own/pallas_call | solution.py:422
  51.7 3.2 %forward_own.5 = (f32[8,256,512]{2,1,0:T(8,128)S(1)}, f32[8,8,512]{2,1,0:T(8,128)S(1)}, bf16[8,512,256]{2,1,0:T(8,128)(2,1)S(1)}, bf16[8,1024,512]{2,1,0:T(8,128)(2,1)S(1)}, f32[8,8,1,512]{3,2,1,0:T(1,128)S(1)}) custom-call(s32[1]{0:T(128)} %bitcast.me_ref, ...), custom_call_target="tpu_custom_call", output_to_operand_aliasing={{0}: (8, {}), {1}: (9, {}), {2}: (10, {}), {3}: (11, {}), {... | custom-call | flops 805306368 | bytes 2097152 | tf_op jit(solution)/shard_map/forward_own/pallas_call | solution.py:422
  55.0 1.1 forward_chunk.1
  56.0 7.8 %collective-permute-done.11.refs_1_ = bf16[3120,128]{1,0:T(8,128)(2,1)S(1)} collective-permute-done((bf16[3120,128]{1,0:T(8,128)(2,1)S(1)}, bf16[3120,128]{1,0:T(8,128)(2,1)S(1)}, u32[]{:S(2)}, u32[]{:S(2)}) %collective-permute-start.11) | collective-permute-done | bytes 798752 | tf_op jit(solution)/shard_map/ppermute | solution.py:715
  63.8 2.2 %forward_far.1 = (bf16[1024,128]{1,0:T(8,128)(2,1)S(1)}, bf16[1024,128]{1,0:T(8,128)(2,1)S(1)}, bf16[128,1024]{1,0:T(8,128)(2,1)S(1)}, f32[8,256,512]{2,1,0:T(8,...) custom-call(s32[1]{0:T(128)} %bitcast.me_ref, ...), custom_call_target="tpu_custom_call", output_to_operand_aliasing={{3}: (5, {}), {4}: (6, {})} | custom-call | flops 6442450944 | bytes 12582912 | tf_op jit(solution)/shard_map/forward_far/pallas_call | solution.py:510
  66.0 0.1 collective-permute-start.12
  66.1 1.2 collective-permute-done.12
  67.2 1.5 %collective-permute-start.13 = (f32[8,4,128]{2,1,0:T(4,128)S(1)}, f32[8,4,128]{2,1,0:T(4,128)S(1)}, u32[]{:S(2)}, u32[]{:S(2)}) collective-permute-start(f32[8,4,128]{2,1,0:T(4,128)S(1)} %add.8.refs_7_), channel_id=1, source_target_pairs={{0,2},{2,0},{4,6},{6,4},{1,3},{3,1},{5,7},{7,5},{8,10},{10,8},{12,... | collective-permute-start | bytes 49160 | tf_op jit(solution)/shard_map/ppermute | solution.py:705
  68.7 2.4 %collective-permute-start.14 = (f32[8,4,128]{2,1,0:T(4,128)S(1)}, f32[8,4,128]{2,1,0:T(4,128)S(1)}, u32[]{:S(2)}, u32[]{:S(2)}) collective-permute-start(f32[8,4,128]{2,1,0:T(4,128)S(1)} %add.8.refs_7_), channel_id=1, source_target_pairs={{0,4},{2,6},{4,0},{6,2},{1,5},{3,7},{5,1},{7,3},{8,12},{10,14},{12... | collective-permute-start | bytes 49160 | tf_op jit(solution)/shard_map/ppermute | solution.py:705
  71.1 1.7 %collective-permute-done.14.refs_9_ = f32[8,4,128]{2,1,0:T(4,128)S(1)} collective-permute-done((f32[8,4,128]{2,1,0:T(4,128)S(1)}, f32[8,4,128]{2,1,0:T(4,128)S(1)}, u32[]{:S(2)}, u32[]{:S(2)}) %collective-permute-start.14) | collective-permute-done | bytes 16416 | tf_op jit(solution)/shard_map/ppermute | solution.py:705
  72.8 2.9 %collective-permute-done.15.refs_10_ = f32[8,4,128]{2,1,0:T(4,128)S(1)} collective-permute-done((f32[8,4,128]{2,1,0:T(4,128)S(1)}, f32[8,4,128]{2,1,0:T(4,128)S(1)}, u32[]{:S(2)}, u32[]{:S(2)}) %collective-permute-start.15) | collective-permute-done | bytes 16416 | tf_op jit(solution)/shard_map/ppermute | solution.py:705
  75.7 2.4 %backward_chunk.4 = (bf16[2,1024,128]{2,1,0:T(8,128)(2,1)S(1)}, f32[8,128,512]{2,1,0:T(8,128)S(1)}, bf16[8,512,128]{2,1,0:T(8,128)(2,1)S(1)}, f32[8,1,512]{2,1,0:T(1,128)S(1)}) custom-call(s32[1]{0:T(128)} %bitcast.me_ref, s32[8]{0:T(128)S(1)} %maximum_convert_fusion.back_ref, bf16[8,512,256]{2,1,0:T(8,128)(2,1)S(1)} %get-tuple-element.109.qq_s.refs_0_, ...), custom_call_target="tpu_custom_call" | custom-call | flops 5368709120 | bytes 33554432 | tf_op jit(solution)/shard_map/backward_chunk/pallas_call | solution.py:667
  78.1 1.3 collective-permute-start.16
  79.4 0.9 backward_chunk.5
  80.3 1.9 %collective-permute-start.20 = (bf16[2,1024,128]{2,1,0:T(8,128)(2,1)S(1)}, bf16[2,1024,128]{2,1,0:T(8,128)(2,1)S(1)}, u32[]{:S(2)}, u32[]{:S(2)}) collective-permute-start(bf16[2,1024,128]{2,1,0:T(8,128)(2,1)S(1)} %get-tuple-element.148), channel_id=1, source_target_pairs={{8,0},{16,8},{24,16},{9,1},{17,9},{25,17},{10,2},{18,10},{26,18},{... | collective-permute-start | bytes 1572872 | tf_op jit(solution)/shard_map/ppermute | solution.py:715
  82.2 2.7 %backward_chunk.6 = (f32[2,1024,128]{2,1,0:T(8,128)S(1)}, bf16[4,256,128]{2,1,0:T(8,128)(2,1)S(1)}) custom-call(s32[1]{0:T(128)} %bitcast.me_ref, s32[8]{0:T(128)S(1)} %maximum_convert_fusion.back_ref, bf16[8,512,256]{2,1,0:T(8,128)(2,1)S(1)} %get-tuple-element.109.qq_s.refs_0_, bf16[1024,128]{1,0:T(8,128)(2,1)S(1)} %get-tuple-element.93.refs_2_.refs_1_, ...), custom_call_target="tpu_custom_call" | custom-call | flops 1 | bytes 1 | tf_op jit(solution)/shard_map/backward_chunk/pallas_call | solution.py:667
  84.9 0.1 collective-permute-start.19
  85.0 17.1 %collective-permute-done.16.refs_0_ = bf16[2,1024,128]{2,1,0:T(8,128)(2,1)S(1)} collective-permute-done((bf16[2,1024,128]{2,1,0:T(8,128)(2,1)S(1)}, bf16[2,1024,128]{2,1,0:T(8,128)(2,1)S(1)}, u32[]{:S(2)}, u32[]{:S(2)}) %collective-permute-start.16) | collective-permute-done | bytes 524320 | tf_op jit(solution)/shard_map/ppermute | solution.py:715
  102.1 4.3 %backward_chunk.7 = (f32[2,1024,128]{2,1,0:T(8,128)S(1)}, bf16[4,256,128]{2,1,0:T(8,128)(2,1)S(1)}, bf16[4,256,128]{2,1,0:T(8,128)(2,1)S(1)}, bf16[4,256,128]{2,1,0:T(8,128)(2,1)S(1)}) custom-call(s32[1]{0:T(128)} %bitcast.me_ref, s32[8]{0:T(128)S(1)} %maximum_convert_fusion.back_ref, ...), custom_call_target="tpu_custom_call", output_to_operand_aliasing={{0}: (12, {})} | custom-call | flops 1 | bytes 1 | tf_op jit(solution)/shard_map/backward_chunk/pallas_call | solution.py:667
  106.5 0.9 collective-permute-start.17
  107.3 10.6 %collective-permute-done.20.refs_1_ = bf16[2,1024,128]{2,1,0:T(8,128)(2,1)S(1)} collective-permute-done((bf16[2,1024,128]{2,1,0:T(8,128)(2,1)S(1)}, bf16[2,1024,128]{2,1,0:T(8,128)(2,1)S(1)}, u32[]{:S(2)}, u32[]{:S(2)}) %collective-permute-start.20) | collective-permute-done | bytes 524320 | tf_op jit(solution)/shard_map/ppermute | solution.py:715
  117.9 0.2 combine.1
  118.1 1.3 collective-permute-start.21
  119.4 1.7 %collective-permute-start.22 = (bf16[2,256,128]{2,1,0:T(8,128)(2,1)S(1)}, bf16[2,256,128]{2,1,0:T(8,128)(2,1)S(1)}, u32[]{:S(2)}, u32[]{:S(2)}) collective-permute-start(bf16[2,256,128]{2,1,0:T(8,128)(2,1)S(1)} %get-tuple-element.151), channel_id=1, source_target_pairs={{0,4},{2,6},{4,0},{6,2},{1,5},{3,7},{5,1},{7,3},{8,12},{10,14},{12... | collective-permute-start | bytes 393224 | tf_op jit(solution)/shard_map/ppermute | solution.py:705
  121.2 0.5 collective-permute-start.23
  121.7 2.2 %collective-permute-done.21 = bf16[2,256,128]{2,1,0:T(8,128)(2,1)S(1)} collective-permute-done((bf16[2,256,128]{2,1,0:T(8,128)(2,1)S(1)}, bf16[2,256,128]{2,1,0:T(8,128)(2,1)S(1)}, u32[]{:S(2)}, u32[]{:S(2)}) %collective-permute-start.21) | collective-permute-done | bytes 131104 | tf_op jit(solution)/shard_map/ppermute | solution.py:705
  123.9 0.9 collective-permute-done.22
  124.8 2.2 %collective-permute-done.23 = bf16[2,256,128]{2,1,0:T(8,128)(2,1)S(1)} collective-permute-done((bf16[2,256,128]{2,1,0:T(8,128)(2,1)S(1)}, bf16[2,256,128]{2,1,0:T(8,128)(2,1)S(1)}, u32[]{:S(2)}, u32[]{:S(2)}) %collective-permute-start.23) | collective-permute-done | bytes 131104 | tf_op jit(solution)/shard_map/ppermute | solution.py:705
  127.0 1.6 %join_heads.3 = (f32[1024,128]{1,0:T(8,128)}, f32[1024,128]{1,0:T(8,128)}) custom-call(bf16[2,1,256,128]{3,2,1,0:T(8,128)(2,1)S(1)} %bitcast.32, bf16[2,1,256,128]{3,2,1,0:T(8,128)(2,1)S(1)} %bitcast.33, bf16[2,1,256,128]{3,2,1,0:T(8,128)(2,1)S(1)} %bitcast.34, bf16[2,1,256,128]{3,2,1,0:T(8,128)(2,1)S(1)} %bitcast.35), custom_call_target="tpu_custom_call" | custom-call | bytes 1572864 | tf_op jit(solution)/shard_map/join_heads/pallas_call | solution.py:128
  128.6 2.5 %join_heads.2 = f32[4096,128]{1,0:T(8,128)} custom-call(bf16[1,4,256,128]{3,2,1,0:T(8,128)(2,1)S(1)} %bitcast.29, bf16[1,4,256,128]{3,2,1,0:T(8,128)(2,1)S(1)} %collective-permute-done.17.refs_1_, bf16[1,4,256,128]{3,2,1,0:T(8,128)(2,1)S(1)} %collective-permute-done.18.refs_2_, bf16[1,4,256,128]{3,2,1,0:T(8,128)(2,1)S(1)} %collective-permute-done.19.refs_3_), custom_call_target="tpu_custom_call" | custom-call | bytes 3145728 | tf_op jit(solution)/shard_map/join_heads/pallas_call | solution.py:128
  (17 shorter events, 0.1 us)
Async XLA Ops:
  3.5 12.5 %collective-permute-start.3 = (bf16[1040,128]{1,0:T(8,128)(2,1)}, bf16[1040,128]{1,0:T(8,128)(2,1)S(1)}, u32[]{:S(2)}, u32[]{:S(2)}) collective-permute-start(bf16[1040,128]{1,0:T(8,128)(2,1)} %get-tuple-element.79.refs_1_), channel_id=1, source_target_pairs={{0,8},{8,16},{16,24},{1,9},{9,17},{17,25},{2,10},{10,18},{18,26},{... | collective-permute-start | bytes 798728 | tf_op jit(solution)/shard_map/ppermute | solution.py:715
  7.0 15.1 %collective-permute-start.2 = (bf16[1040,128]{1,0:T(8,128)(2,1)}, bf16[1040,128]{1,0:T(8,128)(2,1)S(1)}, u32[]{:S(2)}, u32[]{:S(2)}) collective-permute-start(bf16[1040,128]{1,0:T(8,128)(2,1)} %get-tuple-element.82), channel_id=1, source_target_pairs={{0,6},{2,4},{4,2},{6,0},{1,7},{3,5},{5,3},{7,1},{8,14},{10,12},{12... | collective-permute-start | bytes 798728 | tf_op jit(solution)/shard_map/ppermute | solution.py:705
  9.5 14.2 %collective-permute-start.1 = (bf16[1040,128]{1,0:T(8,128)(2,1)}, bf16[1040,128]{1,0:T(8,128)(2,1)S(1)}, u32[]{:S(2)}, u32[]{:S(2)}) collective-permute-start(bf16[1040,128]{1,0:T(8,128)(2,1)} %get-tuple-element.81), channel_id=1, source_target_pairs={{0,4},{2,6},{4,0},{6,2},{1,5},{3,7},{5,1},{7,3},{8,12},{10,14},{12... | collective-permute-start | bytes 798728 | tf_op jit(solution)/shard_map/ppermute | solution.py:705
  10.1 13.8 %collective-permute-start = (bf16[1040,128]{1,0:T(8,128)(2,1)}, bf16[1040,128]{1,0:T(8,128)(2,1)S(1)}, u32[]{:S(2)}, u32[]{:S(2)}) collective-permute-start(bf16[1040,128]{1,0:T(8,128)(2,1)} %get-tuple-element.80), channel_id=1, source_target_pairs={{0,2},{2,0},{4,6},{6,4},{1,3},{3,1},{5,7},{7,5},{8,10},{10,8},{12,... | collective-permute-start | bytes 798728 | tf_op jit(solution)/shard_map/ppermute | solution.py:705
  11.4 1.2 copy-start
  12.6 1.2 copy-start.1
  16.0 8.9 %collective-permute-start.7 = (bf16[1040,128]{1,0:T(8,128)(2,1)S(1)}, bf16[1040,128]{1,0:T(8,128)(2,1)S(1)}, u32[]{:S(2)}, u32[]{:S(2)}) collective-permute-start(bf16[1040,128]{1,0:T(8,128)(2,1)S(1)} %collective-permute-done.3.refs_0_), channel_id=1, source_target_pairs={{0,8},{8,16},{16,24},{1,9},{9,17},{17,25},{2,10},{10,18},{18,26},{... | collective-permute-start | bytes 798728 | tf_op jit(solution)/shard_map/ppermute | solution.py:715
  20.6 15.3 %collective-permute-start.4 = (bf16[2048,128]{1,0:T(8,128)(2,1)S(1)}, bf16[2048,128]{1,0:T(8,128)(2,1)S(1)}, u32[]{:S(2)}, u32[]{:S(2)}) collective-permute-start(bf16[2048,128]{1,0:T(8,128)(2,1)S(1)} %get-tuple-element.90), channel_id=1, source_target_pairs={{0,2},{2,0},{4,6},{6,4},{1,3},{3,1},{5,7},{7,5},{8,10},{10,8},{12,... | collective-permute-start | bytes 1572872 | tf_op jit(solution)/shard_map/ppermute | solution.py:705
  22.1 25.9 %collective-permute-start.6 = (bf16[2048,128]{1,0:T(8,128)(2,1)S(1)}, bf16[2048,128]{1,0:T(8,128)(2,1)S(1)}, u32[]{:S(2)}, u32[]{:S(2)}) collective-permute-start(bf16[2048,128]{1,0:T(8,128)(2,1)S(1)} %get-tuple-element.98), channel_id=1, source_target_pairs={{0,4},{2,6},{4,0},{6,2},{1,5},{3,7},{5,1},{7,3},{8,12},{10,14},{12... | collective-permute-start | bytes 1572872 | tf_op jit(solution)/shard_map/ppermute | solution.py:705
  24.9 16.0 %collective-permute-start.8 = (bf16[1040,128]{1,0:T(8,128)(2,1)S(1)}, bf16[1040,128]{1,0:T(8,128)(2,1)S(1)}, u32[]{:S(2)}, u32[]{:S(2)}) collective-permute-start(bf16[1040,128]{1,0:T(8,128)(2,1)S(1)} %collective-permute-done.refs_2_), channel_id=1, source_target_pairs={{0,8},{8,16},{16,24},{1,9},{9,17},{17,25},{2,10},{10,18},{18,26},{... | collective-permute-start | bytes 798728 | tf_op jit(solution)/shard_map/ppermute | solution.py:715
  28.6 13.0 %collective-permute-start.9 = (bf16[1040,128]{1,0:T(8,128)(2,1)S(1)}, bf16[1040,128]{1,0:T(8,128)(2,1)S(1)}, u32[]{:S(2)}, u32[]{:S(2)}) collective-permute-start(bf16[1040,128]{1,0:T(8,128)(2,1)S(1)} %collective-permute-done.1.refs_3_), channel_id=1, source_target_pairs={{0,8},{8,16},{16,24},{1,9},{9,17},{17,25},{2,10},{10,18},{18,26},{... | collective-permute-start | bytes 798728 | tf_op jit(solution)/shard_map/ppermute | solution.py:715
  30.8 1.0 copy-start.2
  33.8 10.8 %collective-permute-start.10 = (bf16[1040,128]{1,0:T(8,128)(2,1)S(1)}, bf16[1040,128]{1,0:T(8,128)(2,1)S(1)}, u32[]{:S(2)}, u32[]{:S(2)}) collective-permute-start(bf16[1040,128]{1,0:T(8,128)(2,1)S(1)} %collective-permute-done.2.refs_4_), channel_id=1, source_target_pairs={{0,8},{8,16},{16,24},{1,9},{9,17},{17,25},{2,10},{10,18},{18,26},{... | collective-permute-start | bytes 798728 | tf_op jit(solution)/shard_map/ppermute | solution.py:715
  35.9 15.8 %collective-permute-start.5 = (bf16[2048,128]{1,0:T(8,128)(2,1)S(1)}, bf16[2048,128]{1,0:T(8,128)(2,1)S(1)}, u32[]{:S(2)}, u32[]{:S(2)}) collective-permute-start(bf16[2048,128]{1,0:T(8,128)(2,1)S(1)} %get-tuple-element.91), channel_id=1, source_target_pairs={{0,6},{2,4},{4,2},{6,0},{1,7},{3,5},{5,3},{7,1},{8,14},{10,12},{12... | collective-permute-start | bytes 1572872 | tf_op jit(solution)/shard_map/ppermute | solution.py:705
  44.7 19.1 %collective-permute-start.11 = (bf16[3120,128]{1,0:T(8,128)(2,1)S(1)}, bf16[3120,128]{1,0:T(8,128)(2,1)S(1)}, u32[]{:S(2)}, u32[]{:S(2)}) collective-permute-start(bf16[3120,128]{1,0:T(8,128)(2,1)S(1)} %constant_dynamic-update-slice_fusion.refs_1_), channel_id=1, source_target_pairs={{0,8},{8,16},{16,24},{1,9},{9,17},{17,25},{2,10},{10,18},{18,26},{... | collective-permute-start | bytes 2396168 | tf_op jit(solution)/shard_map/ppermute | solution.py:715
  66.0 1.2 collective-permute-start.12
  67.2 3.9 %collective-permute-start.13 = (f32[8,4,128]{2,1,0:T(4,128)S(1)}, f32[8,4,128]{2,1,0:T(4,128)S(1)}, u32[]{:S(2)}, u32[]{:S(2)}) collective-permute-start(f32[8,4,128]{2,1,0:T(4,128)S(1)} %add.8.refs_7_), channel_id=1, source_target_pairs={{0,2},{2,0},{4,6},{6,4},{1,3},{3,1},{5,7},{7,5},{8,10},{10,8},{12,... | collective-permute-start | bytes 49160 | tf_op jit(solution)/shard_map/ppermute | solution.py:705
  68.7 4.1 %collective-permute-start.14 = (f32[8,4,128]{2,1,0:T(4,128)S(1)}, f32[8,4,128]{2,1,0:T(4,128)S(1)}, u32[]{:S(2)}, u32[]{:S(2)}) collective-permute-start(f32[8,4,128]{2,1,0:T(4,128)S(1)} %add.8.refs_7_), channel_id=1, source_target_pairs={{0,4},{2,6},{4,0},{6,2},{1,5},{3,7},{5,1},{7,3},{8,12},{10,14},{12... | collective-permute-start | bytes 49160 | tf_op jit(solution)/shard_map/ppermute | solution.py:705
  71.1 4.6 %collective-permute-start.15 = (f32[8,4,128]{2,1,0:T(4,128)S(1)}, f32[8,4,128]{2,1,0:T(4,128)S(1)}, u32[]{:S(2)}, u32[]{:S(2)}) collective-permute-start(f32[8,4,128]{2,1,0:T(4,128)S(1)} %add.8.refs_7_), channel_id=1, source_target_pairs={{0,6},{2,4},{4,2},{6,0},{1,7},{3,5},{5,3},{7,1},{8,14},{10,12},{12... | collective-permute-start | bytes 49160 | tf_op jit(solution)/shard_map/ppermute | solution.py:705
  78.1 24.0 %collective-permute-start.16 = (bf16[2,1024,128]{2,1,0:T(8,128)(2,1)S(1)}, bf16[2,1024,128]{2,1,0:T(8,128)(2,1)S(1)}, u32[]{:S(2)}, u32[]{:S(2)}) collective-permute-start(bf16[2,1024,128]{2,1,0:T(8,128)(2,1)S(1)} %get-tuple-element.137), channel_id=1, source_target_pairs={{16,0},{24,8},{17,1},{25,9},{18,2},{26,10},{19,3},{27,11},{20,4},{... | collective-permute-start | bytes 1572872 | tf_op jit(solution)/shard_map/ppermute | solution.py:715
  80.3 37.7 %collective-permute-start.20 = (bf16[2,1024,128]{2,1,0:T(8,128)(2,1)S(1)}, bf16[2,1024,128]{2,1,0:T(8,128)(2,1)S(1)}, u32[]{:S(2)}, u32[]{:S(2)}) collective-permute-start(bf16[2,1024,128]{2,1,0:T(8,128)(2,1)S(1)} %get-tuple-element.148), channel_id=1, source_target_pairs={{8,0},{16,8},{24,16},{9,1},{17,9},{25,17},{10,2},{18,10},{26,18},{... | collective-permute-start | bytes 1572872 | tf_op jit(solution)/shard_map/ppermute | solution.py:715
  84.9 22.4 %collective-permute-start.19 = (bf16[1,4,256,128]{3,2,1,0:T(8,128)(2,1)S(1)}, bf16[1,4,256,128]{3,2,1,0:T(8,128)(2,1)S(1)}, u32[]{:S(2)}, u32[]{:S(2)}) collective-permute-start(bf16[1,4,256,128]{3,2,1,0:T(8,128)(2,1)S(1)} %bitcast.38), channel_id=1, source_target_pairs={{0,6},{2,4},{4,2},{6,0},{1,7},{3,5},{5,3},{7,1},{8,14},{10,12},{12... | collective-permute-start | bytes 786440 | tf_op jit(solution)/shard_map/ppermute | solution.py:705
  106.5 22.2 %collective-permute-start.17 = (bf16[1,4,256,128]{3,2,1,0:T(8,128)(2,1)S(1)}, bf16[1,4,256,128]{3,2,1,0:T(8,128)(2,1)S(1)}, u32[]{:S(2)}, u32[]{:S(2)}) collective-permute-start(bf16[1,4,256,128]{3,2,1,0:T(8,128)(2,1)S(1)} %bitcast.37), channel_id=1, source_target_pairs={{0,2},{2,0},{4,6},{6,4},{1,3},{3,1},{5,7},{7,5},{8,10},{10,8},{12,... | collective-permute-start | bytes 786440 | tf_op jit(solution)/shard_map/ppermute | solution.py:705
  107.3 21.3 %collective-permute-start.18 = (bf16[1,4,256,128]{3,2,1,0:T(8,128)(2,1)S(1)}, bf16[1,4,256,128]{3,2,1,0:T(8,128)(2,1)S(1)}, u32[]{:S(2)}, u32[]{:S(2)}) collective-permute-start(bf16[1,4,256,128]{3,2,1,0:T(8,128)(2,1)S(1)} %bitcast.36), channel_id=1, source_target_pairs={{0,4},{2,6},{4,0},{6,2},{1,5},{3,7},{5,1},{7,3},{8,12},{10,14},{12... | collective-permute-start | bytes 786440 | tf_op jit(solution)/shard_map/ppermute | solution.py:705
  118.1 5.7 %collective-permute-start.21 = (bf16[2,256,128]{2,1,0:T(8,128)(2,1)S(1)}, bf16[2,256,128]{2,1,0:T(8,128)(2,1)S(1)}, u32[]{:S(2)}, u32[]{:S(2)}) collective-permute-start(bf16[2,256,128]{2,1,0:T(8,128)(2,1)S(1)} %get-tuple-element.150), channel_id=1, source_target_pairs={{0,2},{2,0},{4,6},{6,4},{1,3},{3,1},{5,7},{7,5},{8,10},{10,8},{12,... | collective-permute-start | bytes 393224 | tf_op jit(solution)/shard_map/ppermute | solution.py:705
  119.4 5.4 %collective-permute-start.22 = (bf16[2,256,128]{2,1,0:T(8,128)(2,1)S(1)}, bf16[2,256,128]{2,1,0:T(8,128)(2,1)S(1)}, u32[]{:S(2)}, u32[]{:S(2)}) collective-permute-start(bf16[2,256,128]{2,1,0:T(8,128)(2,1)S(1)} %get-tuple-element.151), channel_id=1, source_target_pairs={{0,4},{2,6},{4,0},{6,2},{1,5},{3,7},{5,1},{7,3},{8,12},{10,14},{12... | collective-permute-start | bytes 393224 | tf_op jit(solution)/shard_map/ppermute | solution.py:705
  121.2 5.9 %collective-permute-start.23 = (bf16[2,256,128]{2,1,0:T(8,128)(2,1)S(1)}, bf16[2,256,128]{2,1,0:T(8,128)(2,1)S(1)}, u32[]{:S(2)}, u32[]{:S(2)}) collective-permute-start(bf16[2,256,128]{2,1,0:T(8,128)(2,1)S(1)} %get-tuple-element.152), channel_id=1, source_target_pairs={{0,6},{2,4},{4,2},{6,0},{1,7},{3,5},{5,3},{7,1},{8,14},{10,12},{12... | collective-permute-start | bytes 393224 | tf_op jit(solution)/shard_map/ppermute | solution.py:705
where the time goes:
time: 133 us; the launch traced here: 131 us
  waiting for transfers between devices  51.3 us (39%)
  starting transfers between devices  41.4 us (31%)
  Pallas kernels  31.8 us (24%)
  local copies, waits for them, and re-layouts  4.95 us (4%)
    ppermute x8, waiting for transfers between devices, moved_on(): return lax.ppermute(value, 'span', pairs)  40.2 us
    ppermute x8, starting transfers between devices, moved_on(): return lax.ppermute(value, 'span', pairs)  21.2 us
    ppermute x15, starting transfers between devices, exchanged_with(): lax.ppermute(piece, 'part', [(i, i ^ m) for i in range(parts)])  20 us
    pallas_call x4, Pallas kernels, backward_chunk(): pl.pallas_call(kernel, in_specs=[SMEM, SMEM] + [VMEM] * len(operands), ou...  10.3 us
    ppermute x15, waiting for transfers between devices, exchanged_with(): lax.ppermute(piece, 'part', [(i, i ^ m) for i in range(parts)])  10 us
    pallas_call x3, Pallas kernels, forward_own(): pl.pallas_call(kernel, in_specs=[SMEM, SMEM] + [VMEM] * len(operands), ou...  8.92 us
    pallas_call x2, Pallas kernels, split_heads(): pl.pallas_call(kernel, in_specs=[SMEM] * len(scalars) + [pl.BlockSpec(mem...  5.09 us
    pallas_call x2, Pallas kernels, join_heads(): pl.pallas_call(kernel, grid=(steps,), in_specs=[pl.BlockSpec((count, per_...  4.08 us
  transfers between devices with their start and end apart: 24, of which 12 were waited for; matrix products, arithmetic and copies ran while one was open for 2% of the time, Pallas kernels for 17%

commit v1 on v0

--- a/solution.py
+++ b/solution.py
@@ -636,8 +636,7 @@
 
         each_block(len(order) * per, query_block)
         if not closing:
-            dkv_out[0] = (dkv_s[0] * sh.scale).astype(BF16)
-            dkv_out[1] = dkv_s[1].astype(BF16)
+            dkv_out[...] = dkv_s[...].astype(BF16)
 
     def array(*shape, dtype=F32):
         return jax.ShapeDtypeStruct(shape, dtype)
@@ -678,27 +677,42 @@
     )(me, back, *operands)
 
 
+def add_arrived(held, arrived):
+    def kernel(held_ref, *refs):
+        total = held_ref[...]
+        for ref in refs[:-1]:
+            total += ref[...].astype(F32)
+        refs[-1][...] = total
+
+    return pl.pallas_call(
+        kernel,
+        in_specs=[VMEM] * (1 + len(arrived)),
+        out_specs=VMEM,
+        out_shape=jax.ShapeDtypeStruct(held.shape, F32),
+        input_output_aliases={0: 0},
+        compiler_params=params(),
+        cost_estimate=cost(0, 10 * held.size),
+        name="add_arrived",
+    )(held, *arrived)
+
+
 def combine(sh, me, arrived, held):
-    count = len(arrived)
-
-    def kernel(me_ref, held_ref, *refs):
-        for m, out in enumerate(refs[count:]):
+    def kernel(me_ref, held_ref, arrived_ref, *outs):
+        for m, out in enumerate(outs):
             slot = pl.ds(slot_of(me_ref, m, sh.rows), sh.rows)
             for a, factor in ((0, sh.scale), (1, 1.0)):
-                part = held_ref[a, slot, :] * factor
-                for ref in refs[:count]:
-                    part += ref[a, slot, :].astype(F32)
-                out[a] = part.astype(BF16)
+                total = held_ref[a, slot, :] + arrived_ref[a, slot, :].astype(F32)
+                out[a] = (total * factor).astype(BF16)
 
     return pl.pallas_call(
         kernel,
-        in_specs=[SMEM] + [VMEM] * (1 + count),
+        in_specs=[SMEM, VMEM, VMEM],
         out_specs=[VMEM] * sh.parts,
         out_shape=[jax.ShapeDtypeStruct((2, sh.rows, sh.width), BF16)] * sh.parts,
         compiler_params=params(),
         cost_estimate=cost(0, 1),
         name="combine",
-    )(me, held, *arrived)
+    )(me, held, arrived)
 
 
 def exchanged_with(piece, parts, m):
@@ -809,8 +823,6 @@
     turns = [turn[::-1] for turn in (everyone[-1:], everyone[:-1]) if turn]
     held, dq_pieces = None, [None] * parts
     for order in turns:
-        if held is not None:
-            arrived[0], held = lax.optimization_barrier((arrived[0], held))
         held, *done = backward_chunk(
             sh, me, back, qq, spans[0], 0, grads, lse, dots, dq, None, order, held
         )
@@ -818,7 +830,9 @@
             dq_pieces[m] = piece.reshape(1, group, rows, width)
     dq_pieces = exchanged(dq_pieces, parts)
     dq_pieces[-1], held = lax.optimization_barrier((dq_pieces[-1], held))
-    dkv_pieces = exchanged(combine(sh, me, arrived, held), parts)
+    if arrived[1:]:
+        held = add_arrived(held, arrived[:-1])
+    dkv_pieces = exchanged(combine(sh, me, arrived[-1], held), parts)
     (product_queries,) = join_heads(dq_pieces, 1, group)
     dkv_pieces = [p.reshape(2, 1, rows, width) for p in dkv_pieces]
     product_keys, product_values = join_heads(dkv_pieces, 2, 1)

time: 133 us -> 131 us (0.985)
  the two profiles are of different devices: /device:TPU:8 before, /device:TPU:20 now
where the time goes in v1:
time: 131 us; the launch traced here: 130 us
  Pallas kernels  66 us (50%)
  starting transfers between devices  34.2 us (26%)
  waiting for transfers between devices  23 us (18%)
  local copies, waits for them, and re-layouts  4.95 us (4%)
    pallas_call x4, Pallas kernels, backward_chunk(): pl.pallas_call(kernel, in_specs=[SMEM, SMEM] + [VMEM] * len(operands), ou...  25 us
    pallas_call x2, Pallas kernels, forward_chunk(): pl.pallas_call(kernel, in_specs=[SMEM, SMEM] + [VMEM] * len(operands), ou...  20.4 us
    ppermute x8, starting transfers between devices, moved_on(): return lax.ppermute(value, 'span', pairs)  17.3 us
    ppermute x15, starting transfers between devices, exchanged_with(): lax.ppermute(piece, 'part', [(i, i ^ m) for i in range(parts)])  16.8 us
    pallas_call x3, Pallas kernels, forward_own(): pl.pallas_call(kernel, in_specs=[SMEM, SMEM] + [VMEM] * len(operands), ou...  11.1 us
    ppermute x15, waiting for transfers between devices, exchanged_with(): lax.ppermute(piece, 'part', [(i, i ^ m) for i in range(parts)])  11.1 us
    ppermute x8, waiting for transfers between devices, moved_on(): return lax.ppermute(value, 'span', pairs)  10.8 us
    pallas_call x2, Pallas kernels, split_heads(): pl.pallas_call(kernel, in_specs=[SMEM] * len(scalars) + [pl.BlockSpec(mem...  5.09 us
  transfers between devices with their start and end apart: 24, of which 10 were waited for; matrix products, arithmetic and copies ran while one was open for 2% of the time, Pallas kernels for 38%

profile of v1, /device:TPU:20, one launch (start us, length us, event | category | flops | bytes accessed | tf_op | source)
XLA Modules:
  0.0 129.9 jit_solution(8062079580404356509)
XLA Ops:
  0.6 2.9 %split_heads.2 = (bf16[1040,128]{1,0:T(8,128)(2,1)}, bf16[1040,128]{1,0:T(8,128)(2,1)}, bf16[1040,128]{1,0:T(8,128)(2,1)}, bf16[1040,128]{1,0:T(8,128)(2,1)}) custom-call(s32[2]{0:T(128)} %refs_0_.1, bf16[1024,128]{1,0:T(8,128)(2,1)} %bitcast.41, bf16[1024,128]{1,0:T(8,128)(2,1)} %bitcast.42, bf16[1024,128]{1,0:T(8,128)(2,1)} %bitcast.43, ...), custom_call_target="tpu_custom_call" | custom-call | bytes 2097152 | tf_op jit(solution)/shard_map/split_heads/pallas_call | solution.py:99
  3.5 3.5 %collective-permute-start.3 = (bf16[1040,128]{1,0:T(8,128)(2,1)}, bf16[1040,128]{1,0:T(8,128)(2,1)S(1)}, u32[]{:S(2)}, u32[]{:S(2)}) collective-permute-start(bf16[1040,128]{1,0:T(8,128)(2,1)} %get-tuple-element.77.refs_1_), channel_id=1, source_target_pairs={{0,8},{8,16},{16,24},{1,9},{9,17},{17,25},{2,10},{10,18},{18,26},{... | collective-permute-start | bytes 798728 | tf_op jit(solution)/shard_map/ppermute | solution.py:729
  7.0 1.5 %collective-permute-start.2 = (bf16[1040,128]{1,0:T(8,128)(2,1)}, bf16[1040,128]{1,0:T(8,128)(2,1)S(1)}, u32[]{:S(2)}, u32[]{:S(2)}) collective-permute-start(bf16[1040,128]{1,0:T(8,128)(2,1)} %get-tuple-element.80), channel_id=1, source_target_pairs={{0,6},{2,4},{4,2},{6,0},{1,7},{3,5},{5,3},{7,1},{8,14},{10,12},{12... | collective-permute-start | bytes 798728 | tf_op jit(solution)/shard_map/ppermute | solution.py:719
  8.5 1.5 %collective-permute-start.1 = (bf16[1040,128]{1,0:T(8,128)(2,1)}, bf16[1040,128]{1,0:T(8,128)(2,1)S(1)}, u32[]{:S(2)}, u32[]{:S(2)}) collective-permute-start(bf16[1040,128]{1,0:T(8,128)(2,1)} %get-tuple-element.79), channel_id=1, source_target_pairs={{0,4},{2,6},{4,0},{6,2},{1,5},{3,7},{5,1},{7,3},{8,12},{10,14},{12... | collective-permute-start | bytes 798728 | tf_op jit(solution)/shard_map/ppermute | solution.py:719
  10.1 0.5 collective-permute-start
  10.6 0.8 slice_reduce_fusion.3
  11.4 1.2 copy-done
  12.6 1.2 copy-done.1
  13.8 2.2 %split_heads.3 = (bf16[2048,128]{1,0:T(8,128)(2,1)S(1)}, bf16[2048,128]{1,0:T(8,128)(2,1)S(1)}, bf16[2048,128]{1,0:T(8,128)(2,1)S(1)}, bf16[2048,128]{1,0:T(8,128)(2,1)S(1)}) custom-call(bf16[4096,128]{1,0:T(8,128)(2,1)S(1)} %bitcast.27, bf16[4096,128]{1,0:T(8,128)(2,1)S(1)} %bitcast.28), custom_call_target="tpu_custom_call" | custom-call | bytes 4194304 | tf_op jit(solution)/shard_map/split_heads/pallas_call | solution.py:99
  16.0 0.0 collective-permute-done.3.refs_0_
  16.0 1.9 %collective-permute-start.7 = (bf16[1040,128]{1,0:T(8,128)(2,1)S(1)}, bf16[1040,128]{1,0:T(8,128)(2,1)S(1)}, u32[]{:S(2)}, u32[]{:S(2)}) collective-permute-start(bf16[1040,128]{1,0:T(8,128)(2,1)S(1)} %collective-permute-done.3.refs_0_), channel_id=1, source_target_pairs={{0,8},{8,16},{16,24},{1,9},{9,17},{17,25},{2,10},{10,18},{18,26},{... | collective-permute-start | bytes 798728 | tf_op jit(solution)/shard_map/ppermute | solution.py:729
  18.0 0.7 multiply_bitcast_fusion
  18.7 0.1 copy.28
  18.8 0.2 broadcast_in_dim.3
  19.0 1.6 %collective-permute-start.4 = (bf16[2048,128]{1,0:T(8,128)(2,1)S(1)}, bf16[2048,128]{1,0:T(8,128)(2,1)S(1)}, u32[]{:S(2)}, u32[]{:S(2)}) collective-permute-start(bf16[2048,128]{1,0:T(8,128)(2,1)S(1)} %get-tuple-element.88), channel_id=1, source_target_pairs={{0,2},{2,0},{4,6},{6,4},{1,3},{3,1},{5,7},{7,5},{8,10},{10,8},{12,... | collective-permute-start | bytes 1572872 | tf_op jit(solution)/shard_map/ppermute | solution.py:719
  20.6 0.0 collective-permute-done.2.refs_4_
  20.6 0.5 collective-permute-start.6
  21.1 0.1 slice_reduce_fusion
  21.2 0.7 collective-permute-done.1.refs_3_
  21.9 0.1 slice_reduce_fusion.1
  22.0 0.0 collective-permute-done.refs_2_
  22.0 3.0 %collective-permute-done.7.refs_0_ = bf16[1040,128]{1,0:T(8,128)(2,1)S(1)} collective-permute-done((bf16[1040,128]{1,0:T(8,128)(2,1)S(1)}, bf16[1040,128]{1,0:T(8,128)(2,1)S(1)}, u32[]{:S(2)}, u32[]{:S(2)}) %collective-permute-start.7) | collective-permute-done | bytes 266272 | tf_op jit(solution)/shard_map/ppermute | solution.py:729
  25.0 2.2 %collective-permute-start.8 = (bf16[1040,128]{1,0:T(8,128)(2,1)S(1)}, bf16[1040,128]{1,0:T(8,128)(2,1)S(1)}, u32[]{:S(2)}, u32[]{:S(2)}) collective-permute-start(bf16[1040,128]{1,0:T(8,128)(2,1)S(1)} %collective-permute-done.refs_2_), channel_id=1, source_target_pairs={{0,8},{8,16},{16,24},{1,9},{9,17},{17,25},{2,10},{10,18},{18,26},{... | collective-permute-start | bytes 798728 | tf_op jit(solution)/shard_map/ppermute | solution.py:729
  27.1 0.1 slice_reduce_fusion.2
  27.3 0.1 maximum_convert_fusion.back_ref
  27.3 1.9 %collective-permute-start.9 = (bf16[1040,128]{1,0:T(8,128)(2,1)S(1)}, bf16[1040,128]{1,0:T(8,128)(2,1)S(1)}, u32[]{:S(2)}, u32[]{:S(2)}) collective-permute-start(bf16[1040,128]{1,0:T(8,128)(2,1)S(1)} %collective-permute-done.1.refs_3_), channel_id=1, source_target_pairs={{0,8},{8,16},{16,24},{1,9},{9,17},{17,25},{2,10},{10,18},{18,26},{... | collective-permute-start | bytes 798728 | tf_op jit(solution)/shard_map/ppermute | solution.py:729
  29.3 0.0 copy-start.2
  29.3 0.9 copy-done.2
  30.2 4.1 %forward_own.3 = (f32[8,256,512]{2,1,0:T(8,128)S(1)}, f32[8,8,512]{2,1,0:T(8,128)S(1)}, bf16[8,512,256]{2,1,0:T(8,128)(2,1)S(1)}, bf16[8,1024,512]{2,1,0:T(8,128...) custom-call(s32[1]{0:T(128)} %bitcast.me_ref, ...), custom_call_target="tpu_custom_call" | custom-call | flops 805306368 | bytes 2097152 | tf_op jit(solution)/shard_map/forward_own/pallas_call | solution.py:422
  34.3 1.9 %collective-permute-start.10 = (bf16[1040,128]{1,0:T(8,128)(2,1)S(1)}, bf16[1040,128]{1,0:T(8,128)(2,1)S(1)}, u32[]{:S(2)}, u32[]{:S(2)}) collective-permute-start(bf16[1040,128]{1,0:T(8,128)(2,1)S(1)} %collective-permute-done.2.refs_4_), channel_id=1, source_target_pairs={{0,8},{8,16},{16,24},{1,9},{9,17},{17,25},{2,10},{10,18},{18,26},{... | collective-permute-start | bytes 798728 | tf_op jit(solution)/shard_map/ppermute | solution.py:729
  36.2 0.0 collective-permute-done.4.refs_0_
  36.2 0.3 collective-permute-start.5
  36.5 4.1 %collective-permute-done.9 = bf16[1040,128]{1,0:T(8,128)(2,1)S(1)} collective-permute-done((bf16[1040,128]{1,0:T(8,128)(2,1)S(1)}, bf16[1040,128]{1,0:T(8,128)(2,1)S(1)}, u32[]{:S(2)}, u32[]{:S(2)}) %collective-permute-start.9) | collective-permute-done | bytes 266272 | tf_op jit(solution)/shard_map/ppermute | solution.py:729
  40.6 3.7 %collective-permute-done.10 = bf16[1040,128]{1,0:T(8,128)(2,1)S(1)} collective-permute-done((bf16[1040,128]{1,0:T(8,128)(2,1)S(1)}, bf16[1040,128]{1,0:T(8,128)(2,1)S(1)}, u32[]{:S(2)}, u32[]{:S(2)}) %collective-permute-start.10) | collective-permute-done | bytes 266272 | tf_op jit(solution)/shard_map/ppermute | solution.py:729
  44.4 2.7 %collective-permute-start.11 = (bf16[3120,128]{1,0:T(8,128)(2,1)S(1)}, bf16[3120,128]{1,0:T(8,128)(2,1)S(1)}, u32[]{:S(2)}, u32[]{:S(2)}) collective-permute-start(bf16[3120,128]{1,0:T(8,128)(2,1)S(1)} %constant_dynamic-update-slice_fusion.refs_1_), channel_id=1, source_target_pairs={{0,8},{8,16},{16,24},{1,9},{9,17},{17,25},{2,10},{10,18},{18,26},{... | collective-permute-start | bytes 2396168 | tf_op jit(solution)/shard_map/ppermute | solution.py:729
  47.1 4.5 %forward_own.4 = (f32[8,256,512]{2,1,0:T(8,128)S(1)}, f32[8,8,512]{2,1,0:T(8,128)S(1)}, bf16[8,512,256]{2,1,0:T(8,128)(2,1)S(1)}, bf16[8,1024,512]{2,1,0:T(8,128)(2,1)S(1)}, f32[8,8,1,512]{3,2,1,0:T(1,128)S(1)}) custom-call(s32[1]{0:T(128)} %bitcast.me_ref, ...), custom_call_target="tpu_custom_call", output_to_operand_aliasing={{0}: (9, {}), {1}: (10, {}), {2}: (11, {}), {3}: (12, {}), ... | custom-call | flops 1610612736 | bytes 2097152 | tf_op jit(solution)/shard_map/forward_own/pallas_call | solution.py:422
  51.6 2.6 %forward_own.5 = (f32[8,256,512]{2,1,0:T(8,128)S(1)}, f32[8,8,512]{2,1,0:T(8,128)S(1)}, bf16[8,512,256]{2,1,0:T(8,128)(2,1)S(1)}, bf16[8,1024,512]{2,1,0:T(8,128)(2,1)S(1)}, f32[8,8,1,512]{3,2,1,0:T(1,128)S(1)}) custom-call(s32[1]{0:T(128)} %bitcast.me_ref, ...), custom_call_target="tpu_custom_call", output_to_operand_aliasing={{0}: (8, {}), {1}: (9, {}), {2}: (10, {}), {3}: (11, {}), {... | custom-call | flops 805306368 | bytes 2097152 | tf_op jit(solution)/shard_map/forward_own/pallas_call | solution.py:422
  54.2 14.4 %forward_chunk.1 = (bf16[1024,128]{1,0:T(8,128)(2,1)S(1)}, bf16[1024,128]{1,0:T(8,128)(2,1)S(1)}, bf16[128,1024]{1,0:T(8,128)(2,1)S(1)}, f32[8,256,512]{2,1,0:T(...) custom-call(s32[1]{0:T(128)} %bitcast.me_ref, ...), custom_call_target="tpu_custom_call", output_to_operand_aliasing={{3}: (5, {}), {4}: (6, {})} | custom-call | flops 6442450944 | bytes 12582912 | tf_op jit(solution)/shard_map/forward_chunk/pallas_call | solution.py:510
  68.6 6.1 %forward_far.1 = (bf16[1024,128]{1,0:T(8,128)(2,1)S(1)}, bf16[1024,128]{1,0:T(8,128)(2,1)S(1)}, bf16[128,1024]{1,0:T(8,128)(2,1)S(1)}, f32[8,256,512]{2,1,0:T(8,...) custom-call(s32[1]{0:T(128)} %bitcast.me_ref, ...), custom_call_target="tpu_custom_call", output_to_operand_aliasing={{3}: (5, {}), {4}: (6, {})} | custom-call | flops 6442450944 | bytes 12582912 | tf_op jit(solution)/shard_map/forward_far/pallas_call | solution.py:510
  74.6 0.1 collective-permute-start.12
  74.7 1.2 collective-permute-done.12
  75.9 2.3 %collective-permute-start.13 = (f32[8,4,128]{2,1,0:T(4,128)S(1)}, f32[8,4,128]{2,1,0:T(4,128)S(1)}, u32[]{:S(2)}, u32[]{:S(2)}) collective-permute-start(f32[8,4,128]{2,1,0:T(4,128)S(1)} %add.8.refs_7_), channel_id=1, source_target_pairs={{0,2},{2,0},{4,6},{6,4},{1,3},{3,1},{5,7},{7,5},{8,10},{10,8},{12,... | collective-permute-start | bytes 49160 | tf_op jit(solution)/shard_map/ppermute | solution.py:719
  78.2 1.0 collective-permute-start.14
  79.2 0.7 collective-permute-start.15
  79.8 0.1 collective-permute-done.13.refs_8_
  79.9 2.0 %collective-permute-done.14.refs_9_ = f32[8,4,128]{2,1,0:T(4,128)S(1)} collective-permute-done((f32[8,4,128]{2,1,0:T(4,128)S(1)}, f32[8,4,128]{2,1,0:T(4,128)S(1)}, u32[]{:S(2)}, u32[]{:S(2)}) %collective-permute-start.14) | collective-permute-done | bytes 16416 | tf_op jit(solution)/shard_map/ppermute | solution.py:719
  81.9 1.9 %collective-permute-done.15.refs_10_ = f32[8,4,128]{2,1,0:T(4,128)S(1)} collective-permute-done((f32[8,4,128]{2,1,0:T(4,128)S(1)}, f32[8,4,128]{2,1,0:T(4,128)S(1)}, u32[]{:S(2)}, u32[]{:S(2)}) %collective-permute-start.15) | collective-permute-done | bytes 16416 | tf_op jit(solution)/shard_map/ppermute | solution.py:719
  83.8 5.8 %backward_chunk.4 = (bf16[2,1024,128]{2,1,0:T(8,128)(2,1)S(1)}, f32[8,128,512]{2,1,0:T(8,128)S(1)}, bf16[8,512,128]{2,1,0:T(8,128)(2,1)S(1)}, f32[8,1,512]{2,1,0:T(1,128)S(1)}) custom-call(s32[1]{0:T(128)} %bitcast.me_ref, s32[8]{0:T(128)S(1)} %maximum_convert_fusion.back_ref, bf16[8,512,256]{2,1,0:T(8,128)(2,1)S(1)} %get-tuple-element.107.qq_s.refs_0_, ...), custom_call_target="tpu_custom_call" | custom-call | flops 5368709120 | bytes 33554432 | tf_op jit(solution)/shard_map/backward_chunk/pallas_call | solution.py:666
  89.6 1.3 %collective-permute-start.19 = (bf16[2,1024,128]{2,1,0:T(8,128)(2,1)S(1)}, bf16[2,1024,128]{2,1,0:T(8,128)(2,1)S(1)}, u32[]{:S(2)}, u32[]{:S(2)}) collective-permute-start(bf16[2,1024,128]{2,1,0:T(8,128)(2,1)S(1)} %get-tuple-element.143), channel_id=1, source_target_pairs={{16,0},{24,8},{17,1},{25,9},{18,2},{26,10},{19,3},{27,11},{20,4},{... | collective-permute-start | bytes 1572872 | tf_op jit(solution)/shard_map/ppermute | solution.py:729
  91.0 10.6 %backward_chunk.5 = (bf16[2,1024,128]{2,1,0:T(8,128)(2,1)S(1)}, f32[8,128,512]{2,1,0:T(8,128)S(1)}) custom-call(s32[1]{0:T(128)} %bitcast.me_ref, s32[8]{0:T(128)S(1)} %maximum_convert_fusion.back_ref, bf16[8,512,256]{2,1,0:T(8,128)(2,1)S(1)} %get-tuple-element.107.qq_s.refs_0_, ...), custom_call_target="tpu_custom_call", output_to_operand_aliasing={{1}: (11, {})} | custom-call | flops 5368709120 | bytes 33554432 | tf_op jit(solution)/shard_map/backward_chunk/pallas_call | solution.py:666
  101.5 1.9 %collective-permute-start.20 = (bf16[2,1024,128]{2,1,0:T(8,128)(2,1)S(1)}, bf16[2,1024,128]{2,1,0:T(8,128)(2,1)S(1)}, u32[]{:S(2)}, u32[]{:S(2)}) collective-permute-start(bf16[2,1024,128]{2,1,0:T(8,128)(2,1)S(1)} %get-tuple-element.144), channel_id=1, source_target_pairs={{8,0},{16,8},{24,16},{9,1},{17,9},{25,17},{10,2},{18,10},{26,18},{... | collective-permute-start | bytes 1572872 | tf_op jit(solution)/shard_map/ppermute | solution.py:729
  103.5 2.2 %backward_chunk.6 = (f32[2,1024,128]{2,1,0:T(8,128)S(1)}, bf16[4,256,128]{2,1,0:T(8,128)(2,1)S(1)}) custom-call(s32[1]{0:T(128)} %bitcast.me_ref, s32[8]{0:T(128)S(1)} %maximum_convert_fusion.back_ref, bf16[8,512,256]{2,1,0:T(8,128)(2,1)S(1)} %get-tuple-element.107.qq_s.refs_0_, bf16[1024,128]{1,0:T(8,128)(2,1)S(1)} %get-tuple-element.91.refs_2_.refs_1_, ...), custom_call_target="tpu_custom_call" | custom-call | flops 1 | bytes 1 | tf_op jit(solution)/shard_map/backward_chunk/pallas_call | solution.py:666
  105.7 1.7 %collective-permute-start.18 = (bf16[1,4,256,128]{3,2,1,0:T(8,128)(2,1)S(1)}, bf16[1,4,256,128]{3,2,1,0:T(8,128)(2,1)S(1)}, u32[]{:S(2)}, u32[]{:S(2)}) collective-permute-start(bf16[1,4,256,128]{3,2,1,0:T(8,128)(2,1)S(1)} %bitcast.38), channel_id=1, source_target_pairs={{0,6},{2,4},{4,2},{6,0},{1,7},{3,5},{5,3},{7,1},{8,14},{10,12},{12... | collective-permute-start | bytes 786440 | tf_op jit(solution)/shard_map/ppermute | solution.py:719
  107.4 6.4 %backward_chunk.7 = (f32[2,1024,128]{2,1,0:T(8,128)S(1)}, bf16[4,256,128]{2,1,0:T(8,128)(2,1)S(1)}, bf16[4,256,128]{2,1,0:T(8,128)(2,1)S(1)}, bf16[4,256,128]{2,1,0:T(8,128)(2,1)S(1)}) custom-call(s32[1]{0:T(128)} %bitcast.me_ref, s32[8]{0:T(128)S(1)} %maximum_convert_fusion.back_ref, ...), custom_call_target="tpu_custom_call", output_to_operand_aliasing={{0}: (12, {})} | custom-call | flops 1 | bytes 1 | tf_op jit(solution)/shard_map/backward_chunk/pallas_call | solution.py:666
  113.7 1.8 %collective-permute-start.16 = (bf16[1,4,256,128]{3,2,1,0:T(8,128)(2,1)S(1)}, bf16[1,4,256,128]{3,2,1,0:T(8,128)(2,1)S(1)}, u32[]{:S(2)}, u32[]{:S(2)}) collective-permute-start(bf16[1,4,256,128]{3,2,1,0:T(8,128)(2,1)S(1)} %bitcast.37), channel_id=1, source_target_pairs={{0,2},{2,0},{4,6},{6,4},{1,3},{3,1},{5,7},{7,5},{8,10},{10,8},{12,... | collective-permute-start | bytes 786440 | tf_op jit(solution)/shard_map/ppermute | solution.py:719
  115.5 0.2 add_arrived.1.held_ref
  115.7 0.1 combine.1
  115.8 1.3 collective-permute-start.21
  117.1 1.2 collective-permute-start.22
  118.3 1.1 collective-permute-start.23
  119.4 3.6 %collective-permute-done.16.refs_1_ = bf16[1,4,256,128]{3,2,1,0:T(8,128)(2,1)S(1)} collective-permute-done((bf16[1,4,256,128]{3,2,1,0:T(8,128)(2,1)S(1)}, bf16[1,4,256,128]{3,2,1,0:T(8,128)(2,1)S(1)}, u32[]{:S(2)}, u32[]{:S(2)}) %collective-permute-start.16) | collective-permute-done | bytes 262176 | tf_op jit(solution)/shard_map/ppermute | solution.py:719
  123.1 2.8 %collective-permute-done.17.refs_2_ = bf16[1,4,256,128]{3,2,1,0:T(8,128)(2,1)S(1)} collective-permute-done((bf16[1,4,256,128]{3,2,1,0:T(8,128)(2,1)S(1)}, bf16[1,4,256,128]{3,2,1,0:T(8,128)(2,1)S(1)}, u32[]{:S(2)}, u32[]{:S(2)}) %collective-permute-start.17) | collective-permute-done | bytes 262176 | tf_op jit(solution)/shard_map/ppermute | solution.py:719
  125.8 2.5 %join_heads.2 = f32[4096,128]{1,0:T(8,128)} custom-call(bf16[1,4,256,128]{3,2,1,0:T(8,128)(2,1)S(1)} %bitcast.29, bf16[1,4,256,128]{3,2,1,0:T(8,128)(2,1)S(1)} %collective-permute-done.16.refs_1_, bf16[1,4,256,128]{3,2,1,0:T(8,128)(2,1)S(1)} %collective-permute-done.17.refs_2_, bf16[1,4,256,128]{3,2,1,0:T(8,128)(2,1)S(1)} %collective-permute-done.18.refs_3_), custom_call_target="tpu_custom_call" | custom-call | bytes 3145728 | tf_op jit(solution)/shard_map/join_heads/pallas_call | solution.py:128
  128.3 1.6 %join_heads.3 = (f32[1024,128]{1,0:T(8,128)}, f32[1024,128]{1,0:T(8,128)}) custom-call(bf16[2,1,256,128]{3,2,1,0:T(8,128)(2,1)S(1)} %bitcast.32, bf16[2,1,256,128]{3,2,1,0:T(8,128)(2,1)S(1)} %bitcast.33, bf16[2,1,256,128]{3,2,1,0:T(8,128)(2,1)S(1)} %bitcast.34, bf16[2,1,256,128]{3,2,1,0:T(8,128)(2,1)S(1)} %bitcast.35), custom_call_target="tpu_custom_call" | custom-call | bytes 1572864 | tf_op jit(solution)/shard_map/join_heads/pallas_call | solution.py:128
  (18 shorter events, 0.1 us)
Async XLA Ops:
  3.5 12.5 %collective-permute-start.3 = (bf16[1040,128]{1,0:T(8,128)(2,1)}, bf16[1040,128]{1,0:T(8,128)(2,1)S(1)}, u32[]{:S(2)}, u32[]{:S(2)}) collective-permute-start(bf16[1040,128]{1,0:T(8,128)(2,1)} %get-tuple-element.77.refs_1_), channel_id=1, source_target_pairs={{0,8},{8,16},{16,24},{1,9},{9,17},{17,25},{2,10},{10,18},{18,26},{... | collective-permute-start | bytes 798728 | tf_op jit(solution)/shard_map/ppermute | solution.py:729
  7.0 13.5 %collective-permute-start.2 = (bf16[1040,128]{1,0:T(8,128)(2,1)}, bf16[1040,128]{1,0:T(8,128)(2,1)S(1)}, u32[]{:S(2)}, u32[]{:S(2)}) collective-permute-start(bf16[1040,128]{1,0:T(8,128)(2,1)} %get-tuple-element.80), channel_id=1, source_target_pairs={{0,6},{2,4},{4,2},{6,0},{1,7},{3,5},{5,3},{7,1},{8,14},{10,12},{12... | collective-permute-start | bytes 798728 | tf_op jit(solution)/shard_map/ppermute | solution.py:719
  8.5 13.3 %collective-permute-start.1 = (bf16[1040,128]{1,0:T(8,128)(2,1)}, bf16[1040,128]{1,0:T(8,128)(2,1)S(1)}, u32[]{:S(2)}, u32[]{:S(2)}) collective-permute-start(bf16[1040,128]{1,0:T(8,128)(2,1)} %get-tuple-element.79), channel_id=1, source_target_pairs={{0,4},{2,6},{4,0},{6,2},{1,5},{3,7},{5,1},{7,3},{8,12},{10,14},{12... | collective-permute-start | bytes 798728 | tf_op jit(solution)/shard_map/ppermute | solution.py:719
  10.1 11.9 %collective-permute-start = (bf16[1040,128]{1,0:T(8,128)(2,1)}, bf16[1040,128]{1,0:T(8,128)(2,1)S(1)}, u32[]{:S(2)}, u32[]{:S(2)}) collective-permute-start(bf16[1040,128]{1,0:T(8,128)(2,1)} %get-tuple-element.78), channel_id=1, source_target_pairs={{0,2},{2,0},{4,6},{6,4},{1,3},{3,1},{5,7},{7,5},{8,10},{10,8},{12,... | collective-permute-start | bytes 798728 | tf_op jit(solution)/shard_map/ppermute | solution.py:719
  11.4 1.2 copy-start
  12.6 1.2 copy-start.1
  16.0 8.9 %collective-permute-start.7 = (bf16[1040,128]{1,0:T(8,128)(2,1)S(1)}, bf16[1040,128]{1,0:T(8,128)(2,1)S(1)}, u32[]{:S(2)}, u32[]{:S(2)}) collective-permute-start(bf16[1040,128]{1,0:T(8,128)(2,1)S(1)} %collective-permute-done.3.refs_0_), channel_id=1, source_target_pairs={{0,8},{8,16},{16,24},{1,9},{9,17},{17,25},{2,10},{10,18},{18,26},{... | collective-permute-start | bytes 798728 | tf_op jit(solution)/shard_map/ppermute | solution.py:729
  19.0 17.2 %collective-permute-start.4 = (bf16[2048,128]{1,0:T(8,128)(2,1)S(1)}, bf16[2048,128]{1,0:T(8,128)(2,1)S(1)}, u32[]{:S(2)}, u32[]{:S(2)}) collective-permute-start(bf16[2048,128]{1,0:T(8,128)(2,1)S(1)} %get-tuple-element.88), channel_id=1, source_target_pairs={{0,2},{2,0},{4,6},{6,4},{1,3},{3,1},{5,7},{7,5},{8,10},{10,8},{12,... | collective-permute-start | bytes 1572872 | tf_op jit(solution)/shard_map/ppermute | solution.py:719
  20.6 26.5 %collective-permute-start.6 = (bf16[2048,128]{1,0:T(8,128)(2,1)S(1)}, bf16[2048,128]{1,0:T(8,128)(2,1)S(1)}, u32[]{:S(2)}, u32[]{:S(2)}) collective-permute-start(bf16[2048,128]{1,0:T(8,128)(2,1)S(1)} %get-tuple-element.96), channel_id=1, source_target_pairs={{0,4},{2,6},{4,0},{6,2},{1,5},{3,7},{5,1},{7,3},{8,12},{10,14},{12... | collective-permute-start | bytes 1572872 | tf_op jit(solution)/shard_map/ppermute | solution.py:719
  25.0 11.5 %collective-permute-start.8 = (bf16[1040,128]{1,0:T(8,128)(2,1)S(1)}, bf16[1040,128]{1,0:T(8,128)(2,1)S(1)}, u32[]{:S(2)}, u32[]{:S(2)}) collective-permute-start(bf16[1040,128]{1,0:T(8,128)(2,1)S(1)} %collective-permute-done.refs_2_), channel_id=1, source_target_pairs={{0,8},{8,16},{16,24},{1,9},{9,17},{17,25},{2,10},{10,18},{18,26},{... | collective-permute-start | bytes 798728 | tf_op jit(solution)/shard_map/ppermute | solution.py:729
  27.3 13.2 %collective-permute-start.9 = (bf16[1040,128]{1,0:T(8,128)(2,1)S(1)}, bf16[1040,128]{1,0:T(8,128)(2,1)S(1)}, u32[]{:S(2)}, u32[]{:S(2)}) collective-permute-start(bf16[1040,128]{1,0:T(8,128)(2,1)S(1)} %collective-permute-done.1.refs_3_), channel_id=1, source_target_pairs={{0,8},{8,16},{16,24},{1,9},{9,17},{17,25},{2,10},{10,18},{18,26},{... | collective-permute-start | bytes 798728 | tf_op jit(solution)/shard_map/ppermute | solution.py:729
  29.3 1.0 copy-start.2
  34.3 10.0 %collective-permute-start.10 = (bf16[1040,128]{1,0:T(8,128)(2,1)S(1)}, bf16[1040,128]{1,0:T(8,128)(2,1)S(1)}, u32[]{:S(2)}, u32[]{:S(2)}) collective-permute-start(bf16[1040,128]{1,0:T(8,128)(2,1)S(1)} %collective-permute-done.2.refs_4_), channel_id=1, source_target_pairs={{0,8},{8,16},{16,24},{1,9},{9,17},{17,25},{2,10},{10,18},{18,26},{... | collective-permute-start | bytes 798728 | tf_op jit(solution)/shard_map/ppermute | solution.py:729
  36.2 15.3 %collective-permute-start.5 = (bf16[2048,128]{1,0:T(8,128)(2,1)S(1)}, bf16[2048,128]{1,0:T(8,128)(2,1)S(1)}, u32[]{:S(2)}, u32[]{:S(2)}) collective-permute-start(bf16[2048,128]{1,0:T(8,128)(2,1)S(1)} %get-tuple-element.89), channel_id=1, source_target_pairs={{0,6},{2,4},{4,2},{6,0},{1,7},{3,5},{5,3},{7,1},{8,14},{10,12},{12... | collective-permute-start | bytes 1572872 | tf_op jit(solution)/shard_map/ppermute | solution.py:719
  44.4 24.2 %collective-permute-start.11 = (bf16[3120,128]{1,0:T(8,128)(2,1)S(1)}, bf16[3120,128]{1,0:T(8,128)(2,1)S(1)}, u32[]{:S(2)}, u32[]{:S(2)}) collective-permute-start(bf16[3120,128]{1,0:T(8,128)(2,1)S(1)} %constant_dynamic-update-slice_fusion.refs_1_), channel_id=1, source_target_pairs={{0,8},{8,16},{16,24},{1,9},{9,17},{17,25},{2,10},{10,18},{18,26},{... | collective-permute-start | bytes 2396168 | tf_op jit(solution)/shard_map/ppermute | solution.py:729
  74.6 1.2 collective-permute-start.12
  75.9 4.0 %collective-permute-start.13 = (f32[8,4,128]{2,1,0:T(4,128)S(1)}, f32[8,4,128]{2,1,0:T(4,128)S(1)}, u32[]{:S(2)}, u32[]{:S(2)}) collective-permute-start(f32[8,4,128]{2,1,0:T(4,128)S(1)} %add.8.refs_7_), channel_id=1, source_target_pairs={{0,2},{2,0},{4,6},{6,4},{1,3},{3,1},{5,7},{7,5},{8,10},{10,8},{12,... | collective-permute-start | bytes 49160 | tf_op jit(solution)/shard_map/ppermute | solution.py:719
  78.2 3.7 %collective-permute-start.14 = (f32[8,4,128]{2,1,0:T(4,128)S(1)}, f32[8,4,128]{2,1,0:T(4,128)S(1)}, u32[]{:S(2)}, u32[]{:S(2)}) collective-permute-start(f32[8,4,128]{2,1,0:T(4,128)S(1)} %add.8.refs_7_), channel_id=1, source_target_pairs={{0,4},{2,6},{4,0},{6,2},{1,5},{3,7},{5,1},{7,3},{8,12},{10,14},{12... | collective-permute-start | bytes 49160 | tf_op jit(solution)/shard_map/ppermute | solution.py:719
  79.2 4.6 %collective-permute-start.15 = (f32[8,4,128]{2,1,0:T(4,128)S(1)}, f32[8,4,128]{2,1,0:T(4,128)S(1)}, u32[]{:S(2)}, u32[]{:S(2)}) collective-permute-start(f32[8,4,128]{2,1,0:T(4,128)S(1)} %add.8.refs_7_), channel_id=1, source_target_pairs={{0,6},{2,4},{4,2},{6,0},{1,7},{3,5},{5,3},{7,1},{8,14},{10,12},{12... | collective-permute-start | bytes 49160 | tf_op jit(solution)/shard_map/ppermute | solution.py:719
  89.6 25.9 %collective-permute-start.19 = (bf16[2,1024,128]{2,1,0:T(8,128)(2,1)S(1)}, bf16[2,1024,128]{2,1,0:T(8,128)(2,1)S(1)}, u32[]{:S(2)}, u32[]{:S(2)}) collective-permute-start(bf16[2,1024,128]{2,1,0:T(8,128)(2,1)S(1)} %get-tuple-element.143), channel_id=1, source_target_pairs={{16,0},{24,8},{17,1},{25,9},{18,2},{26,10},{19,3},{27,11},{20,4},{... | collective-permute-start | bytes 1572872 | tf_op jit(solution)/shard_map/ppermute | solution.py:729
  101.5 14.2 %collective-permute-start.20 = (bf16[2,1024,128]{2,1,0:T(8,128)(2,1)S(1)}, bf16[2,1024,128]{2,1,0:T(8,128)(2,1)S(1)}, u32[]{:S(2)}, u32[]{:S(2)}) collective-permute-start(bf16[2,1024,128]{2,1,0:T(8,128)(2,1)S(1)} %get-tuple-element.144), channel_id=1, source_target_pairs={{8,0},{16,8},{24,16},{9,1},{17,9},{25,17},{10,2},{18,10},{26,18},{... | collective-permute-start | bytes 1572872 | tf_op jit(solution)/shard_map/ppermute | solution.py:729
  105.7 9.8 %collective-permute-start.18 = (bf16[1,4,256,128]{3,2,1,0:T(8,128)(2,1)S(1)}, bf16[1,4,256,128]{3,2,1,0:T(8,128)(2,1)S(1)}, u32[]{:S(2)}, u32[]{:S(2)}) collective-permute-start(bf16[1,4,256,128]{3,2,1,0:T(8,128)(2,1)S(1)} %bitcast.38), channel_id=1, source_target_pairs={{0,6},{2,4},{4,2},{6,0},{1,7},{3,5},{5,3},{7,1},{8,14},{10,12},{12... | collective-permute-start | bytes 786440 | tf_op jit(solution)/shard_map/ppermute | solution.py:719
  113.7 9.3 %collective-permute-start.16 = (bf16[1,4,256,128]{3,2,1,0:T(8,128)(2,1)S(1)}, bf16[1,4,256,128]{3,2,1,0:T(8,128)(2,1)S(1)}, u32[]{:S(2)}, u32[]{:S(2)}) collective-permute-start(bf16[1,4,256,128]{3,2,1,0:T(8,128)(2,1)S(1)} %bitcast.37), channel_id=1, source_target_pairs={{0,2},{2,0},{4,6},{6,4},{1,3},{3,1},{5,7},{7,5},{8,10},{10,8},{12,... | collective-permute-start | bytes 786440 | tf_op jit(solution)/shard_map/ppermute | solution.py:719
  115.5 10.3 %collective-permute-start.17 = (bf16[1,4,256,128]{3,2,1,0:T(8,128)(2,1)S(1)}, bf16[1,4,256,128]{3,2,1,0:T(8,128)(2,1)S(1)}, u32[]{:S(2)}, u32[]{:S(2)}) collective-permute-start(bf16[1,4,256,128]{3,2,1,0:T(8,128)(2,1)S(1)} %bitcast.36), channel_id=1, source_target_pairs={{0,4},{2,6},{4,0},{6,2},{1,5},{3,7},{5,1},{7,3},{8,12},{10,14},{12... | collective-permute-start | bytes 786440 | tf_op jit(solution)/shard_map/ppermute | solution.py:719
  115.8 12.4 %collective-permute-start.21 = (bf16[2,256,128]{2,1,0:T(8,128)(2,1)S(1)}, bf16[2,256,128]{2,1,0:T(8,128)(2,1)S(1)}, u32[]{:S(2)}, u32[]{:S(2)}) collective-permute-start(bf16[2,256,128]{2,1,0:T(8,128)(2,1)S(1)} %get-tuple-element.146), channel_id=1, source_target_pairs={{0,2},{2,0},{4,6},{6,4},{1,3},{3,1},{5,7},{7,5},{8,10},{10,8},{12,... | collective-permute-start | bytes 393224 | tf_op jit(solution)/shard_map/ppermute | solution.py:719
  117.1 11.2 %collective-permute-start.22 = (bf16[2,256,128]{2,1,0:T(8,128)(2,1)S(1)}, bf16[2,256,128]{2,1,0:T(8,128)(2,1)S(1)}, u32[]{:S(2)}, u32[]{:S(2)}) collective-permute-start(bf16[2,256,128]{2,1,0:T(8,128)(2,1)S(1)} %get-tuple-element.147), channel_id=1, source_target_pairs={{0,4},{2,6},{4,0},{6,2},{1,5},{3,7},{5,1},{7,3},{8,12},{10,14},{12... | collective-permute-start | bytes 393224 | tf_op jit(solution)/shard_map/ppermute | solution.py:719
  118.3 10.0 %collective-permute-start.23 = (bf16[2,256,128]{2,1,0:T(8,128)(2,1)S(1)}, bf16[2,256,128]{2,1,0:T(8,128)(2,1)S(1)}, u32[]{:S(2)}, u32[]{:S(2)}) collective-permute-start(bf16[2,256,128]{2,1,0:T(8,128)(2,1)S(1)} %get-tuple-element.148), channel_id=1, source_target_pairs={{0,6},{2,4},{4,2},{6,0},{1,7},{3,5},{5,3},{7,1},{8,14},{10,12},{12... | collective-permute-start | bytes 393224 | tf_op jit(solution)/shard_map/ppermute | solution.py:719

commit v2 on v1

--- a/solution.py
+++ b/solution.py
@@ -108,33 +108,41 @@
     )(*scalars, *arrays)
 
 
-def join_heads(pieces, count, per_part):
-    parts = len(pieces)
-    rows, width = pieces[0].shape[-2:]
-    heads = parts * per_part
-
+def join_heads(groups):
+    parts = len(groups[0][0])
+    rows, width = groups[0][0][0].shape[-2:]
     steps = 4
     cut = rows // steps
 
     def kernel(*refs):
-        ins, outs = refs[:parts], refs[parts:]
+        ins, outs = list(refs[: parts * len(groups)]), list(refs[parts * len(groups) :])
         mine = lax.axis_index("part")
-        for a in range(count):
-            for m in range(parts):
-                for r in range(per_part):
-                    head = jnp.bitwise_xor(mine, m) * per_part + r
-                    outs[a][pl.ds(head, cut, stride=heads), :] = ins[m][a, r].astype(F32)
-
+        for _, count, per_part in groups:
+            for a in range(count):
+                for m in range(parts):
+                    for r in range(per_part):
+                        head = jnp.bitwise_xor(mine, m) * per_part + r
+                        rows_of_head = pl.ds(head, cut, stride=parts * per_part)
+                        outs[a][rows_of_head, :] = ins[m][a, r].astype(F32)
+            del ins[:parts], outs[:count]
+
+    in_specs, out_specs, out_shape = [], [], []
+    for _, count, per_part in groups:
+        heads = parts * per_part
+        block = (count, per_part, cut, width)
+        in_specs += [pl.BlockSpec(block, lambda i: (0, 0, i, 0))] * parts
+        out_specs += [pl.BlockSpec((cut * heads, width), lambda i: (i, 0))] * count
+        out_shape += [jax.ShapeDtypeStruct((rows * heads, width), F32)] * count
     return pl.pallas_call(
         kernel,
         grid=(steps,),
-        in_specs=[pl.BlockSpec((count, per_part, cut, width), lambda i: (0, 0, i, 0))] * parts,
-        out_specs=[pl.BlockSpec((cut * heads, width), lambda i: (i, 0))] * count,
-        out_shape=[jax.ShapeDtypeStruct((rows * heads, width), F32)] * count,
+        in_specs=in_specs,
+        out_specs=out_specs,
+        out_shape=out_shape,
         compiler_params=params(),
-        cost_estimate=cost(0, 6 * count * rows * heads * width),
+        cost_estimate=cost(0, sum(6 * shape.size for shape in out_shape)),
         name="join_heads",
-    )(*pieces)
+    )(*[piece for pieces, _, _ in groups for piece in pieces])
 
 
 def slot_of(me_ref, m, rows):
@@ -820,9 +828,9 @@
             everyone, None,
         )
         arrived.append(moved_on(part, -distance))
-    turns = [turn[::-1] for turn in (everyone[-1:], everyone[:-1]) if turn]
+    turns = [everyone[-1:], everyone[1:-1], everyone[:1]] if parts > 1 else [everyone]
     held, dq_pieces = None, [None] * parts
-    for order in turns:
+    for order in filter(None, turns):
         held, *done = backward_chunk(
             sh, me, back, qq, spans[0], 0, grads, lse, dots, dq, None, order, held
         )
@@ -833,9 +841,10 @@
     if arrived[1:]:
         held = add_arrived(held, arrived[:-1])
     dkv_pieces = exchanged(combine(sh, me, arrived[-1], held), parts)
-    (product_queries,) = join_heads(dq_pieces, 1, group)
     dkv_pieces = [p.reshape(2, 1, rows, width) for p in dkv_pieces]
-    product_keys, product_values = join_heads(dkv_pieces, 2, 1)
+    product_queries, product_keys, product_values = join_heads(
+        [(dq_pieces, 1, group), (dkv_pieces, 2, 1)]
+    )
     return (
         product_queries.reshape(queries.shape),
         product_keys.reshape(keys.shape),

time: 131 us -> 127 us (0.969)
  the two profiles are of different devices: /device:TPU:20 before, /device:TPU:8 now
where the time goes in v2:
time: 127 us; the launch traced here: 125 us
  starting transfers between devices  43.6 us (34%)
  Pallas kernels  39.9 us (31%)
  waiting for transfers between devices  34.8 us (27%)
  local copies, waits for them, and re-layouts  4.95 us (4%)
    ppermute x8, waiting for transfers between devices, moved_on(): return lax.ppermute(value, 'span', pairs)  24.6 us
    ppermute x15, starting transfers between devices, exchanged_with(): lax.ppermute(piece, 'part', [(i, i ^ m) for i in range(parts)])  22.4 us
    ppermute x8, starting transfers between devices, moved_on(): return lax.ppermute(value, 'span', pairs)  21.1 us
    pallas_call x5, Pallas kernels, backward_chunk(): pl.pallas_call(kernel, in_specs=[SMEM, SMEM] + [VMEM] * len(operands), ou...  14.4 us
    pallas_call x3, Pallas kernels, forward_own(): pl.pallas_call(kernel, in_specs=[SMEM, SMEM] + [VMEM] * len(operands), ou...  9.26 us
    ppermute x15, waiting for transfers between devices, exchanged_with(): lax.ppermute(piece, 'part', [(i, i ^ m) for i in range(parts)])  9.05 us
    pallas_call x2, Pallas kernels, forward_chunk(): pl.pallas_call(kernel, in_specs=[SMEM, SMEM] + [VMEM] * len(operands), ou...  8.1 us
    pallas_call x2, Pallas kernels, split_heads(): pl.pallas_call(kernel, in_specs=[SMEM] * len(scalars) + [pl.BlockSpec(mem...  5.1 us
  transfers between devices with their start and end apart: 24, of which 13 were waited for; matrix products, arithmetic and copies ran while one was open for 2% of the time, Pallas kernels for 24%

profile of v2, /device:TPU:8, one launch (start us, length us, event | category | flops | bytes accessed | tf_op | source)
XLA Modules:
  0.0 124.9 jit_solution(16155408339495496709)
XLA Ops:
  0.6 2.9 %split_heads.2 = (bf16[1040,128]{1,0:T(8,128)(2,1)}, bf16[1040,128]{1,0:T(8,128)(2,1)}, bf16[1040,128]{1,0:T(8,128)(2,1)}, bf16[1040,128]{1,0:T(8,128)(2,1)}) custom-call(s32[2]{0:T(128)} %refs_0_.1, bf16[1024,128]{1,0:T(8,128)(2,1)} %bitcast.40, bf16[1024,128]{1,0:T(8,128)(2,1)} %bitcast.41, bf16[1024,128]{1,0:T(8,128)(2,1)} %bitcast.42, ...), custom_call_target="tpu_custom_call" | custom-call | bytes 2097152 | tf_op jit(solution)/shard_map/split_heads/pallas_call | solution.py:99
  3.6 3.5 %collective-permute-start.3 = (bf16[1040,128]{1,0:T(8,128)(2,1)}, bf16[1040,128]{1,0:T(8,128)(2,1)S(1)}, u32[]{:S(2)}, u32[]{:S(2)}) collective-permute-start(bf16[1040,128]{1,0:T(8,128)(2,1)} %get-tuple-element.79.refs_1_), channel_id=1, source_target_pairs={{0,8},{8,16},{16,24},{1,9},{9,17},{17,25},{2,10},{10,18},{18,26},{... | collective-permute-start | bytes 798728 | tf_op jit(solution)/shard_map/ppermute | solution.py:737
  7.0 2.5 %collective-permute-start.2 = (bf16[1040,128]{1,0:T(8,128)(2,1)}, bf16[1040,128]{1,0:T(8,128)(2,1)S(1)}, u32[]{:S(2)}, u32[]{:S(2)}) collective-permute-start(bf16[1040,128]{1,0:T(8,128)(2,1)} %get-tuple-element.82), channel_id=1, source_target_pairs={{0,6},{2,4},{4,2},{6,0},{1,7},{3,5},{5,3},{7,1},{8,14},{10,12},{12... | collective-permute-start | bytes 798728 | tf_op jit(solution)/shard_map/ppermute | solution.py:727
  9.6 0.5 collective-permute-start.1
  10.1 0.5 collective-permute-start
  10.6 0.8 slice_reduce_fusion.3
  11.4 1.2 copy-done
  12.6 1.2 copy-done.1
  13.9 2.2 %split_heads.3 = (bf16[2048,128]{1,0:T(8,128)(2,1)S(1)}, bf16[2048,128]{1,0:T(8,128)(2,1)S(1)}, bf16[2048,128]{1,0:T(8,128)(2,1)S(1)}, bf16[2048,128]{1,0:T(8,128)(2,1)S(1)}) custom-call(bf16[4096,128]{1,0:T(8,128)(2,1)S(1)} %bitcast.27, bf16[4096,128]{1,0:T(8,128)(2,1)S(1)} %bitcast.28), custom_call_target="tpu_custom_call" | custom-call | bytes 4194304 | tf_op jit(solution)/shard_map/split_heads/pallas_call | solution.py:99
  16.1 3.5 %collective-permute-start.7 = (bf16[1040,128]{1,0:T(8,128)(2,1)S(1)}, bf16[1040,128]{1,0:T(8,128)(2,1)S(1)}, u32[]{:S(2)}, u32[]{:S(2)}) collective-permute-start(bf16[1040,128]{1,0:T(8,128)(2,1)S(1)} %collective-permute-done.3.refs_0_), channel_id=1, source_target_pairs={{0,8},{8,16},{16,24},{1,9},{9,17},{17,25},{2,10},{10,18},{18,26},{... | collective-permute-start | bytes 798728 | tf_op jit(solution)/shard_map/ppermute | solution.py:737
  19.5 0.7 multiply_bitcast_fusion
  20.2 0.1 copy.29
  20.4 0.2 broadcast_in_dim.3
  20.6 1.6 %collective-permute-start.4 = (bf16[2048,128]{1,0:T(8,128)(2,1)S(1)}, bf16[2048,128]{1,0:T(8,128)(2,1)S(1)}, u32[]{:S(2)}, u32[]{:S(2)}) collective-permute-start(bf16[2048,128]{1,0:T(8,128)(2,1)S(1)} %get-tuple-element.90), channel_id=1, source_target_pairs={{0,2},{2,0},{4,6},{6,4},{1,3},{3,1},{5,7},{7,5},{8,10},{10,8},{12,... | collective-permute-start | bytes 1572872 | tf_op jit(solution)/shard_map/ppermute | solution.py:727
  22.1 1.5 %collective-permute-start.6 = (bf16[2048,128]{1,0:T(8,128)(2,1)S(1)}, bf16[2048,128]{1,0:T(8,128)(2,1)S(1)}, u32[]{:S(2)}, u32[]{:S(2)}) collective-permute-start(bf16[2048,128]{1,0:T(8,128)(2,1)S(1)} %get-tuple-element.98), channel_id=1, source_target_pairs={{0,4},{2,6},{4,0},{6,2},{1,5},{3,7},{5,1},{7,3},{8,12},{10,14},{12... | collective-permute-start | bytes 1572872 | tf_op jit(solution)/shard_map/ppermute | solution.py:727
  23.7 0.1 slice_reduce_fusion
  23.8 0.1 slice_reduce_fusion.1
  23.9 1.1 collective-permute-done.7.refs_0_
  25.0 3.5 %collective-permute-start.8 = (bf16[1040,128]{1,0:T(8,128)(2,1)S(1)}, bf16[1040,128]{1,0:T(8,128)(2,1)S(1)}, u32[]{:S(2)}, u32[]{:S(2)}) collective-permute-start(bf16[1040,128]{1,0:T(8,128)(2,1)S(1)} %collective-permute-done.refs_2_), channel_id=1, source_target_pairs={{0,8},{8,16},{16,24},{1,9},{9,17},{17,25},{2,10},{10,18},{18,26},{... | collective-permute-start | bytes 798728 | tf_op jit(solution)/shard_map/ppermute | solution.py:737
  28.4 0.1 slice_reduce_fusion.2
  28.6 0.1 maximum_convert_fusion.back_ref
  28.6 2.2 %collective-permute-start.9 = (bf16[1040,128]{1,0:T(8,128)(2,1)S(1)}, bf16[1040,128]{1,0:T(8,128)(2,1)S(1)}, u32[]{:S(2)}, u32[]{:S(2)}) collective-permute-start(bf16[1040,128]{1,0:T(8,128)(2,1)S(1)} %collective-permute-done.1.refs_3_), channel_id=1, source_target_pairs={{0,8},{8,16},{16,24},{1,9},{9,17},{17,25},{2,10},{10,18},{18,26},{... | collective-permute-start | bytes 798728 | tf_op jit(solution)/shard_map/ppermute | solution.py:737
  30.8 0.0 copy-start.2
  30.9 0.9 copy-done.2
  31.8 2.2 %forward_own.3 = (f32[8,256,512]{2,1,0:T(8,128)S(1)}, f32[8,8,512]{2,1,0:T(8,128)S(1)}, bf16[8,512,256]{2,1,0:T(8,128)(2,1)S(1)}, bf16[8,1024,512]{2,1,0:T(8,128...) custom-call(s32[1]{0:T(128)} %bitcast.me_ref, ...), custom_call_target="tpu_custom_call" | custom-call | flops 805306368 | bytes 2097152 | tf_op jit(solution)/shard_map/forward_own/pallas_call | solution.py:430
  34.0 1.9 %collective-permute-start.10 = (bf16[1040,128]{1,0:T(8,128)(2,1)S(1)}, bf16[1040,128]{1,0:T(8,128)(2,1)S(1)}, u32[]{:S(2)}, u32[]{:S(2)}) collective-permute-start(bf16[1040,128]{1,0:T(8,128)(2,1)S(1)} %collective-permute-done.2.refs_4_), channel_id=1, source_target_pairs={{0,8},{8,16},{16,24},{1,9},{9,17},{17,25},{2,10},{10,18},{18,26},{... | collective-permute-start | bytes 798728 | tf_op jit(solution)/shard_map/ppermute | solution.py:737
  35.9 5.1 %collective-permute-start.5 = (bf16[2048,128]{1,0:T(8,128)(2,1)S(1)}, bf16[2048,128]{1,0:T(8,128)(2,1)S(1)}, u32[]{:S(2)}, u32[]{:S(2)}) collective-permute-start(bf16[2048,128]{1,0:T(8,128)(2,1)S(1)} %get-tuple-element.91), channel_id=1, source_target_pairs={{0,6},{2,4},{4,2},{6,0},{1,7},{3,5},{5,3},{7,1},{8,14},{10,12},{12... | collective-permute-start | bytes 1572872 | tf_op jit(solution)/shard_map/ppermute | solution.py:727
  41.0 0.6 collective-permute-done.9
  41.6 3.0 %collective-permute-done.10 = bf16[1040,128]{1,0:T(8,128)(2,1)S(1)} collective-permute-done((bf16[1040,128]{1,0:T(8,128)(2,1)S(1)}, bf16[1040,128]{1,0:T(8,128)(2,1)S(1)}, u32[]{:S(2)}, u32[]{:S(2)}) %collective-permute-start.10) | collective-permute-done | bytes 266272 | tf_op jit(solution)/shard_map/ppermute | solution.py:737
  44.7 3.3 %collective-permute-start.11 = (bf16[3120,128]{1,0:T(8,128)(2,1)S(1)}, bf16[3120,128]{1,0:T(8,128)(2,1)S(1)}, u32[]{:S(2)}, u32[]{:S(2)}) collective-permute-start(bf16[3120,128]{1,0:T(8,128)(2,1)S(1)} %constant_dynamic-update-slice_fusion.refs_1_), channel_id=1, source_target_pairs={{0,8},{8,16},{16,24},{1,9},{9,17},{17,25},{2,10},{10,18},{18,26},{... | collective-permute-start | bytes 2396168 | tf_op jit(solution)/shard_map/ppermute | solution.py:737
  48.1 4.8 %forward_own.4 = (f32[8,256,512]{2,1,0:T(8,128)S(1)}, f32[8,8,512]{2,1,0:T(8,128)S(1)}, bf16[8,512,256]{2,1,0:T(8,128)(2,1)S(1)}, bf16[8,1024,512]{2,1,0:T(8,128)(2,1)S(1)}, f32[8,8,1,512]{3,2,1,0:T(1,128)S(1)}) custom-call(s32[1]{0:T(128)} %bitcast.me_ref, ...), custom_call_target="tpu_custom_call", output_to_operand_aliasing={{0}: (9, {}), {1}: (10, {}), {2}: (11, {}), {3}: (12, {}), ... | custom-call | flops 1610612736 | bytes 2097152 | tf_op jit(solution)/shard_map/forward_own/pallas_call | solution.py:430
  52.9 2.3 %forward_own.5 = (f32[8,256,512]{2,1,0:T(8,128)S(1)}, f32[8,8,512]{2,1,0:T(8,128)S(1)}, bf16[8,512,256]{2,1,0:T(8,128)(2,1)S(1)}, bf16[8,1024,512]{2,1,0:T(8,128)(2,1)S(1)}, f32[8,8,1,512]{3,2,1,0:T(1,128)S(1)}) custom-call(s32[1]{0:T(128)} %bitcast.me_ref, ...), custom_call_target="tpu_custom_call", output_to_operand_aliasing={{0}: (8, {}), {1}: (9, {}), {2}: (10, {}), {3}: (11, {}), {... | custom-call | flops 805306368 | bytes 2097152 | tf_op jit(solution)/shard_map/forward_own/pallas_call | solution.py:430
  55.2 5.9 %forward_chunk.1 = (bf16[1024,128]{1,0:T(8,128)(2,1)S(1)}, bf16[1024,128]{1,0:T(8,128)(2,1)S(1)}, bf16[128,1024]{1,0:T(8,128)(2,1)S(1)}, f32[8,256,512]{2,1,0:T(...) custom-call(s32[1]{0:T(128)} %bitcast.me_ref, ...), custom_call_target="tpu_custom_call", output_to_operand_aliasing={{3}: (5, {}), {4}: (6, {})} | custom-call | flops 6442450944 | bytes 12582912 | tf_op jit(solution)/shard_map/forward_chunk/pallas_call | solution.py:518
  61.1 2.7 %collective-permute-done.11.refs_1_ = bf16[3120,128]{1,0:T(8,128)(2,1)S(1)} collective-permute-done((bf16[3120,128]{1,0:T(8,128)(2,1)S(1)}, bf16[3120,128]{1,0:T(8,128)(2,1)S(1)}, u32[]{:S(2)}, u32[]{:S(2)}) %collective-permute-start.11) | collective-permute-done | bytes 798752 | tf_op jit(solution)/shard_map/ppermute | solution.py:737
  63.8 2.2 %forward_far.1 = (bf16[1024,128]{1,0:T(8,128)(2,1)S(1)}, bf16[1024,128]{1,0:T(8,128)(2,1)S(1)}, bf16[128,1024]{1,0:T(8,128)(2,1)S(1)}, f32[8,256,512]{2,1,0:T(8,...) custom-call(s32[1]{0:T(128)} %bitcast.me_ref, ...), custom_call_target="tpu_custom_call", output_to_operand_aliasing={{3}: (5, {}), {4}: (6, {})} | custom-call | flops 6442450944 | bytes 12582912 | tf_op jit(solution)/shard_map/forward_far/pallas_call | solution.py:518
  66.0 0.1 collective-permute-start.12
  66.1 1.2 collective-permute-done.12
  67.2 1.9 %collective-permute-start.13 = (f32[8,4,128]{2,1,0:T(4,128)S(1)}, f32[8,4,128]{2,1,0:T(4,128)S(1)}, u32[]{:S(2)}, u32[]{:S(2)}) collective-permute-start(f32[8,4,128]{2,1,0:T(4,128)S(1)} %add.8.refs_7_), channel_id=1, source_target_pairs={{0,2},{2,0},{4,6},{6,4},{1,3},{3,1},{5,7},{7,5},{8,10},{10,8},{12,... | collective-permute-start | bytes 49160 | tf_op jit(solution)/shard_map/ppermute | solution.py:727
  69.1 1.1 collective-permute-start.14
  70.3 0.5 collective-permute-start.15
  70.8 0.2 collective-permute-done.13.refs_8_
  71.0 1.9 %collective-permute-done.14.refs_9_ = f32[8,4,128]{2,1,0:T(4,128)S(1)} collective-permute-done((f32[8,4,128]{2,1,0:T(4,128)S(1)}, f32[8,4,128]{2,1,0:T(4,128)S(1)}, u32[]{:S(2)}, u32[]{:S(2)}) %collective-permute-start.14) | collective-permute-done | bytes 16416 | tf_op jit(solution)/shard_map/ppermute | solution.py:727
  72.9 2.0 %collective-permute-done.15.refs_10_ = f32[8,4,128]{2,1,0:T(4,128)S(1)} collective-permute-done((f32[8,4,128]{2,1,0:T(4,128)S(1)}, f32[8,4,128]{2,1,0:T(4,128)S(1)}, u32[]{:S(2)}, u32[]{:S(2)}) %collective-permute-start.15) | collective-permute-done | bytes 16416 | tf_op jit(solution)/shard_map/ppermute | solution.py:727
  74.9 2.4 %backward_chunk.5 = (bf16[2,1024,128]{2,1,0:T(8,128)(2,1)S(1)}, f32[8,128,512]{2,1,0:T(8,128)S(1)}, bf16[8,512,128]{2,1,0:T(8,128)(2,1)S(1)}, f32[8,1,512]{2,1,0:T(1,128)S(1)}) custom-call(s32[1]{0:T(128)} %bitcast.me_ref, s32[8]{0:T(128)S(1)} %maximum_convert_fusion.back_ref, bf16[8,512,256]{2,1,0:T(8,128)(2,1)S(1)} %get-tuple-element.109.qq_s.refs_0_, ...), custom_call_target="tpu_custom_call" | custom-call | flops 5368709120 | bytes 33554432 | tf_op jit(solution)/shard_map/backward_chunk/pallas_call | solution.py:674
  77.3 1.3 %collective-permute-start.19 = (bf16[2,1024,128]{2,1,0:T(8,128)(2,1)S(1)}, bf16[2,1024,128]{2,1,0:T(8,128)(2,1)S(1)}, u32[]{:S(2)}, u32[]{:S(2)}) collective-permute-start(bf16[2,1024,128]{2,1,0:T(8,128)(2,1)S(1)} %get-tuple-element.146), channel_id=1, source_target_pairs={{16,0},{24,8},{17,1},{25,9},{18,2},{26,10},{19,3},{27,11},{20,4},{... | collective-permute-start | bytes 1572872 | tf_op jit(solution)/shard_map/ppermute | solution.py:737
  78.6 4.4 %backward_chunk.6 = (bf16[2,1024,128]{2,1,0:T(8,128)(2,1)S(1)}, f32[8,128,512]{2,1,0:T(8,128)S(1)}) custom-call(s32[1]{0:T(128)} %bitcast.me_ref, s32[8]{0:T(128)S(1)} %maximum_convert_fusion.back_ref, bf16[8,512,256]{2,1,0:T(8,128)(2,1)S(1)} %get-tuple-element.109.qq_s.refs_0_, ...), custom_call_target="tpu_custom_call", output_to_operand_aliasing={{1}: (11, {})} | custom-call | flops 5368709120 | bytes 33554432 | tf_op jit(solution)/shard_map/backward_chunk/pallas_call | solution.py:674
  82.9 1.9 %collective-permute-start.20 = (bf16[2,1024,128]{2,1,0:T(8,128)(2,1)S(1)}, bf16[2,1024,128]{2,1,0:T(8,128)(2,1)S(1)}, u32[]{:S(2)}, u32[]{:S(2)}) collective-permute-start(bf16[2,1024,128]{2,1,0:T(8,128)(2,1)S(1)} %get-tuple-element.147), channel_id=1, source_target_pairs={{8,0},{16,8},{24,16},{9,1},{17,9},{25,17},{10,2},{18,10},{26,18},{... | collective-permute-start | bytes 1572872 | tf_op jit(solution)/shard_map/ppermute | solution.py:737
  84.9 2.0 %backward_chunk.7 = (f32[2,1024,128]{2,1,0:T(8,128)S(1)}, bf16[4,256,128]{2,1,0:T(8,128)(2,1)S(1)}) custom-call(s32[1]{0:T(128)} %bitcast.me_ref, s32[8]{0:T(128)S(1)} %maximum_convert_fusion.back_ref, bf16[8,512,256]{2,1,0:T(8,128)(2,1)S(1)} %get-tuple-element.109.qq_s.refs_0_, bf16[1024,128]{1,0:T(8,128)(2,1)S(1)} %get-tuple-element.93.refs_2_.refs_1_, ...), custom_call_target="tpu_custom_call" | custom-call | flops 1 | bytes 1 | tf_op jit(solution)/shard_map/backward_chunk/pallas_call | solution.py:674
  86.8 0.4 collective-permute-start.18
  87.2 4.0 %backward_chunk.8 = (f32[2,1024,128]{2,1,0:T(8,128)S(1)}, bf16[4,256,128]{2,1,0:T(8,128)(2,1)S(1)}, bf16[4,256,128]{2,1,0:T(8,128)(2,1)S(1)}) custom-call(s32[1]{0:T(128)} %bitcast.me_ref, s32[8]{0:T(128)S(1)} %maximum_convert_fusion.back_ref, bf16[8,512,256]{2,1,0:T(8,128)(2,1)S(1)} %get-tuple-element.109.qq_s.refs_0_, ...), custom_call_target="tpu_custom_call", output_to_operand_aliasing={{0}: (12, {})} | custom-call | flops 1 | bytes 1 | tf_op jit(solution)/shard_map/backward_chunk/pallas_call | solution.py:674
  91.2 1.5 %collective-permute-start.16 = (bf16[1,4,256,128]{3,2,1,0:T(8,128)(2,1)S(1)}, bf16[1,4,256,128]{3,2,1,0:T(8,128)(2,1)S(1)}, u32[]{:S(2)}, u32[]{:S(2)}) collective-permute-start(bf16[1,4,256,128]{3,2,1,0:T(8,128)(2,1)S(1)} %bitcast.37), channel_id=1, source_target_pairs={{0,2},{2,0},{4,6},{6,4},{1,3},{3,1},{5,7},{7,5},{8,10},{10,8},{12,... | collective-permute-start | bytes 786440 | tf_op jit(solution)/shard_map/ppermute | solution.py:727
  92.7 1.8 %collective-permute-start.17 = (bf16[1,4,256,128]{3,2,1,0:T(8,128)(2,1)S(1)}, bf16[1,4,256,128]{3,2,1,0:T(8,128)(2,1)S(1)}, u32[]{:S(2)}, u32[]{:S(2)}) collective-permute-start(bf16[1,4,256,128]{3,2,1,0:T(8,128)(2,1)S(1)} %bitcast.36), channel_id=1, source_target_pairs={{0,4},{2,6},{4,0},{6,2},{1,5},{3,7},{5,1},{7,3},{8,12},{10,14},{12... | collective-permute-start | bytes 786440 | tf_op jit(solution)/shard_map/ppermute | solution.py:727
  94.5 1.7 %backward_chunk.9 = (f32[2,1024,128]{2,1,0:T(8,128)S(1)}, bf16[4,256,128]{2,1,0:T(8,128)(2,1)S(1)}) custom-call(s32[1]{0:T(128)} %bitcast.me_ref, s32[8]{0:T(128)S(1)} %maximum_convert_fusion.back_ref, bf16[8,512,256]{2,1,0:T(8,128)(2,1)S(1)} %get-tuple-element.109.qq_s.refs_0_, ...), custom_call_target="tpu_custom_call", output_to_operand_aliasing={{0}: (12, {})} | custom-call | flops 1 | bytes 1 | tf_op jit(solution)/shard_map/backward_chunk/pallas_call | solution.py:674
  96.2 5.4 %collective-permute-done.19.refs_0_ = bf16[2,1024,128]{2,1,0:T(8,128)(2,1)S(1)} collective-permute-done((bf16[2,1024,128]{2,1,0:T(8,128)(2,1)S(1)}, bf16[2,1024,128]{2,1,0:T(8,128)(2,1)S(1)}, u32[]{:S(2)}, u32[]{:S(2)}) %collective-permute-start.19) | collective-permute-done | bytes 524320 | tf_op jit(solution)/shard_map/ppermute | solution.py:737
  101.6 0.2 add_arrived.1.held_ref
  101.8 11.8 %collective-permute-done.20.arrived_ref = bf16[2,1024,128]{2,1,0:T(8,128)(2,1)S(1)} collective-permute-done((bf16[2,1024,128]{2,1,0:T(8,128)(2,1)S(1)}, bf16[2,1024,128]{2,1,0:T(8,128)(2,1)S(1)}, u32[]{:S(2)}, u32[]{:S(2)}) %collective-permute-start.20) | collective-permute-done | bytes 524320 | tf_op jit(solution)/shard_map/ppermute | solution.py:737
  113.6 0.1 combine.1
  113.7 0.8 collective-permute-start.21
  114.6 1.7 %collective-permute-start.22 = (bf16[2,256,128]{2,1,0:T(8,128)(2,1)S(1)}, bf16[2,256,128]{2,1,0:T(8,128)(2,1)S(1)}, u32[]{:S(2)}, u32[]{:S(2)}) collective-permute-start(bf16[2,256,128]{2,1,0:T(8,128)(2,1)S(1)} %get-tuple-element.150), channel_id=1, source_target_pairs={{0,4},{2,6},{4,0},{6,2},{1,5},{3,7},{5,1},{7,3},{8,12},{10,14},{12... | collective-permute-start | bytes 393224 | tf_op jit(solution)/shard_map/ppermute | solution.py:727
  116.3 1.0 collective-permute-start.23
  117.3 1.6 %collective-permute-done.21 = bf16[2,256,128]{2,1,0:T(8,128)(2,1)S(1)} collective-permute-done((bf16[2,256,128]{2,1,0:T(8,128)(2,1)S(1)}, bf16[2,256,128]{2,1,0:T(8,128)(2,1)S(1)}, u32[]{:S(2)}, u32[]{:S(2)}) %collective-permute-start.21) | collective-permute-done | bytes 131104 | tf_op jit(solution)/shard_map/ppermute | solution.py:727
  118.8 1.1 collective-permute-done.22
  119.9 2.3 %collective-permute-done.23 = bf16[2,256,128]{2,1,0:T(8,128)(2,1)S(1)} collective-permute-done((bf16[2,256,128]{2,1,0:T(8,128)(2,1)S(1)}, bf16[2,256,128]{2,1,0:T(8,128)(2,1)S(1)}, u32[]{:S(2)}, u32[]{:S(2)}) %collective-permute-start.23) | collective-permute-done | bytes 131104 | tf_op jit(solution)/shard_map/ppermute | solution.py:727
  122.2 2.7 %join_heads.1 = (f32[4096,128]{1,0:T(8,128)}, f32[1024,128]{1,0:T(8,128)}, f32[1024,128]{1,0:T(8,128)}) custom-call(bf16[1,4,256,128]{3,2,1,0:T(8,128)(2,1)S(1)} %bitcast.31, bf16[1,4,256,128]{3,2,1,0:T(8,128)(2,1)S(1)} %collective-permute-done.16.refs_1_, bf16[1,4,256,128]{3,2,1,0:T(8,128)(2,1)S(1)} %collective-permute-done.17.refs_2_, ...), custom_call_target="tpu_custom_call" | custom-call | bytes 4718592 | tf_op jit(solution)/shard_map/join_heads/pallas_call | solution.py:136
  (18 shorter events, 0.1 us)
Async XLA Ops:
  3.6 12.5 %collective-permute-start.3 = (bf16[1040,128]{1,0:T(8,128)(2,1)}, bf16[1040,128]{1,0:T(8,128)(2,1)S(1)}, u32[]{:S(2)}, u32[]{:S(2)}) collective-permute-start(bf16[1040,128]{1,0:T(8,128)(2,1)} %get-tuple-element.79.refs_1_), channel_id=1, source_target_pairs={{0,8},{8,16},{16,24},{1,9},{9,17},{17,25},{2,10},{10,18},{18,26},{... | collective-permute-start | bytes 798728 | tf_op jit(solution)/shard_map/ppermute | solution.py:737
  7.0 15.1 %collective-permute-start.2 = (bf16[1040,128]{1,0:T(8,128)(2,1)}, bf16[1040,128]{1,0:T(8,128)(2,1)S(1)}, u32[]{:S(2)}, u32[]{:S(2)}) collective-permute-start(bf16[1040,128]{1,0:T(8,128)(2,1)} %get-tuple-element.82), channel_id=1, source_target_pairs={{0,6},{2,4},{4,2},{6,0},{1,7},{3,5},{5,3},{7,1},{8,14},{10,12},{12... | collective-permute-start | bytes 798728 | tf_op jit(solution)/shard_map/ppermute | solution.py:727
  9.6 14.2 %collective-permute-start.1 = (bf16[1040,128]{1,0:T(8,128)(2,1)}, bf16[1040,128]{1,0:T(8,128)(2,1)S(1)}, u32[]{:S(2)}, u32[]{:S(2)}) collective-permute-start(bf16[1040,128]{1,0:T(8,128)(2,1)} %get-tuple-element.81), channel_id=1, source_target_pairs={{0,4},{2,6},{4,0},{6,2},{1,5},{3,7},{5,1},{7,3},{8,12},{10,14},{12... | collective-permute-start | bytes 798728 | tf_op jit(solution)/shard_map/ppermute | solution.py:727
  10.1 13.8 %collective-permute-start = (bf16[1040,128]{1,0:T(8,128)(2,1)}, bf16[1040,128]{1,0:T(8,128)(2,1)S(1)}, u32[]{:S(2)}, u32[]{:S(2)}) collective-permute-start(bf16[1040,128]{1,0:T(8,128)(2,1)} %get-tuple-element.80), channel_id=1, source_target_pairs={{0,2},{2,0},{4,6},{6,4},{1,3},{3,1},{5,7},{7,5},{8,10},{10,8},{12,... | collective-permute-start | bytes 798728 | tf_op jit(solution)/shard_map/ppermute | solution.py:727
  11.4 1.2 copy-start
  12.6 1.2 copy-start.1
  16.1 8.9 %collective-permute-start.7 = (bf16[1040,128]{1,0:T(8,128)(2,1)S(1)}, bf16[1040,128]{1,0:T(8,128)(2,1)S(1)}, u32[]{:S(2)}, u32[]{:S(2)}) collective-permute-start(bf16[1040,128]{1,0:T(8,128)(2,1)S(1)} %collective-permute-done.3.refs_0_), channel_id=1, source_target_pairs={{0,8},{8,16},{16,24},{1,9},{9,17},{17,25},{2,10},{10,18},{18,26},{... | collective-permute-start | bytes 798728 | tf_op jit(solution)/shard_map/ppermute | solution.py:737
  20.6 15.3 %collective-permute-start.4 = (bf16[2048,128]{1,0:T(8,128)(2,1)S(1)}, bf16[2048,128]{1,0:T(8,128)(2,1)S(1)}, u32[]{:S(2)}, u32[]{:S(2)}) collective-permute-start(bf16[2048,128]{1,0:T(8,128)(2,1)S(1)} %get-tuple-element.90), channel_id=1, source_target_pairs={{0,2},{2,0},{4,6},{6,4},{1,3},{3,1},{5,7},{7,5},{8,10},{10,8},{12,... | collective-permute-start | bytes 1572872 | tf_op jit(solution)/shard_map/ppermute | solution.py:727
  22.1 25.9 %collective-permute-start.6 = (bf16[2048,128]{1,0:T(8,128)(2,1)S(1)}, bf16[2048,128]{1,0:T(8,128)(2,1)S(1)}, u32[]{:S(2)}, u32[]{:S(2)}) collective-permute-start(bf16[2048,128]{1,0:T(8,128)(2,1)S(1)} %get-tuple-element.98), channel_id=1, source_target_pairs={{0,4},{2,6},{4,0},{6,2},{1,5},{3,7},{5,1},{7,3},{8,12},{10,14},{12... | collective-permute-start | bytes 1572872 | tf_op jit(solution)/shard_map/ppermute | solution.py:727
  25.0 16.0 %collective-permute-start.8 = (bf16[1040,128]{1,0:T(8,128)(2,1)S(1)}, bf16[1040,128]{1,0:T(8,128)(2,1)S(1)}, u32[]{:S(2)}, u32[]{:S(2)}) collective-permute-start(bf16[1040,128]{1,0:T(8,128)(2,1)S(1)} %collective-permute-done.refs_2_), channel_id=1, source_target_pairs={{0,8},{8,16},{16,24},{1,9},{9,17},{17,25},{2,10},{10,18},{18,26},{... | collective-permute-start | bytes 798728 | tf_op jit(solution)/shard_map/ppermute | solution.py:737
  28.6 13.0 %collective-permute-start.9 = (bf16[1040,128]{1,0:T(8,128)(2,1)S(1)}, bf16[1040,128]{1,0:T(8,128)(2,1)S(1)}, u32[]{:S(2)}, u32[]{:S(2)}) collective-permute-start(bf16[1040,128]{1,0:T(8,128)(2,1)S(1)} %collective-permute-done.1.refs_3_), channel_id=1, source_target_pairs={{0,8},{8,16},{16,24},{1,9},{9,17},{17,25},{2,10},{10,18},{18,26},{... | collective-permute-start | bytes 798728 | tf_op jit(solution)/shard_map/ppermute | solution.py:737
  30.8 1.0 copy-start.2
  34.0 10.7 %collective-permute-start.10 = (bf16[1040,128]{1,0:T(8,128)(2,1)S(1)}, bf16[1040,128]{1,0:T(8,128)(2,1)S(1)}, u32[]{:S(2)}, u32[]{:S(2)}) collective-permute-start(bf16[1040,128]{1,0:T(8,128)(2,1)S(1)} %collective-permute-done.2.refs_4_), channel_id=1, source_target_pairs={{0,8},{8,16},{16,24},{1,9},{9,17},{17,25},{2,10},{10,18},{18,26},{... | collective-permute-start | bytes 798728 | tf_op jit(solution)/shard_map/ppermute | solution.py:737
  35.9 17.0 %collective-permute-start.5 = (bf16[2048,128]{1,0:T(8,128)(2,1)S(1)}, bf16[2048,128]{1,0:T(8,128)(2,1)S(1)}, u32[]{:S(2)}, u32[]{:S(2)}) collective-permute-start(bf16[2048,128]{1,0:T(8,128)(2,1)S(1)} %get-tuple-element.91), channel_id=1, source_target_pairs={{0,6},{2,4},{4,2},{6,0},{1,7},{3,5},{5,3},{7,1},{8,14},{10,12},{12... | collective-permute-start | bytes 1572872 | tf_op jit(solution)/shard_map/ppermute | solution.py:727
  44.7 19.1 %collective-permute-start.11 = (bf16[3120,128]{1,0:T(8,128)(2,1)S(1)}, bf16[3120,128]{1,0:T(8,128)(2,1)S(1)}, u32[]{:S(2)}, u32[]{:S(2)}) collective-permute-start(bf16[3120,128]{1,0:T(8,128)(2,1)S(1)} %constant_dynamic-update-slice_fusion.refs_1_), channel_id=1, source_target_pairs={{0,8},{8,16},{16,24},{1,9},{9,17},{17,25},{2,10},{10,18},{18,26},{... | collective-permute-start | bytes 2396168 | tf_op jit(solution)/shard_map/ppermute | solution.py:737
  66.0 1.2 %collective-permute-start.12 = (f32[8,4,128]{2,1,0:T(4,128)S(1)}, f32[8,4,128]{2,1,0:T(4,128)S(1)}, u32[]{:S(2)}, u32[]{:S(2)}) collective-permute-start(f32[8,4,128]{2,1,0:T(4,128)S(1)} %get-tuple-element.127), channel_id=1, source_target_pairs={{0,1},{1,0},{2,3},{3,2},{4,5},{5,4},{6,7},{7,6},{8,9},{9,8},{10,11... | collective-permute-start | bytes 49160 | tf_op jit(solution)/shard_map/ppermute | solution.py:746
  67.2 3.7 %collective-permute-start.13 = (f32[8,4,128]{2,1,0:T(4,128)S(1)}, f32[8,4,128]{2,1,0:T(4,128)S(1)}, u32[]{:S(2)}, u32[]{:S(2)}) collective-permute-start(f32[8,4,128]{2,1,0:T(4,128)S(1)} %add.8.refs_7_), channel_id=1, source_target_pairs={{0,2},{2,0},{4,6},{6,4},{1,3},{3,1},{5,7},{7,5},{8,10},{10,8},{12,... | collective-permute-start | bytes 49160 | tf_op jit(solution)/shard_map/ppermute | solution.py:727
  69.1 3.7 %collective-permute-start.14 = (f32[8,4,128]{2,1,0:T(4,128)S(1)}, f32[8,4,128]{2,1,0:T(4,128)S(1)}, u32[]{:S(2)}, u32[]{:S(2)}) collective-permute-start(f32[8,4,128]{2,1,0:T(4,128)S(1)} %add.8.refs_7_), channel_id=1, source_target_pairs={{0,4},{2,6},{4,0},{6,2},{1,5},{3,7},{5,1},{7,3},{8,12},{10,14},{12... | collective-permute-start | bytes 49160 | tf_op jit(solution)/shard_map/ppermute | solution.py:727
  70.3 4.6 %collective-permute-start.15 = (f32[8,4,128]{2,1,0:T(4,128)S(1)}, f32[8,4,128]{2,1,0:T(4,128)S(1)}, u32[]{:S(2)}, u32[]{:S(2)}) collective-permute-start(f32[8,4,128]{2,1,0:T(4,128)S(1)} %add.8.refs_7_), channel_id=1, source_target_pairs={{0,6},{2,4},{4,2},{6,0},{1,7},{3,5},{5,3},{7,1},{8,14},{10,12},{12... | collective-permute-start | bytes 49160 | tf_op jit(solution)/shard_map/ppermute | solution.py:727
  77.3 24.4 %collective-permute-start.19 = (bf16[2,1024,128]{2,1,0:T(8,128)(2,1)S(1)}, bf16[2,1024,128]{2,1,0:T(8,128)(2,1)S(1)}, u32[]{:S(2)}, u32[]{:S(2)}) collective-permute-start(bf16[2,1024,128]{2,1,0:T(8,128)(2,1)S(1)} %get-tuple-element.146), channel_id=1, source_target_pairs={{16,0},{24,8},{17,1},{25,9},{18,2},{26,10},{19,3},{27,11},{20,4},{... | collective-permute-start | bytes 1572872 | tf_op jit(solution)/shard_map/ppermute | solution.py:737
  82.9 30.7 %collective-permute-start.20 = (bf16[2,1024,128]{2,1,0:T(8,128)(2,1)S(1)}, bf16[2,1024,128]{2,1,0:T(8,128)(2,1)S(1)}, u32[]{:S(2)}, u32[]{:S(2)}) collective-permute-start(bf16[2,1024,128]{2,1,0:T(8,128)(2,1)S(1)} %get-tuple-element.147), channel_id=1, source_target_pairs={{8,0},{16,8},{24,16},{9,1},{17,9},{25,17},{10,2},{18,10},{26,18},{... | collective-permute-start | bytes 1572872 | tf_op jit(solution)/shard_map/ppermute | solution.py:737
  86.8 9.4 %collective-permute-start.18 = (bf16[1,4,256,128]{3,2,1,0:T(8,128)(2,1)S(1)}, bf16[1,4,256,128]{3,2,1,0:T(8,128)(2,1)S(1)}, u32[]{:S(2)}, u32[]{:S(2)}) collective-permute-start(bf16[1,4,256,128]{3,2,1,0:T(8,128)(2,1)S(1)} %bitcast.38), channel_id=1, source_target_pairs={{0,6},{2,4},{4,2},{6,0},{1,7},{3,5},{5,3},{7,1},{8,14},{10,12},{12... | collective-permute-start | bytes 786440 | tf_op jit(solution)/shard_map/ppermute | solution.py:727
  91.2 26.1 %collective-permute-start.16 = (bf16[1,4,256,128]{3,2,1,0:T(8,128)(2,1)S(1)}, bf16[1,4,256,128]{3,2,1,0:T(8,128)(2,1)S(1)}, u32[]{:S(2)}, u32[]{:S(2)}) collective-permute-start(bf16[1,4,256,128]{3,2,1,0:T(8,128)(2,1)S(1)} %bitcast.37), channel_id=1, source_target_pairs={{0,2},{2,0},{4,6},{6,4},{1,3},{3,1},{5,7},{7,5},{8,10},{10,8},{12,... | collective-permute-start | bytes 786440 | tf_op jit(solution)/shard_map/ppermute | solution.py:727
  92.7 24.6 %collective-permute-start.17 = (bf16[1,4,256,128]{3,2,1,0:T(8,128)(2,1)S(1)}, bf16[1,4,256,128]{3,2,1,0:T(8,128)(2,1)S(1)}, u32[]{:S(2)}, u32[]{:S(2)}) collective-permute-start(bf16[1,4,256,128]{3,2,1,0:T(8,128)(2,1)S(1)} %bitcast.36), channel_id=1, source_target_pairs={{0,4},{2,6},{4,0},{6,2},{1,5},{3,7},{5,1},{7,3},{8,12},{10,14},{12... | collective-permute-start | bytes 786440 | tf_op jit(solution)/shard_map/ppermute | solution.py:727
  113.7 5.1 %collective-permute-start.21 = (bf16[2,256,128]{2,1,0:T(8,128)(2,1)S(1)}, bf16[2,256,128]{2,1,0:T(8,128)(2,1)S(1)}, u32[]{:S(2)}, u32[]{:S(2)}) collective-permute-start(bf16[2,256,128]{2,1,0:T(8,128)(2,1)S(1)} %get-tuple-element.149), channel_id=1, source_target_pairs={{0,2},{2,0},{4,6},{6,4},{1,3},{3,1},{5,7},{7,5},{8,10},{10,8},{12,... | collective-permute-start | bytes 393224 | tf_op jit(solution)/shard_map/ppermute | solution.py:727
  114.6 5.3 %collective-permute-start.22 = (bf16[2,256,128]{2,1,0:T(8,128)(2,1)S(1)}, bf16[2,256,128]{2,1,0:T(8,128)(2,1)S(1)}, u32[]{:S(2)}, u32[]{:S(2)}) collective-permute-start(bf16[2,256,128]{2,1,0:T(8,128)(2,1)S(1)} %get-tuple-element.150), channel_id=1, source_target_pairs={{0,4},{2,6},{4,0},{6,2},{1,5},{3,7},{5,1},{7,3},{8,12},{10,14},{12... | collective-permute-start | bytes 393224 | tf_op jit(solution)/shard_map/ppermute | solution.py:727
  116.3 5.9 %collective-permute-start.23 = (bf16[2,256,128]{2,1,0:T(8,128)(2,1)S(1)}, bf16[2,256,128]{2,1,0:T(8,128)(2,1)S(1)}, u32[]{:S(2)}, u32[]{:S(2)}) collective-permute-start(bf16[2,256,128]{2,1,0:T(8,128)(2,1)S(1)} %get-tuple-element.151), channel_id=1, source_target_pairs={{0,6},{2,4},{4,2},{6,0},{1,7},{3,5},{5,3},{7,1},{8,14},{10,12},{12... | collective-permute-start | bytes 393224 | tf_op jit(solution)/shard_map/ppermute | solution.py:727

commit v3 on v2

--- a/solution.py
+++ b/solution.py
@@ -842,9 +842,8 @@
         held = add_arrived(held, arrived[:-1])
     dkv_pieces = exchanged(combine(sh, me, arrived[-1], held), parts)
     dkv_pieces = [p.reshape(2, 1, rows, width) for p in dkv_pieces]
-    product_queries, product_keys, product_values = join_heads(
-        [(dq_pieces, 1, group), (dkv_pieces, 2, 1)]
-    )
+    (product_queries,) = join_heads([(dq_pieces, 1, group)])
+    product_keys, product_values = join_heads([(dkv_pieces, 2, 1)])
     return (
         product_queries.reshape(queries.shape),
         product_keys.reshape(keys.shape),

time: 127 us -> 131 us (1.031); the launches traced: 125 us -> 132 us
  Pallas kernels: 39.9 us -> 59.2 us
  waiting for transfers between devices: 34.8 us -> 22.5 us
    ppermute x8, waiting for transfers between devices: 24.6 us -> 15.9 us  [moved_on(): return lax.ppermute(value, 'span', pairs)]
    pallas_call x5, Pallas kernels: 14.4 us -> 22 us  [backward_chunk(): pl.pallas_call(kernel, in_specs=[SMEM, SMEM] + [VMEM] * len(operands), ou...]
    pallas_call x2, Pallas kernels: 8.1 us -> 15.2 us  [forward_chunk(): pl.pallas_call(kernel, in_specs=[SMEM, SMEM] + [VMEM] * len(operands), ou...]
    ppermute x15, waiting for transfers between devices: 9.05 us -> 5.45 us  [exchanged_with(): lax.ppermute(piece, 'part', [(i, i ^ m) for i in range(parts)])]
    pallas_call x3, Pallas kernels: 9.26 us -> 12.6 us  [forward_own(): pl.pallas_call(kernel, in_specs=[SMEM, SMEM] + [VMEM] * len(operands), ou...]
    pallas_call x1 -> x2, Pallas kernels: 2.73 us -> 4.07 us  [join_heads(): pl.pallas_call(kernel, grid=(steps,), in_specs=in_specs, out_specs=out_sp...]
  transfers between devices with their start and end apart: 24 -> 24, of which waited for: 13 -> 11; matrix products, arithmetic and copies ran while one was open for 2% -> 2% of each run, Pallas kernels for 24% -> 38%
where the time goes in v3:
time: 131 us; the launch traced here: 132 us
  Pallas kernels  59.2 us (45%)
  starting transfers between devices  43.5 us (33%)
  waiting for transfers between devices  22.5 us (17%)
  local copies, waits for them, and re-layouts  4.95 us (4%)
    ppermute x15, starting transfers between devices, exchanged_with(): lax.ppermute(piece, 'part', [(i, i ^ m) for i in range(parts)])  22.3 us
    pallas_call x5, Pallas kernels, backward_chunk(): pl.pallas_call(kernel, in_specs=[SMEM, SMEM] + [VMEM] * len(operands), ou...  22 us
    ppermute x8, starting transfers between devices, moved_on(): return lax.ppermute(value, 'span', pairs)  21.1 us
    ppermute x8, waiting for transfers between devices, moved_on(): return lax.ppermute(value, 'span', pairs)  15.9 us
    pallas_call x2, Pallas kernels, forward_chunk(): pl.pallas_call(kernel, in_specs=[SMEM, SMEM] + [VMEM] * len(operands), ou...  15.2 us
    pallas_call x3, Pallas kernels, forward_own(): pl.pallas_call(kernel, in_specs=[SMEM, SMEM] + [VMEM] * len(operands), ou...  12.6 us
    ppermute x15, waiting for transfers between devices, exchanged_with(): lax.ppermute(piece, 'part', [(i, i ^ m) for i in range(parts)])  5.45 us
    pallas_call x2, Pallas kernels, split_heads(): pl.pallas_call(kernel, in_specs=[SMEM] * len(scalars) + [pl.BlockSpec(mem...  5.1 us
  transfers between devices with their start and end apart: 24, of which 11 were waited for; matrix products, arithmetic and copies ran while one was open for 2% of the time, Pallas kernels for 38%

profile of v3, /device:TPU:8, one launch (start us, length us, event | category | flops | bytes accessed | tf_op | source)
XLA Modules:
  0.0 131.9 jit_solution(13105441081160383679)
XLA Ops:
  0.6 2.9 %split_heads.2 = (bf16[1040,128]{1,0:T(8,128)(2,1)}, bf16[1040,128]{1,0:T(8,128)(2,1)}, bf16[1040,128]{1,0:T(8,128)(2,1)}, bf16[1040,128]{1,0:T(8,128)(2,1)}) custom-call(s32[2]{0:T(128)} %refs_0_.1, bf16[1024,128]{1,0:T(8,128)(2,1)} %bitcast.41, bf16[1024,128]{1,0:T(8,128)(2,1)} %bitcast.42, bf16[1024,128]{1,0:T(8,128)(2,1)} %bitcast.43, ...), custom_call_target="tpu_custom_call" | custom-call | bytes 2097152 | tf_op jit(solution)/shard_map/split_heads/pallas_call | solution.py:99
  3.6 3.5 %collective-permute-start.3 = (bf16[1040,128]{1,0:T(8,128)(2,1)}, bf16[1040,128]{1,0:T(8,128)(2,1)S(1)}, u32[]{:S(2)}, u32[]{:S(2)}) collective-permute-start(bf16[1040,128]{1,0:T(8,128)(2,1)} %get-tuple-element.78.refs_1_), channel_id=1, source_target_pairs={{0,8},{8,16},{16,24},{1,9},{9,17},{17,25},{2,10},{10,18},{18,26},{... | collective-permute-start | bytes 798728 | tf_op jit(solution)/shard_map/ppermute | solution.py:737
  7.0 2.5 %collective-permute-start.2 = (bf16[1040,128]{1,0:T(8,128)(2,1)}, bf16[1040,128]{1,0:T(8,128)(2,1)S(1)}, u32[]{:S(2)}, u32[]{:S(2)}) collective-permute-start(bf16[1040,128]{1,0:T(8,128)(2,1)} %get-tuple-element.81), channel_id=1, source_target_pairs={{0,6},{2,4},{4,2},{6,0},{1,7},{3,5},{5,3},{7,1},{8,14},{10,12},{12... | collective-permute-start | bytes 798728 | tf_op jit(solution)/shard_map/ppermute | solution.py:727
  9.6 0.5 collective-permute-start.1
  10.1 0.5 collective-permute-start
  10.6 0.8 slice_reduce_fusion.3
  11.4 1.2 copy-done
  12.6 1.2 copy-done.1
  13.9 2.2 %split_heads.3 = (bf16[2048,128]{1,0:T(8,128)(2,1)S(1)}, bf16[2048,128]{1,0:T(8,128)(2,1)S(1)}, bf16[2048,128]{1,0:T(8,128)(2,1)S(1)}, bf16[2048,128]{1,0:T(8,128)(2,1)S(1)}) custom-call(bf16[4096,128]{1,0:T(8,128)(2,1)S(1)} %bitcast.27, bf16[4096,128]{1,0:T(8,128)(2,1)S(1)} %bitcast.28), custom_call_target="tpu_custom_call" | custom-call | bytes 4194304 | tf_op jit(solution)/shard_map/split_heads/pallas_call | solution.py:99
  16.0 0.0 collective-permute-done.3.refs_0_
  16.1 3.5 %collective-permute-start.7 = (bf16[1040,128]{1,0:T(8,128)(2,1)S(1)}, bf16[1040,128]{1,0:T(8,128)(2,1)S(1)}, u32[]{:S(2)}, u32[]{:S(2)}) collective-permute-start(bf16[1040,128]{1,0:T(8,128)(2,1)S(1)} %collective-permute-done.3.refs_0_), channel_id=1, source_target_pairs={{0,8},{8,16},{16,24},{1,9},{9,17},{17,25},{2,10},{10,18},{18,26},{... | collective-permute-start | bytes 798728 | tf_op jit(solution)/shard_map/ppermute | solution.py:737
  19.5 0.7 multiply_bitcast_fusion
  20.2 0.1 copy.29
  20.4 0.2 broadcast_in_dim.3
  20.6 1.6 %collective-permute-start.4 = (bf16[2048,128]{1,0:T(8,128)(2,1)S(1)}, bf16[2048,128]{1,0:T(8,128)(2,1)S(1)}, u32[]{:S(2)}, u32[]{:S(2)}) collective-permute-start(bf16[2048,128]{1,0:T(8,128)(2,1)S(1)} %get-tuple-element.89), channel_id=1, source_target_pairs={{0,2},{2,0},{4,6},{6,4},{1,3},{3,1},{5,7},{7,5},{8,10},{10,8},{12,... | collective-permute-start | bytes 1572872 | tf_op jit(solution)/shard_map/ppermute | solution.py:727
  22.1 1.5 %collective-permute-start.6 = (bf16[2048,128]{1,0:T(8,128)(2,1)S(1)}, bf16[2048,128]{1,0:T(8,128)(2,1)S(1)}, u32[]{:S(2)}, u32[]{:S(2)}) collective-permute-start(bf16[2048,128]{1,0:T(8,128)(2,1)S(1)} %get-tuple-element.97), channel_id=1, source_target_pairs={{0,4},{2,6},{4,0},{6,2},{1,5},{3,7},{5,1},{7,3},{8,12},{10,14},{12... | collective-permute-start | bytes 1572872 | tf_op jit(solution)/shard_map/ppermute | solution.py:727
  23.7 0.1 slice_reduce_fusion
  23.8 0.0 collective-permute-done.1.refs_3_
  23.8 0.1 slice_reduce_fusion.1
  23.9 1.1 collective-permute-done.7.refs_0_
  25.0 3.5 %collective-permute-start.8 = (bf16[1040,128]{1,0:T(8,128)(2,1)S(1)}, bf16[1040,128]{1,0:T(8,128)(2,1)S(1)}, u32[]{:S(2)}, u32[]{:S(2)}) collective-permute-start(bf16[1040,128]{1,0:T(8,128)(2,1)S(1)} %collective-permute-done.refs_2_), channel_id=1, source_target_pairs={{0,8},{8,16},{16,24},{1,9},{9,17},{17,25},{2,10},{10,18},{18,26},{... | collective-permute-start | bytes 798728 | tf_op jit(solution)/shard_map/ppermute | solution.py:737
  28.4 0.1 slice_reduce_fusion.2
  28.6 0.1 maximum_convert_fusion.back_ref
  28.6 2.2 %collective-permute-start.9 = (bf16[1040,128]{1,0:T(8,128)(2,1)S(1)}, bf16[1040,128]{1,0:T(8,128)(2,1)S(1)}, u32[]{:S(2)}, u32[]{:S(2)}) collective-permute-start(bf16[1040,128]{1,0:T(8,128)(2,1)S(1)} %collective-permute-done.1.refs_3_), channel_id=1, source_target_pairs={{0,8},{8,16},{16,24},{1,9},{9,17},{17,25},{2,10},{10,18},{18,26},{... | collective-permute-start | bytes 798728 | tf_op jit(solution)/shard_map/ppermute | solution.py:737
  30.8 0.0 copy-start.2
  30.9 0.9 copy-done.2
  31.8 2.2 %forward_own.3 = (f32[8,256,512]{2,1,0:T(8,128)S(1)}, f32[8,8,512]{2,1,0:T(8,128)S(1)}, bf16[8,512,256]{2,1,0:T(8,128)(2,1)S(1)}, bf16[8,1024,512]{2,1,0:T(8,128...) custom-call(s32[1]{0:T(128)} %bitcast.me_ref, ...), custom_call_target="tpu_custom_call" | custom-call | flops 805306368 | bytes 2097152 | tf_op jit(solution)/shard_map/forward_own/pallas_call | solution.py:430
  34.0 1.9 %collective-permute-start.10 = (bf16[1040,128]{1,0:T(8,128)(2,1)S(1)}, bf16[1040,128]{1,0:T(8,128)(2,1)S(1)}, u32[]{:S(2)}, u32[]{:S(2)}) collective-permute-start(bf16[1040,128]{1,0:T(8,128)(2,1)S(1)} %collective-permute-done.2.refs_4_), channel_id=1, source_target_pairs={{0,8},{8,16},{16,24},{1,9},{9,17},{17,25},{2,10},{10,18},{18,26},{... | collective-permute-start | bytes 798728 | tf_op jit(solution)/shard_map/ppermute | solution.py:737
  35.9 5.1 %collective-permute-start.5 = (bf16[2048,128]{1,0:T(8,128)(2,1)S(1)}, bf16[2048,128]{1,0:T(8,128)(2,1)S(1)}, u32[]{:S(2)}, u32[]{:S(2)}) collective-permute-start(bf16[2048,128]{1,0:T(8,128)(2,1)S(1)} %get-tuple-element.90), channel_id=1, source_target_pairs={{0,6},{2,4},{4,2},{6,0},{1,7},{3,5},{5,3},{7,1},{8,14},{10,12},{12... | collective-permute-start | bytes 1572872 | tf_op jit(solution)/shard_map/ppermute | solution.py:727
  41.0 0.6 collective-permute-done.9
  41.6 3.0 %collective-permute-done.10 = bf16[1040,128]{1,0:T(8,128)(2,1)S(1)} collective-permute-done((bf16[1040,128]{1,0:T(8,128)(2,1)S(1)}, bf16[1040,128]{1,0:T(8,128)(2,1)S(1)}, u32[]{:S(2)}, u32[]{:S(2)}) %collective-permute-start.10) | collective-permute-done | bytes 266272 | tf_op jit(solution)/shard_map/ppermute | solution.py:737
  44.7 3.3 %collective-permute-start.11 = (bf16[3120,128]{1,0:T(8,128)(2,1)S(1)}, bf16[3120,128]{1,0:T(8,128)(2,1)S(1)}, u32[]{:S(2)}, u32[]{:S(2)}) collective-permute-start(bf16[3120,128]{1,0:T(8,128)(2,1)S(1)} %constant_dynamic-update-slice_fusion.refs_1_), channel_id=1, source_target_pairs={{0,8},{8,16},{16,24},{1,9},{9,17},{17,25},{2,10},{10,18},{18,26},{... | collective-permute-start | bytes 2396168 | tf_op jit(solution)/shard_map/ppermute | solution.py:737
  48.1 5.9 %forward_own.4 = (f32[8,256,512]{2,1,0:T(8,128)S(1)}, f32[8,8,512]{2,1,0:T(8,128)S(1)}, bf16[8,512,256]{2,1,0:T(8,128)(2,1)S(1)}, bf16[8,1024,512]{2,1,0:T(8,128)(2,1)S(1)}, f32[8,8,1,512]{3,2,1,0:T(1,128)S(1)}) custom-call(s32[1]{0:T(128)} %bitcast.me_ref, ...), custom_call_target="tpu_custom_call", output_to_operand_aliasing={{0}: (9, {}), {1}: (10, {}), {2}: (11, {}), {3}: (12, {}), ... | custom-call | flops 1610612736 | bytes 2097152 | tf_op jit(solution)/shard_map/forward_own/pallas_call | solution.py:430
  54.0 4.5 %forward_own.5 = (f32[8,256,512]{2,1,0:T(8,128)S(1)}, f32[8,8,512]{2,1,0:T(8,128)S(1)}, bf16[8,512,256]{2,1,0:T(8,128)(2,1)S(1)}, bf16[8,1024,512]{2,1,0:T(8,128)(2,1)S(1)}, f32[8,8,1,512]{3,2,1,0:T(1,128)S(1)}) custom-call(s32[1]{0:T(128)} %bitcast.me_ref, ...), custom_call_target="tpu_custom_call", output_to_operand_aliasing={{0}: (8, {}), {1}: (9, {}), {2}: (10, {}), {3}: (11, {}), {... | custom-call | flops 805306368 | bytes 2097152 | tf_op jit(solution)/shard_map/forward_own/pallas_call | solution.py:430
  58.5 13.0 %forward_chunk.1 = (bf16[1024,128]{1,0:T(8,128)(2,1)S(1)}, bf16[1024,128]{1,0:T(8,128)(2,1)S(1)}, bf16[128,1024]{1,0:T(8,128)(2,1)S(1)}, f32[8,256,512]{2,1,0:T(...) custom-call(s32[1]{0:T(128)} %bitcast.me_ref, ...), custom_call_target="tpu_custom_call", output_to_operand_aliasing={{3}: (5, {}), {4}: (6, {})} | custom-call | flops 6442450944 | bytes 12582912 | tf_op jit(solution)/shard_map/forward_chunk/pallas_call | solution.py:518
  71.5 2.2 %forward_far.1 = (bf16[1024,128]{1,0:T(8,128)(2,1)S(1)}, bf16[1024,128]{1,0:T(8,128)(2,1)S(1)}, bf16[128,1024]{1,0:T(8,128)(2,1)S(1)}, f32[8,256,512]{2,1,0:T(8,...) custom-call(s32[1]{0:T(128)} %bitcast.me_ref, ...), custom_call_target="tpu_custom_call", output_to_operand_aliasing={{3}: (5, {}), {4}: (6, {})} | custom-call | flops 6442450944 | bytes 12582912 | tf_op jit(solution)/shard_map/forward_far/pallas_call | solution.py:518
  73.7 0.1 collective-permute-start.12
  73.8 1.2 collective-permute-done.12
  75.0 0.8 collective-permute-start.13
  75.8 2.7 %collective-permute-start.15 = (f32[8,4,128]{2,1,0:T(4,128)S(1)}, f32[8,4,128]{2,1,0:T(4,128)S(1)}, u32[]{:S(2)}, u32[]{:S(2)}) collective-permute-start(f32[8,4,128]{2,1,0:T(4,128)S(1)} %add.8.refs_7_), channel_id=1, source_target_pairs={{0,6},{2,4},{4,2},{6,0},{1,7},{3,5},{5,3},{7,1},{8,14},{10,12},{12... | collective-permute-start | bytes 49160 | tf_op jit(solution)/shard_map/ppermute | solution.py:727
  78.5 0.2 collective-permute-done.13.refs_8_
  78.7 0.8 collective-permute-done.14.refs_9_
  79.5 0.9 collective-permute-done.15.refs_10_
  80.4 2.4 %backward_chunk.5 = (bf16[2,1024,128]{2,1,0:T(8,128)(2,1)S(1)}, f32[8,128,512]{2,1,0:T(8,128)S(1)}, bf16[8,512,128]{2,1,0:T(8,128)(2,1)S(1)}, f32[8,1,512]{2,1,0:T(1,128)S(1)}) custom-call(s32[1]{0:T(128)} %bitcast.me_ref, s32[8]{0:T(128)S(1)} %maximum_convert_fusion.back_ref, bf16[8,512,256]{2,1,0:T(8,128)(2,1)S(1)} %get-tuple-element.108.qq_s.refs_0_, ...), custom_call_target="tpu_custom_call" | custom-call | flops 5368709120 | bytes 33554432 | tf_op jit(solution)/shard_map/backward_chunk/pallas_call | solution.py:674
  82.8 1.3 collective-permute-start.19
  84.1 9.6 %backward_chunk.6 = (bf16[2,1024,128]{2,1,0:T(8,128)(2,1)S(1)}, f32[8,128,512]{2,1,0:T(8,128)S(1)}) custom-call(s32[1]{0:T(128)} %bitcast.me_ref, s32[8]{0:T(128)S(1)} %maximum_convert_fusion.back_ref, bf16[8,512,256]{2,1,0:T(8,128)(2,1)S(1)} %get-tuple-element.108.qq_s.refs_0_, ...), custom_call_target="tpu_custom_call", output_to_operand_aliasing={{1}: (11, {})} | custom-call | flops 5368709120 | bytes 33554432 | tf_op jit(solution)/shard_map/backward_chunk/pallas_call | solution.py:674
  93.7 1.9 %collective-permute-start.20 = (bf16[2,1024,128]{2,1,0:T(8,128)(2,1)S(1)}, bf16[2,1024,128]{2,1,0:T(8,128)(2,1)S(1)}, u32[]{:S(2)}, u32[]{:S(2)}) collective-permute-start(bf16[2,1024,128]{2,1,0:T(8,128)(2,1)S(1)} %get-tuple-element.146), channel_id=1, source_target_pairs={{8,0},{16,8},{24,16},{9,1},{17,9},{25,17},{10,2},{18,10},{26,18},{... | collective-permute-start | bytes 1572872 | tf_op jit(solution)/shard_map/ppermute | solution.py:737
  95.6 3.5 %backward_chunk.7 = (f32[2,1024,128]{2,1,0:T(8,128)S(1)}, bf16[4,256,128]{2,1,0:T(8,128)(2,1)S(1)}) custom-call(s32[1]{0:T(128)} %bitcast.me_ref, s32[8]{0:T(128)S(1)} %maximum_convert_fusion.back_ref, bf16[8,512,256]{2,1,0:T(8,128)(2,1)S(1)} %get-tuple-element.108.qq_s.refs_0_, bf16[1024,128]{1,0:T(8,128)(2,1)S(1)} %get-tuple-element.92.refs_2_.refs_1_, ...), custom_call_target="tpu_custom_call" | custom-call | flops 1 | bytes 1 | tf_op jit(solution)/shard_map/backward_chunk/pallas_call | solution.py:674
  99.2 1.0 collective-permute-start.18
  100.2 4.7 %backward_chunk.8 = (f32[2,1024,128]{2,1,0:T(8,128)S(1)}, bf16[4,256,128]{2,1,0:T(8,128)(2,1)S(1)}, bf16[4,256,128]{2,1,0:T(8,128)(2,1)S(1)}) custom-call(s32[1]{0:T(128)} %bitcast.me_ref, s32[8]{0:T(128)S(1)} %maximum_convert_fusion.back_ref, bf16[8,512,256]{2,1,0:T(8,128)(2,1)S(1)} %get-tuple-element.108.qq_s.refs_0_, ...), custom_call_target="tpu_custom_call", output_to_operand_aliasing={{0}: (12, {})} | custom-call | flops 1 | bytes 1 | tf_op jit(solution)/shard_map/backward_chunk/pallas_call | solution.py:674
  104.9 1.3 collective-permute-start.16
  106.2 1.4 %collective-permute-start.17 = (bf16[1,4,256,128]{3,2,1,0:T(8,128)(2,1)S(1)}, bf16[1,4,256,128]{3,2,1,0:T(8,128)(2,1)S(1)}, u32[]{:S(2)}, u32[]{:S(2)}) collective-permute-start(bf16[1,4,256,128]{3,2,1,0:T(8,128)(2,1)S(1)} %bitcast.36), channel_id=1, source_target_pairs={{0,4},{2,6},{4,0},{6,2},{1,5},{3,7},{5,1},{7,3},{8,12},{10,14},{12... | collective-permute-start | bytes 786440 | tf_op jit(solution)/shard_map/ppermute | solution.py:727
  107.5 1.7 %backward_chunk.9 = (f32[2,1024,128]{2,1,0:T(8,128)S(1)}, bf16[4,256,128]{2,1,0:T(8,128)(2,1)S(1)}) custom-call(s32[1]{0:T(128)} %bitcast.me_ref, s32[8]{0:T(128)S(1)} %maximum_convert_fusion.back_ref, bf16[8,512,256]{2,1,0:T(8,128)(2,1)S(1)} %get-tuple-element.108.qq_s.refs_0_, ...), custom_call_target="tpu_custom_call", output_to_operand_aliasing={{0}: (12, {})} | custom-call | flops 1 | bytes 1 | tf_op jit(solution)/shard_map/backward_chunk/pallas_call | solution.py:674
  109.3 0.2 add_arrived.1.held_ref
  109.5 11.1 %collective-permute-done.20.arrived_ref = bf16[2,1024,128]{2,1,0:T(8,128)(2,1)S(1)} collective-permute-done((bf16[2,1024,128]{2,1,0:T(8,128)(2,1)S(1)}, bf16[2,1024,128]{2,1,0:T(8,128)(2,1)S(1)}, u32[]{:S(2)}, u32[]{:S(2)}) %collective-permute-start.20) | collective-permute-done | bytes 524320 | tf_op jit(solution)/shard_map/ppermute | solution.py:737
  120.7 0.1 combine.1
  120.8 1.3 collective-permute-start.21
  122.0 1.1 collective-permute-start.22
  123.1 1.2 collective-permute-start.23
  124.3 2.5 %join_heads.2 = f32[4096,128]{1,0:T(8,128)} custom-call(bf16[1,4,256,128]{3,2,1,0:T(8,128)(2,1)S(1)} %bitcast.29, bf16[1,4,256,128]{3,2,1,0:T(8,128)(2,1)S(1)} %collective-permute-done.16.refs_1_, bf16[1,4,256,128]{3,2,1,0:T(8,128)(2,1)S(1)} %collective-permute-done.17.refs_2_, bf16[1,4,256,128]{3,2,1,0:T(8,128)(2,1)S(1)} %collective-permute-done.18.refs_3_), custom_call_target="tpu_custom_call" | custom-call | bytes 3145728 | tf_op jit(solution)/shard_map/join_heads/pallas_call | solution.py:136
  126.8 0.1 collective-permute-done.21
  126.9 1.5 %collective-permute-done.22 = bf16[2,256,128]{2,1,0:T(8,128)(2,1)S(1)} collective-permute-done((bf16[2,256,128]{2,1,0:T(8,128)(2,1)S(1)}, bf16[2,256,128]{2,1,0:T(8,128)(2,1)S(1)}, u32[]{:S(2)}, u32[]{:S(2)}) %collective-permute-start.22) | collective-permute-done | bytes 131104 | tf_op jit(solution)/shard_map/ppermute | solution.py:727
  128.5 1.8 %collective-permute-done.23 = bf16[2,256,128]{2,1,0:T(8,128)(2,1)S(1)} collective-permute-done((bf16[2,256,128]{2,1,0:T(8,128)(2,1)S(1)}, bf16[2,256,128]{2,1,0:T(8,128)(2,1)S(1)}, u32[]{:S(2)}, u32[]{:S(2)}) %collective-permute-start.23) | collective-permute-done | bytes 131104 | tf_op jit(solution)/shard_map/ppermute | solution.py:727
  130.2 1.6 %join_heads.3 = (f32[1024,128]{1,0:T(8,128)}, f32[1024,128]{1,0:T(8,128)}) custom-call(bf16[2,1,256,128]{3,2,1,0:T(8,128)(2,1)S(1)} %bitcast.32, bf16[2,1,256,128]{3,2,1,0:T(8,128)(2,1)S(1)} %bitcast.33, bf16[2,1,256,128]{3,2,1,0:T(8,128)(2,1)S(1)} %bitcast.34, bf16[2,1,256,128]{3,2,1,0:T(8,128)(2,1)S(1)} %bitcast.35), custom_call_target="tpu_custom_call" | custom-call | bytes 1572864 | tf_op jit(solution)/shard_map/join_heads/pallas_call | solution.py:136
  (19 shorter events, 0.1 us)
Async XLA Ops:
  3.6 12.5 %collective-permute-start.3 = (bf16[1040,128]{1,0:T(8,128)(2,1)}, bf16[1040,128]{1,0:T(8,128)(2,1)S(1)}, u32[]{:S(2)}, u32[]{:S(2)}) collective-permute-start(bf16[1040,128]{1,0:T(8,128)(2,1)} %get-tuple-element.78.refs_1_), channel_id=1, source_target_pairs={{0,8},{8,16},{16,24},{1,9},{9,17},{17,25},{2,10},{10,18},{18,26},{... | collective-permute-start | bytes 798728 | tf_op jit(solution)/shard_map/ppermute | solution.py:737
  7.0 15.1 %collective-permute-start.2 = (bf16[1040,128]{1,0:T(8,128)(2,1)}, bf16[1040,128]{1,0:T(8,128)(2,1)S(1)}, u32[]{:S(2)}, u32[]{:S(2)}) collective-permute-start(bf16[1040,128]{1,0:T(8,128)(2,1)} %get-tuple-element.81), channel_id=1, source_target_pairs={{0,6},{2,4},{4,2},{6,0},{1,7},{3,5},{5,3},{7,1},{8,14},{10,12},{12... | collective-permute-start | bytes 798728 | tf_op jit(solution)/shard_map/ppermute | solution.py:727
  9.6 14.2 %collective-permute-start.1 = (bf16[1040,128]{1,0:T(8,128)(2,1)}, bf16[1040,128]{1,0:T(8,128)(2,1)S(1)}, u32[]{:S(2)}, u32[]{:S(2)}) collective-permute-start(bf16[1040,128]{1,0:T(8,128)(2,1)} %get-tuple-element.80), channel_id=1, source_target_pairs={{0,4},{2,6},{4,0},{6,2},{1,5},{3,7},{5,1},{7,3},{8,12},{10,14},{12... | collective-permute-start | bytes 798728 | tf_op jit(solution)/shard_map/ppermute | solution.py:727
  10.1 13.8 %collective-permute-start = (bf16[1040,128]{1,0:T(8,128)(2,1)}, bf16[1040,128]{1,0:T(8,128)(2,1)S(1)}, u32[]{:S(2)}, u32[]{:S(2)}) collective-permute-start(bf16[1040,128]{1,0:T(8,128)(2,1)} %get-tuple-element.79), channel_id=1, source_target_pairs={{0,2},{2,0},{4,6},{6,4},{1,3},{3,1},{5,7},{7,5},{8,10},{10,8},{12,... | collective-permute-start | bytes 798728 | tf_op jit(solution)/shard_map/ppermute | solution.py:727
  11.4 1.2 copy-start
  12.6 1.2 copy-start.1
  16.1 8.9 %collective-permute-start.7 = (bf16[1040,128]{1,0:T(8,128)(2,1)S(1)}, bf16[1040,128]{1,0:T(8,128)(2,1)S(1)}, u32[]{:S(2)}, u32[]{:S(2)}) collective-permute-start(bf16[1040,128]{1,0:T(8,128)(2,1)S(1)} %collective-permute-done.3.refs_0_), channel_id=1, source_target_pairs={{0,8},{8,16},{16,24},{1,9},{9,17},{17,25},{2,10},{10,18},{18,26},{... | collective-permute-start | bytes 798728 | tf_op jit(solution)/shard_map/ppermute | solution.py:737
  20.6 15.3 %collective-permute-start.4 = (bf16[2048,128]{1,0:T(8,128)(2,1)S(1)}, bf16[2048,128]{1,0:T(8,128)(2,1)S(1)}, u32[]{:S(2)}, u32[]{:S(2)}) collective-permute-start(bf16[2048,128]{1,0:T(8,128)(2,1)S(1)} %get-tuple-element.89), channel_id=1, source_target_pairs={{0,2},{2,0},{4,6},{6,4},{1,3},{3,1},{5,7},{7,5},{8,10},{10,8},{12,... | collective-permute-start | bytes 1572872 | tf_op jit(solution)/shard_map/ppermute | solution.py:727
  22.1 25.9 %collective-permute-start.6 = (bf16[2048,128]{1,0:T(8,128)(2,1)S(1)}, bf16[2048,128]{1,0:T(8,128)(2,1)S(1)}, u32[]{:S(2)}, u32[]{:S(2)}) collective-permute-start(bf16[2048,128]{1,0:T(8,128)(2,1)S(1)} %get-tuple-element.97), channel_id=1, source_target_pairs={{0,4},{2,6},{4,0},{6,2},{1,5},{3,7},{5,1},{7,3},{8,12},{10,14},{12... | collective-permute-start | bytes 1572872 | tf_op jit(solution)/shard_map/ppermute | solution.py:727
  25.0 16.0 %collective-permute-start.8 = (bf16[1040,128]{1,0:T(8,128)(2,1)S(1)}, bf16[1040,128]{1,0:T(8,128)(2,1)S(1)}, u32[]{:S(2)}, u32[]{:S(2)}) collective-permute-start(bf16[1040,128]{1,0:T(8,128)(2,1)S(1)} %collective-permute-done.refs_2_), channel_id=1, source_target_pairs={{0,8},{8,16},{16,24},{1,9},{9,17},{17,25},{2,10},{10,18},{18,26},{... | collective-permute-start | bytes 798728 | tf_op jit(solution)/shard_map/ppermute | solution.py:737
  28.6 13.0 %collective-permute-start.9 = (bf16[1040,128]{1,0:T(8,128)(2,1)S(1)}, bf16[1040,128]{1,0:T(8,128)(2,1)S(1)}, u32[]{:S(2)}, u32[]{:S(2)}) collective-permute-start(bf16[1040,128]{1,0:T(8,128)(2,1)S(1)} %collective-permute-done.1.refs_3_), channel_id=1, source_target_pairs={{0,8},{8,16},{16,24},{1,9},{9,17},{17,25},{2,10},{10,18},{18,26},{... | collective-permute-start | bytes 798728 | tf_op jit(solution)/shard_map/ppermute | solution.py:737
  30.8 1.0 copy-start.2
  34.0 10.7 %collective-permute-start.10 = (bf16[1040,128]{1,0:T(8,128)(2,1)S(1)}, bf16[1040,128]{1,0:T(8,128)(2,1)S(1)}, u32[]{:S(2)}, u32[]{:S(2)}) collective-permute-start(bf16[1040,128]{1,0:T(8,128)(2,1)S(1)} %collective-permute-done.2.refs_4_), channel_id=1, source_target_pairs={{0,8},{8,16},{16,24},{1,9},{9,17},{17,25},{2,10},{10,18},{18,26},{... | collective-permute-start | bytes 798728 | tf_op jit(solution)/shard_map/ppermute | solution.py:737
  35.9 18.1 %collective-permute-start.5 = (bf16[2048,128]{1,0:T(8,128)(2,1)S(1)}, bf16[2048,128]{1,0:T(8,128)(2,1)S(1)}, u32[]{:S(2)}, u32[]{:S(2)}) collective-permute-start(bf16[2048,128]{1,0:T(8,128)(2,1)S(1)} %get-tuple-element.90), channel_id=1, source_target_pairs={{0,6},{2,4},{4,2},{6,0},{1,7},{3,5},{5,3},{7,1},{8,14},{10,12},{12... | collective-permute-start | bytes 1572872 | tf_op jit(solution)/shard_map/ppermute | solution.py:727
  44.7 26.8 %collective-permute-start.11 = (bf16[3120,128]{1,0:T(8,128)(2,1)S(1)}, bf16[3120,128]{1,0:T(8,128)(2,1)S(1)}, u32[]{:S(2)}, u32[]{:S(2)}) collective-permute-start(bf16[3120,128]{1,0:T(8,128)(2,1)S(1)} %constant_dynamic-update-slice_fusion.refs_1_), channel_id=1, source_target_pairs={{0,8},{8,16},{16,24},{1,9},{9,17},{17,25},{2,10},{10,18},{18,26},{... | collective-permute-start | bytes 2396168 | tf_op jit(solution)/shard_map/ppermute | solution.py:737
  73.7 1.2 collective-permute-start.12
  75.0 3.7 %collective-permute-start.13 = (f32[8,4,128]{2,1,0:T(4,128)S(1)}, f32[8,4,128]{2,1,0:T(4,128)S(1)}, u32[]{:S(2)}, u32[]{:S(2)}) collective-permute-start(f32[8,4,128]{2,1,0:T(4,128)S(1)} %add.8.refs_7_), channel_id=1, source_target_pairs={{0,2},{2,0},{4,6},{6,4},{1,3},{3,1},{5,7},{7,5},{8,10},{10,8},{12,... | collective-permute-start | bytes 49160 | tf_op jit(solution)/shard_map/ppermute | solution.py:727
  75.8 3.7 %collective-permute-start.14 = (f32[8,4,128]{2,1,0:T(4,128)S(1)}, f32[8,4,128]{2,1,0:T(4,128)S(1)}, u32[]{:S(2)}, u32[]{:S(2)}) collective-permute-start(f32[8,4,128]{2,1,0:T(4,128)S(1)} %add.8.refs_7_), channel_id=1, source_target_pairs={{0,4},{2,6},{4,0},{6,2},{1,5},{3,7},{5,1},{7,3},{8,12},{10,14},{12... | collective-permute-start | bytes 49160 | tf_op jit(solution)/shard_map/ppermute | solution.py:727
  75.8 4.6 %collective-permute-start.15 = (f32[8,4,128]{2,1,0:T(4,128)S(1)}, f32[8,4,128]{2,1,0:T(4,128)S(1)}, u32[]{:S(2)}, u32[]{:S(2)}) collective-permute-start(f32[8,4,128]{2,1,0:T(4,128)S(1)} %add.8.refs_7_), channel_id=1, source_target_pairs={{0,6},{2,4},{4,2},{6,0},{1,7},{3,5},{5,3},{7,1},{8,14},{10,12},{12... | collective-permute-start | bytes 49160 | tf_op jit(solution)/shard_map/ppermute | solution.py:727
  82.8 26.5 %collective-permute-start.19 = (bf16[2,1024,128]{2,1,0:T(8,128)(2,1)S(1)}, bf16[2,1024,128]{2,1,0:T(8,128)(2,1)S(1)}, u32[]{:S(2)}, u32[]{:S(2)}) collective-permute-start(bf16[2,1024,128]{2,1,0:T(8,128)(2,1)S(1)} %get-tuple-element.145), channel_id=1, source_target_pairs={{16,0},{24,8},{17,1},{25,9},{18,2},{26,10},{19,3},{27,11},{20,4},{... | collective-permute-start | bytes 1572872 | tf_op jit(solution)/shard_map/ppermute | solution.py:737
  93.7 26.9 %collective-permute-start.20 = (bf16[2,1024,128]{2,1,0:T(8,128)(2,1)S(1)}, bf16[2,1024,128]{2,1,0:T(8,128)(2,1)S(1)}, u32[]{:S(2)}, u32[]{:S(2)}) collective-permute-start(bf16[2,1024,128]{2,1,0:T(8,128)(2,1)S(1)} %get-tuple-element.146), channel_id=1, source_target_pairs={{8,0},{16,8},{24,16},{9,1},{17,9},{25,17},{10,2},{18,10},{26,18},{... | collective-permute-start | bytes 1572872 | tf_op jit(solution)/shard_map/ppermute | solution.py:737
  99.2 10.1 %collective-permute-start.18 = (bf16[1,4,256,128]{3,2,1,0:T(8,128)(2,1)S(1)}, bf16[1,4,256,128]{3,2,1,0:T(8,128)(2,1)S(1)}, u32[]{:S(2)}, u32[]{:S(2)}) collective-permute-start(bf16[1,4,256,128]{3,2,1,0:T(8,128)(2,1)S(1)} %bitcast.38), channel_id=1, source_target_pairs={{0,6},{2,4},{4,2},{6,0},{1,7},{3,5},{5,3},{7,1},{8,14},{10,12},{12... | collective-permute-start | bytes 786440 | tf_op jit(solution)/shard_map/ppermute | solution.py:727
  104.9 19.4 %collective-permute-start.16 = (bf16[1,4,256,128]{3,2,1,0:T(8,128)(2,1)S(1)}, bf16[1,4,256,128]{3,2,1,0:T(8,128)(2,1)S(1)}, u32[]{:S(2)}, u32[]{:S(2)}) collective-permute-start(bf16[1,4,256,128]{3,2,1,0:T(8,128)(2,1)S(1)} %bitcast.37), channel_id=1, source_target_pairs={{0,2},{2,0},{4,6},{6,4},{1,3},{3,1},{5,7},{7,5},{8,10},{10,8},{12,... | collective-permute-start | bytes 786440 | tf_op jit(solution)/shard_map/ppermute | solution.py:727
  106.2 18.2 %collective-permute-start.17 = (bf16[1,4,256,128]{3,2,1,0:T(8,128)(2,1)S(1)}, bf16[1,4,256,128]{3,2,1,0:T(8,128)(2,1)S(1)}, u32[]{:S(2)}, u32[]{:S(2)}) collective-permute-start(bf16[1,4,256,128]{3,2,1,0:T(8,128)(2,1)S(1)} %bitcast.36), channel_id=1, source_target_pairs={{0,4},{2,6},{4,0},{6,2},{1,5},{3,7},{5,1},{7,3},{8,12},{10,14},{12... | collective-permute-start | bytes 786440 | tf_op jit(solution)/shard_map/ppermute | solution.py:727
  120.8 6.2 %collective-permute-start.21 = (bf16[2,256,128]{2,1,0:T(8,128)(2,1)S(1)}, bf16[2,256,128]{2,1,0:T(8,128)(2,1)S(1)}, u32[]{:S(2)}, u32[]{:S(2)}) collective-permute-start(bf16[2,256,128]{2,1,0:T(8,128)(2,1)S(1)} %get-tuple-element.148), channel_id=1, source_target_pairs={{0,2},{2,0},{4,6},{6,4},{1,3},{3,1},{5,7},{7,5},{8,10},{10,8},{12,... | collective-permute-start | bytes 393224 | tf_op jit(solution)/shard_map/ppermute | solution.py:727
  122.0 6.4 %collective-permute-start.22 = (bf16[2,256,128]{2,1,0:T(8,128)(2,1)S(1)}, bf16[2,256,128]{2,1,0:T(8,128)(2,1)S(1)}, u32[]{:S(2)}, u32[]{:S(2)}) collective-permute-start(bf16[2,256,128]{2,1,0:T(8,128)(2,1)S(1)} %get-tuple-element.149), channel_id=1, source_target_pairs={{0,4},{2,6},{4,0},{6,2},{1,5},{3,7},{5,1},{7,3},{8,12},{10,14},{12... | collective-permute-start | bytes 393224 | tf_op jit(solution)/shard_map/ppermute | solution.py:727
  123.1 7.1 %collective-permute-start.23 = (bf16[2,256,128]{2,1,0:T(8,128)(2,1)S(1)}, bf16[2,256,128]{2,1,0:T(8,128)(2,1)S(1)}, u32[]{:S(2)}, u32[]{:S(2)}) collective-permute-start(bf16[2,256,128]{2,1,0:T(8,128)(2,1)S(1)} %get-tuple-element.150), channel_id=1, source_target_pairs={{0,6},{2,4},{4,2},{6,0},{1,7},{3,5},{5,3},{7,1},{8,14},{10,12},{12... | collective-permute-start | bytes 393224 | tf_op jit(solution)/shard_map/ppermute | solution.py:727
